TPU v7x, 256 devices: a whole 4x4x8 slice. The times are simulated.
256 devices in a mesh: dp: 32 (over z, x), mp: 8 (over y, core).
Axes of the slice: x: 4, y: 4, z: 8, core: 2. Of those that a mesh axis runs over, the one named last changes fastest.
Arguments:
- hidden: bfloat16 [4, 4096, 16384], P(None, 'dp', 'mp'), may hold values from -6 to 6
- queries: bfloat16 [4, 4096, 8192], P(None, 'dp', 'mp'), may hold values from -100 to 100
- rotated_token_keys: bfloat16 [4, 4096, 1024], P(None, 'dp', 'mp'), may hold values from -7 to 7
- stored_key_cache: bfloat16 [4096, 8, 64, 128], P('dp', 'mp'), may hold values from -6 to 6
- stored_value_cache: bfloat16 [4096, 8, 64, 128], P('dp', 'mp'), may hold values from -6 to 6
- row_cache_length: int32 [4096], P('dp'), may hold values from 1 to 64, as said below
- value_weight_matrix: bfloat16 [16384, 1024], P('mp'), may hold values from -0.0625 to 0.0625
- adapter_down_factor: float32 [64, 16384], P(None, 'mp'), may hold values from -0.046875 to 0.046875
- learner_down_gradient: bfloat16 [32, 64, 16384], P('dp', None, 'mp'), may hold values from -0.015625 to 0.015625
- adapter_up_factor: float32 [1024, 64], P('mp'), may hold values from -0.75 to 0.75
- learner_up_gradient: bfloat16 [32, 1024, 64], P('dp', 'mp'), may hold values from -0.25 to 0.25
Outputs:
- context: bfloat16 [4, 4096, 8192], P(None, 'dp', 'mp')
Inputs may be any that keep to these rules, and one draw needn't show every extreme that they name: `row_cache_length`: some row has exactly 64 live positions in every draw; the 128 rows of each index of dp share one drawn ceiling, between 8 and 64.
All inputs are finite; a program needn't handle non-finite values.
Results may differ from a plain program's by a relative error of at most 0.0058.
Values sent between devices are 32-bit elements; how exact they have to be, the bound alone decides.
No kernel may reach another device: no remote copies, remote signals or barrier semaphores. Data moves between devices by JAX's collectives and lax.ppermute only.
A program may use at most 64 MiB of HBM per device.

v0:
```python
import jax
import jax.numpy as jnp
from jax import lax
from jax.sharding import PartitionSpec as P

LEARNING_RATE = 0.5
ADAPTER_SCALE = 0.5


def shards(
    hidden,
    queries,
    rotated_token_keys,
    stored_key_cache,
    stored_value_cache,
    row_cache_length,
    value_weight_matrix,
    adapter_down_factor,
    learner_down_gradient,
    adapter_up_factor,
    learner_up_gradient,
):
    step_count, rows_dev, width_dev = hidden.shape
    heads_dev = stored_key_cache.shape[1]
    ctx_len = stored_key_cache.shape[2]
    head_dim = stored_key_cache.shape[3]
    group_size = queries.shape[2] // (heads_dev * head_dim)
    term_a = learner_down_gradient[0].astype(jnp.float32)
    term_b = learner_up_gradient[0].astype(jnp.float32)
    down_gradient_sum, up_gradient_sum = lax.psum((term_a, term_b), "dp")
    stepped_down_factor = adapter_down_factor - LEARNING_RATE * down_gradient_sum
    stepped_up_factor = adapter_up_factor - LEARNING_RATE * up_gradient_sum
    full_b = lax.all_gather(stepped_up_factor, "mp", axis=0, tiled=True)
    adapter_product = lax.dot_general(
        stepped_down_factor,
        full_b,
        (((0,), (1,)), ((), ())),
        precision=lax.Precision.HIGHEST,
        preferred_element_type=jnp.float32,
    )
    merged_value_weight = (
        value_weight_matrix.astype(jnp.float32) + ADAPTER_SCALE * adapter_product
    ).astype(jnp.bfloat16)
    flat_hidden = hidden.reshape(step_count * rows_dev, width_dev)
    value_terms = lax.psum_scatter(
        lax.dot_general(
            merged_value_weight,
            flat_hidden,
            (((0,), (1,)), ((), ())),
            preferred_element_type=jnp.float32,
        ),
        "mp",
        scatter_dimension=0,
        tiled=True,
    )
    new_values = (
        value_terms.astype(jnp.bfloat16)
        .reshape(heads_dev, head_dim, step_count, rows_dev)
        .transpose(3, 0, 2, 1)
    )
    query_rows = queries.reshape(step_count, rows_dev, heads_dev, group_size, head_dim).transpose(
        1, 2, 0, 3, 4
    )
    query_rows = query_rows.reshape(rows_dev, heads_dev, step_count * group_size, head_dim)
    keys_new = rotated_token_keys.reshape(step_count, rows_dev, heads_dev, head_dim).transpose(
        1, 2, 0, 3
    )
    score_scale = 1.0 / jnp.sqrt(jnp.float32(head_dim))
    causal = (
        jnp.arange(step_count, dtype=jnp.int32)[None, :]
        <= (jnp.arange(step_count * group_size, dtype=jnp.int32) // group_size)[:, None]
    )
    fresh_scores = (
        jnp.einsum("rhqd,rhud->rhqu", query_rows, keys_new, preferred_element_type=jnp.float32)
        * score_scale
    )
    fresh_scores = jnp.where(causal[None, None], fresh_scores, -jnp.inf)
    live_mask = jnp.arange(ctx_len, dtype=jnp.int32)[None, :] < row_cache_length[:, None]
    cache_scores = (
        jnp.einsum(
            "rhqd,rhkd->rhqk", query_rows, stored_key_cache, preferred_element_type=jnp.float32
        )
        * score_scale
    )
    cache_scores = jnp.where(live_mask[:, None, None, :], cache_scores, -jnp.inf)
    row_max = jnp.maximum(jnp.max(cache_scores, axis=-1), jnp.max(fresh_scores, axis=-1))
    cache_exp = jnp.where(
        live_mask[:, None, None, :], jnp.exp(cache_scores - row_max[..., None]), 0.0
    )
    fresh_exp = jnp.where(causal[None, None], jnp.exp(fresh_scores - row_max[..., None]), 0.0)
    denominator = jnp.sum(cache_exp, axis=-1) + jnp.sum(fresh_exp, axis=-1)
    cache_weights = (cache_exp / denominator[..., None]).astype(jnp.bfloat16)
    fresh_weights = (fresh_exp / denominator[..., None]).astype(jnp.bfloat16)
    summed = jnp.einsum(
        "rhqk,rhkd->rhqd", cache_weights, stored_value_cache, preferred_element_type=jnp.float32
    )
    summed = summed + jnp.einsum(
        "rhqu,rhud->rhqd", fresh_weights, new_values, preferred_element_type=jnp.float32
    )
    result = summed.astype(jnp.bfloat16).reshape(
        rows_dev, heads_dev, step_count, group_size, head_dim
    )
    return result.transpose(2, 0, 1, 3, 4).reshape(
        step_count, rows_dev, heads_dev * group_size * head_dim
    )


def solution(mesh):
    placed = (
        P(None, "dp", "mp"),
        P(None, "dp", "mp"),
        P(None, "dp", "mp"),
        P("dp", "mp", None, None),
        P("dp", "mp", None, None),
        P("dp"),
        P("mp", None),
        P(None, "mp"),
        P("dp", None, "mp"),
        P("mp", None),
        P("dp", "mp", None),
    )
    return jax.shard_map(
        shards, mesh=mesh, in_specs=placed, out_specs=P(None, "dp", "mp"), check_vma=False
    )
```

profile of v0, /device:TPU:1, one launch (start us, length us, event | category | flops | bytes accessed | tf_op | source)
XLA Modules:
  0.0 224.4 jit_solution(1798512316289575981)
XLA Ops:
  6.5 0.0 copy-start
  6.5 0.0 copy-start.3
  6.5 0.0 all-reduce.2.cloned.1.call-start
  6.5 1.9 bitcast_convert_fusion
  8.5 0.0 all-reduce.2.cloned.1.call-update
  8.5 0.0 reduce-scatter.2.cloned.1.call-start
  8.5 0.7 bitcast_convert_fusion.1
  9.3 118.7 %psum.15 = f32[128,64]{0,1:T(8,128)S(1)} all-reduce(f32[128,64]{0,1:T(8,128)S(1)} %bitcast_convert_fusion.1), channel_id=1, replica_groups=mesh['dp'=32,'mp'=8] {'dp'}, use_global_device_ids=true, to_apply=%region_5.6 | all-reduce | flops 8192 | bytes 65536 | tf_op jit(solution)/shard_map/psum | solution.py:30
  128.0 0.8 multiply_subtract_fusion
  128.7 41.8 %all_gather.3 = f32[1024,64]{0,1:T(8,128)S(1)} all-gather(f32[128,64]{0,1:T(8,128)S(1)} %multiply_subtract_fusion), channel_id=1, replica_groups=mesh['dp'=32,'mp'=8] {'mp'}, dimensions={0}, use_global_device_ids=true | all-gather | bytes 294912 | tf_op jit(solution)/shard_map/all_gather | solution.py:33
  170.5 0.0 all-reduce.2.cloned.1.call-done
  170.5 0.0 copy-done.3
  170.5 9.0 %add_convert_fusion = bf16[2048,1024]{1,0:T(8,128)(2,1)S(1)} fusion(bf16[2048,1024]{1,0:T(8,128)(2,1)} %param.17, f32[1024,64]{0,1:T(8,128)S(1)} %all_gather.3, f32[64,2048]{1,0:T(8,128)S(1)} %copy-done.3, f32[64,2048]{1,0:T(8,128)} %all-reduce.2.cloned.1.call-done), kind=kOutput, calls=%fused_computation | convolution fusion | flops 1619263488 | bytes 9699328 | tf_op jit(solution)/shard_map/dot_general | solution.py:34
  179.5 0.0 copy-done
  179.5 3.7 %fusion.34 = f32[1024,512]{1,0:T(8,128)} fusion(bf16[2048,1024]{1,0:T(8,128)(2,1)S(1)} %add_convert_fusion, bf16[512,2048]{1,0:T(8,128)(2,1)S(1)} %bitcast.52), kind=kOutput, calls=%fused_computation.51 | convolution fusion | flops 2147483648 | bytes 8388608 | tf_op jit(solution)/shard_map/dot_general | solution.py:46
  183.2 0.0 copy-start.2
  183.2 0.0 copy-start.4
  183.2 0.0 copy-start.6
  183.2 0.0 reduce-scatter.2.cloned.1.call-update
  183.3 1.2 copy-done.2
  184.5 0.0 copy-start.1
  184.5 0.3 copy.17
  184.8 0.0 copy-done.4
  184.8 0.1 iota_compare_fusion
  184.9 0.0 copy-done.6
  184.9 0.7 fusion.33
  185.5 0.5 copy-done.1
  186.1 1.3 fusion.4
  187.3 0.0 copy-start.5
  187.4 0.2 fusion.21
  187.6 1.4 fusion.5
  189.0 0.1 copy-done.5
  189.1 2.9 %fusion = f32[128,32,128]{2,1,0:T(8,128)} fusion(bf16[128,1,64,128]{3,2,1,0:T(8,128)(2,1)S(1)} %copy-done.5, f32[128,32,64]{2,1,0:T(8,128)S(1)} %get-tuple-element.6, f32[128,32]{1,0:T(8,128)S(1)} %add.27, f32[128,32]{1,0:T(8,128)S(1)} %max.9, pred[128,64]{1,0:T(8,128)(4,1)S(1)} %iota_compare_fusion), kind=kOutput, calls=%fused_computation.1 | convolution fusion | flops 68681728 | bytes 5283840 | tf_op jit(solution)/shard_map/rhqk,rhkd->rhqd/dot_general | solution.py:94
  192.0 18.7 %reduce-scatter.2.cloned.1.call-done = f32[128,512]{1,0:T(8,128)} async-done(((f32[1024,512]{1,0:T(8,128)}), f32[128,512]{1,0:T(8,128)}) %reduce-scatter.2.cloned.1.call-update) | async-done | bytes 262160 | tf_op jit(solution)/shard_map/reduce_scatter | solution.py:45
  210.7 1.0 convert_element_type.41
  211.7 0.1 copy.14
  211.8 3.1 %fusion.6 = bf16[4,128,1,8,128]{4,3,0,1,2:T(8,128)(2,1)} fusion(f32[128,32,128]{2,1,0:T(8,128)} %fusion, f32[128,32,4]{1,2,0:T(4,128)S(1)} %get-tuple-element.8, bf16[1,128,4,128]{1,2,3,0:T(4,128)(2,1)S(1)} %copy.14, f32[128,32]{1,0:T(8,128)S(1)} %add.27, f32[128,32]{1,0:T(8,128)S(1)} %max.9, pred[32,4]{0,1:T(4,128)(4,1)S(1)} %iota_compare_fusion.1), kind=kOutput, calls=%fused_computation.11 | convolution fusion | flops 5308416 | bytes 3375232 | tf_op jit(solution)/shard_map/rhqu,rhud->rhqd/dot_general | solution.py:97
  214.9 1.3 reshape.164
  216.3 1.3 copy.16
  (5 shorter events, 0.1 us)
Async XLA Ops:
  6.5 173.0 %copy-start = (bf16[4,128,2048]{2,1,0:T(8,128)(2,1)S(1)}, bf16[4,128,2048]{2,1,0:T(8,128)(2,1)}, u32[]{:S(2)}) copy-start(bf16[4,128,2048]{2,1,0:T(8,128)(2,1)} %param.11) | copy-start | bytes 6291460
  6.5 164.0 %copy-start.3 = (f32[64,2048]{1,0:T(8,128)S(1)}, f32[64,2048]{1,0:T(8,128)}, u32[]{:S(2)}) copy-start(f32[64,2048]{1,0:T(8,128)} %param.18) | copy-start | bytes 1572868
  6.5 164.0 %all-reduce.2.cloned.1.call-start = ((), (), s32[]{:S(2)}) async-start(), calls=%async_computation.1 | async-start | bytes 1048576 | tf_op jit(solution)/shard_map/psum | solution.py:30
  8.5 202.2 %reduce-scatter.2.cloned.1.call-start = ((), (), s32[]{:S(2)}) async-start(), calls=%async_computation.2 | async-start | bytes 2359296 | tf_op jit(solution)/shard_map/reduce_scatter | solution.py:45
  183.2 1.2 copy-start.2
  183.2 1.5 copy-start.4
  183.2 1.6 copy-start.6
  184.5 1.6 copy-start.1
  187.3 1.7 copy-start.5
Sparse Core Ops, SparseCore 0:
  10.8 146.5 all-reduce.1
  183.4 27.2 reduce-scatter.1
where the time goes:
time: 227 us; the launch traced here: 224 us
  blocking collectives  161 us (71%)
  matrix products  20.6 us (9%)
  waiting for transfers between devices  18.7 us (8%)
  between operations  13.5 us (6%)
  other arithmetic  6.09 us (3%)
  local copies, waits for them, and re-layouts  4.89 us (2%)
    psum x1, blocking collectives, shards(): down_gradient_sum, up_gradient_sum = lax.psum((term_a, term_b), 'dp')  119 us
    all_gather x1, blocking collectives, shards(): full_b = lax.all_gather(stepped_up_factor, 'mp', axis=0, tiled=True)  41.8 us
    reduce_scatter x1, waiting for transfers between devices, shards(): lax.psum_scatter(lax.dot_general(merged_value_weight, flat_hidden, (((0,)...  18.7 us
    dot_general x1, matrix products, shards(): lax.dot_general(stepped_down_factor, full_b, (((0,), (1,)), ((), ())), pr...  8.98 us
  transfers between devices with their start and end apart: 2, of which 1 were waited for; matrix products, arithmetic and copies ran while one was open for 4% of the time, Pallas kernels for 0%

commit v1 on v0

v1 whole, which is shorter than its diff:
```python
import functools

import jax
import jax.numpy as jnp
from jax import lax
from jax.experimental import pallas as pl
from jax.experimental.pallas import tpu as pltpu
from jax.sharding import PartitionSpec as P

LEARNING_RATE = 0.5
ADAPTER_SCALE = 0.5


def split_bf16(x):
    high = x.astype(jnp.bfloat16)
    low = (x - high.astype(jnp.float32)).astype(jnp.bfloat16)
    return high, low


def finish_kernel(heads, base_ref, u0, u1, u2, u3, b_ref, w_ref, cache_ref, out_ref, value_ref):
    t = pl.program_id(0)
    steps, rows, dim = value_ref.shape

    @pl.when(t == 0)
    def _():
        u = (u0[...] + u1[...]) + (u2[...] + u3[...])
        u_high, u_low = split_bf16(u)
        b_high, b_low = split_bf16(b_ref[...])
        dims = (((0,), (0,)), ((), ()))
        mm = functools.partial(
            lax.dot_general, dimension_numbers=dims, preferred_element_type=jnp.float32
        )
        delta = mm(b_high, u_high) + (mm(b_low, u_high) + mm(b_high, u_low))
        values = base_ref[...] + ADAPTER_SCALE * delta
        for s in range(steps):
            part = values[:, s * rows : (s + 1) * rows].T
            value_ref[s] = part.astype(jnp.bfloat16).astype(jnp.float32)

    for step in range(steps):

        @pl.when(t == step)
        def _():
            for g in range(heads):
                acc = cache_ref[0, :, g * dim : (g + 1) * dim]
                for s in range(step + 1):
                    j = (step * heads + g) * steps + s
                    acc = acc + w_ref[:, j : j + 1] * value_ref[s]
                out_ref[0, :, g * dim : (g + 1) * dim] = acc.astype(out_ref.dtype)


def shards(
    hidden,
    queries,
    rotated_token_keys,
    stored_key_cache,
    stored_value_cache,
    row_cache_length,
    value_weight_matrix,
    adapter_down_factor,
    learner_down_gradient,
    adapter_up_factor,
    learner_up_gradient,
):
    step_count, rows_dev, width_dev = hidden.shape
    heads_dev, ctx_len, head_dim = stored_key_cache.shape[1:]
    group_size = queries.shape[2] // (heads_dev * head_dim)
    rank = adapter_down_factor.shape[0]
    n_dp = lax.axis_size("dp")
    n_mp = lax.axis_size("mp")
    tokens = step_count * rows_dev
    flat_hidden = hidden.reshape(tokens, width_dev)

    term_a = -LEARNING_RATE * learner_down_gradient[0].astype(jnp.float32)
    term_b = -LEARNING_RATE * learner_up_gradient[0].astype(jnp.float32)
    terms = jnp.concatenate([term_a, term_b.T], axis=1)
    width = terms.shape[1]
    terms = terms.reshape(n_dp, rank // n_dp, width)
    mine = jnp.sum(lax.all_to_all(terms, "dp", 0, 0, tiled=True), axis=0)
    steps_ab = lax.all_to_all(
        jnp.broadcast_to(mine[None], terms.shape), "dp", 0, 0, tiled=True
    ).reshape(rank, width)
    new_a = adapter_down_factor + steps_ab[:, :width_dev]
    new_b = adapter_up_factor.T + steps_ab[:, width_dev:]

    base = lax.psum_scatter(
        lax.dot_general(
            value_weight_matrix,
            flat_hidden,
            (((0,), (1,)), ((), ())),
            preferred_element_type=jnp.float32,
        ),
        "mp",
        scatter_dimension=0,
        tiled=True,
    )

    a_split = jnp.concatenate(split_bf16(new_a), axis=0)
    inner = lax.dot_general(
        a_split, flat_hidden, (((1,), (1,)), ((), ())), preferred_element_type=jnp.float32
    )
    inner = inner[:rank] + inner[rank:]
    inner = inner + lax.ppermute(inner, "mp", [(i, i ^ 1) for i in range(n_mp)])
    inner_parts = [inner] + [
        lax.ppermute(inner, "mp", [(i, (i + 2 * k) % n_mp) for i in range(n_mp)])
        for k in range(1, n_mp // 2)
    ]

    query_rows = queries.reshape(step_count, rows_dev, group_size, head_dim).transpose(1, 0, 2, 3)
    query_rows = query_rows.reshape(rows_dev, step_count * group_size, head_dim)
    keys_new = rotated_token_keys.transpose(1, 0, 2)
    key_cache = stored_key_cache[:, 0]
    value_cache = stored_value_cache[:, 0]
    score_scale = 1.0 / jnp.sqrt(jnp.float32(head_dim))
    causal = (
        jnp.arange(step_count, dtype=jnp.int32)[None, :]
        <= (jnp.arange(step_count * group_size, dtype=jnp.int32) // group_size)[:, None]
    )
    fresh_scores = (
        jnp.einsum("rqd,rud->rqu", query_rows, keys_new, preferred_element_type=jnp.float32)
        * score_scale
    )
    fresh_scores = jnp.where(causal[None], fresh_scores, -jnp.inf)
    live_mask = jnp.arange(ctx_len, dtype=jnp.int32)[None, :] < row_cache_length[:, None]
    cache_scores = (
        jnp.einsum("rqd,rkd->rqk", query_rows, key_cache, preferred_element_type=jnp.float32)
        * score_scale
    )
    cache_scores = jnp.where(live_mask[:, None, :], cache_scores, -jnp.inf)
    row_max = jnp.maximum(jnp.max(cache_scores, axis=-1), jnp.max(fresh_scores, axis=-1))
    cache_exp = jnp.where(live_mask[:, None, :], jnp.exp(cache_scores - row_max[..., None]), 0.0)
    fresh_exp = jnp.where(causal[None], jnp.exp(fresh_scores - row_max[..., None]), 0.0)
    denominator = jnp.sum(cache_exp, axis=-1) + jnp.sum(fresh_exp, axis=-1)
    cache_weights = (cache_exp / denominator[..., None]).astype(jnp.bfloat16)
    fresh_weights = (fresh_exp / denominator[..., None]).astype(jnp.bfloat16)
    cache_part = jnp.einsum(
        "rqk,rkd->rqd", cache_weights, value_cache, preferred_element_type=jnp.float32
    )
    cache_part = (
        cache_part.reshape(rows_dev, step_count, group_size, head_dim)
        .transpose(1, 0, 2, 3)
        .reshape(step_count, rows_dev, group_size * head_dim)
    )
    fresh_flat = fresh_weights.astype(jnp.float32).reshape(
        rows_dev, step_count * group_size * step_count
    )

    whole = lambda a: pl.BlockSpec(a.shape, lambda t: (0,) * a.ndim)
    small = [base, *inner_parts, new_b, fresh_flat]
    step_spec = pl.BlockSpec((1, rows_dev, group_size * head_dim), lambda t: (t, 0, 0))
    return pl.pallas_call(
        functools.partial(finish_kernel, group_size),
        grid=(step_count,),
        out_shape=jax.ShapeDtypeStruct(queries.shape, jnp.bfloat16),
        in_specs=[whole(a) for a in small] + [step_spec],
        out_specs=step_spec,
        scratch_shapes=[pltpu.VMEM((step_count, rows_dev, head_dim), jnp.float32)],
        compiler_params=pltpu.CompilerParams(vmem_limit_bytes=16 * 1024 * 1024),
    )(*small, cache_part)


def solution(mesh):
    placed = (
        P(None, "dp", "mp"),
        P(None, "dp", "mp"),
        P(None, "dp", "mp"),
        P("dp", "mp", None, None),
        P("dp", "mp", None, None),
        P("dp"),
        P("mp", None),
        P(None, "mp"),
        P("dp", None, "mp"),
        P("mp", None),
        P("dp", "mp", None),
    )
    return jax.shard_map(
        shards, mesh=mesh, in_specs=placed, out_specs=P(None, "dp", "mp"), check_vma=False
    )
```

time: 227 us -> 97.5 us (0.43)
  blocking collectives: 161 us -> 0 us
  starting transfers between devices: 0.04 us -> 26.2 us
  local copies, waits for them, and re-layouts: 4.89 us -> 13.9 us
  matrix products: 20.6 us -> 13 us
  waiting for transfers between devices: 18.7 us -> 22.9 us
  Pallas kernels: 0 us -> 3.04 us
    psum x1 -> x0, blocking collectives: 119 us -> none  [shards(): down_gradient_sum, up_gradient_sum = lax.psum((term_a, term_b), 'dp')]
    all_gather x1 -> x0, blocking collectives: 41.8 us -> none  [shards(): full_b = lax.all_gather(stepped_up_factor, 'mp', axis=0, tiled=True)]
    reduce_scatter x1, waiting for transfers between devices: 18.7 us -> 0.01 us  [shards(): lax.psum_scatter(lax.dot_general(value_weight_matrix, flat_hidden, (((0,)...]
    all_to_all x0 -> x2, starting transfers between devices: none -> 17.2 us  [the longest x1 11.9 us: shards(): mine = jnp.sum(lax.all_to_all(terms, 'dp', 0, 0, tiled=True), axis=0)]
    all_to_all x0 -> x2, waiting for transfers between devices: none -> 17.2 us  [the longest x1 11.9 us: shards(): mine = jnp.sum(lax.all_to_all(terms, 'dp', 0, 0, tiled=True), axis=0)]
    ppermute x0 -> x4, starting transfers between devices: none -> 8.93 us  [the longest x3 5.06 us: shards(): lax.ppermute(inner, 'mp', [(i, (i + 2 * k) % n_mp) for i in range(n_mp)])]
    dot_general x6 -> x5, matrix products: 20.6 us -> 13 us  [the longest x1 5.89 us: shards(): lax.dot_general(value_weight_matrix, flat_hidden, (((0,), (1,)), ((), ())...]
    ppermute x0 -> x4, waiting for transfers between devices: none -> 5.72 us  [the longest x3 4.99 us: shards(): lax.ppermute(inner, 'mp', [(i, (i + 2 * k) % n_mp) for i in range(n_mp)])]
  transfers between devices with their start and end apart: 2 -> 7, of which waited for: 1 -> 5; matrix products, arithmetic and copies ran while one was open for 4% -> 21% of each run, Pallas kernels for 0% -> 0%
where the time goes in v1:
time: 97.5 us; the launch traced here: 96.9 us
  starting transfers between devices  26.2 us (27%)
  waiting for transfers between devices  22.9 us (23%)
  local copies, waits for them, and re-layouts  13.9 us (14%)
  between operations  13.6 us (14%)
  matrix products  13 us (13%)
  other arithmetic  4.4 us (5%)
  Pallas kernels  3.04 us (3%)
    all_to_all x1, starting transfers between devices, shards(): mine = jnp.sum(lax.all_to_all(terms, 'dp', 0, 0, tiled=True), axis=0)  11.9 us
    all_to_all x1, waiting for transfers between devices, shards(): mine = jnp.sum(lax.all_to_all(terms, 'dp', 0, 0, tiled=True), axis=0)  11.9 us
    unnamed x19, local copies, waits for them, and re-layouts  6.74 us
    dot_general x1, matrix products, shards(): lax.dot_general(value_weight_matrix, flat_hidden, (((0,), (1,)), ((), ())...  5.89 us
    all_to_all x1, starting transfers between devices, shards(): lax.all_to_all(jnp.broadcast_to(mine[None], terms.shape), 'dp', 0, 0, til...  5.36 us
    all_to_all x1, waiting for transfers between devices, shards(): lax.all_to_all(jnp.broadcast_to(mine[None], terms.shape), 'dp', 0, 0, til...  5.28 us
    ppermute x3, starting transfers between devices, shards(): lax.ppermute(inner, 'mp', [(i, (i + 2 * k) % n_mp) for i in range(n_mp)])  5.06 us
    ppermute x3, waiting for transfers between devices, shards(): lax.ppermute(inner, 'mp', [(i, (i + 2 * k) % n_mp) for i in range(n_mp)])  4.99 us
  transfers between devices with their start and end apart: 7, of which 5 were waited for; matrix products, arithmetic and copies ran while one was open for 21% of the time, Pallas kernels for 0%

profile of v1, /device:TPU:1, one launch (start us, length us, event | category | flops | bytes accessed | tf_op | source)
XLA Modules:
  0.0 96.9 jit_solution(10179528259686296720)
XLA Ops:
  6.5 0.0 copy-start
  6.5 1.6 %copy-done = bf16[4,128,2048]{2,1,0:T(8,128)(2,1)S(1)} copy-done((bf16[4,128,2048]{2,1,0:T(8,128)(2,1)S(1)}, bf16[4,128,2048]{2,1,0:T(8,128)(2,1)}, u32[]{:S(2)}) %copy-start) | copy-done | bytes 2097176
  8.1 5.9 %fusion.34 = f32[1024,512]{1,0:T(8,128)} fusion(bf16[2048,1024]{1,0:T(8,128)(2,1)} %param.17, bf16[512,2048]{1,0:T(8,128)(2,1)S(1)} %bitcast.59), kind=kOutput, calls=%fused_computation.52 | convolution fusion | flops 2147483648 | bytes 8388608 | tf_op jit(solution)/shard_map/dot_general | solution.py:86
  14.0 0.0 reduce-scatter.2.cloned.1.call-update
  14.0 0.9 copy-done.4
  15.1 0.0 copy-start.7
  15.1 0.0 copy-start.8
  15.1 1.1 %reshape.93 = f32[32,2,2176]{2,1,0:T(2,128)} reshape(f32[64,2176]{1,0:T(8,128)S(1)} %pad_maximum_fusion) | data formatting | bytes 1114112 | tf_op jit(solution)/shard_map/reshape | solution.py:77
  16.2 11.9 %all-to-all-start = ((f32[32,2,2176]{2,1,0:T(2,128)}), f32[32,2,2176]{2,1,0:T(2,128)S(1)}, u32[]{:S(2)}, u32[]{:S(2)}) async-start(f32[32,2,2176]{2,1,0:T(2,128)} %reshape.93), calls=%async_computation.1 | async-start | bytes 1114112 | tf_op jit(solution)/shard_map/all_to_all | solution.py:78
  28.1 0.0 copy-start.3
  28.1 1.7 %copy.47 = bf16[64,8,8,128]{3,2,1,0:T(8,128)(2,1)S(1)} copy(bf16[64,8,8,128]{3,1,2,0:T(8,128)(2,1)} %bitcast.64) | data formatting | bytes 2097152
  29.8 0.1 iota_compare_fusion
  29.9 0.6 fusion.10
  30.5 0.0 copy-done.3
  30.5 2.5 %fusion.4 = (f32[128,32]{1,0:T(8,128)S(1)}, f32[128,32,64]{2,1,0:T(8,128)}) fusion(pred[128,64]{1,0:T(8,128)(4,1)S(1)} %iota_compare_fusion, bf16[128,1,64,128]{3,2,1,0:T(8,128)(2,1)S(1)} %copy-done.3, bf16[4,128,8,128]{3,2,1,0:T(8,128)(2,1)S(1)} %bitcast.63), kind=kOutput, calls=%fused_computation.8 | convolution fusion | flops 67891200 | bytes 4218880 | tf_op jit(solution)/shard_map/rqd,rkd->rqk/dot_general | solution.py:125
  33.1 11.9 %all-to-all-done = f32[32,2,2176]{2,1,0:T(2,128)S(1)} async-done(((f32[32,2,2176]{2,1,0:T(2,128)}), f32[32,2,2176]{2,1,0:T(2,128)S(1)}, u32[]{:S(2)}, u32[]{:S(2)}) %all-to-all-start) | async-done | bytes 557088 | tf_op jit(solution)/shard_map/all_to_all | solution.py:78
  45.0 0.2 reduce_sum.27
  45.1 0.9 broadcast_in_dim.56
  46.1 5.4 %all-to-all-start.1 = ((f32[32,2,2176]{2,1,0:T(2,128)}), f32[32,2,2176]{2,1,0:T(2,128)S(1)}, u32[]{:S(2)}, u32[]{:S(2)}) async-start(f32[32,2,2176]{2,1,0:T(2,128)} %broadcast_in_dim.56), calls=%async_computation.2 | async-start | bytes 1114112 | tf_op jit(solution)/shard_map/all_to_all | solution.py:79
  51.5 0.1 copy.39
  51.6 0.1 fusion.26
  51.7 0.1 copy.40
  51.8 0.1 copy.41
  51.8 0.1 fusion.27
  52.0 0.1 copy.42
  52.1 2.5 %fusion.8 = f32[128,32]{1,0:T(8,128)S(1)} fusion(f32[128,32,64]{2,1,0:T(8,128)} %get-tuple-element.8, f32[128,32]{1,0:T(8,128)S(1)} %max.7, pred[128,64]{1,0:T(8,128)(4,1)S(1)} %iota_compare_fusion), kind=kLoop, calls=%fused_computation.10 | loop fusion | flops 1306624 | bytes 1089536 | tf_op jit(solution)/shard_map/reduce_sum | solution.py:132
  54.6 0.1 copy.43
  54.7 3.0 %fusion.5 = f32[128,4,8,128]{3,2,1,0:T(8,128)S(1)} fusion(bf16[128,1,64,128]{3,2,1,0:T(8,128)(2,1)} %param.15, f32[128,32,64]{2,1,0:T(8,128)} %get-tuple-element.8, f32[128,32]{1,0:T(8,128)S(1)} %add.30, f32[128,32]{1,0:T(8,128)S(1)} %max.7, pred[128,64]{1,0:T(8,128)(4,1)S(1)} %iota_compare_fusion), kind=kOutput, calls=%fused_computation.9 | convolution fusion | flops 68681728 | bytes 5283840 | tf_op jit(solution)/shard_map/rqk,rkd->rqd/dot_general | solution.py:135
  57.7 1.5 %copy.61 = f32[128,4,8,128]{3,2,0,1:T(8,128)} copy(f32[128,4,8,128]{3,2,1,0:T(8,128)S(1)} %fusion.5) | data formatting | bytes 4194304 | tf_op jit(solution)/shard_map/reshape | solution.py:139
  59.2 2.7 %reshape.100.cache_ref = f32[4,128,1024]{2,1,0:T(8,128)} reshape(f32[4,128,8,128]{3,2,1,0:T(8,128)} %bitcast.61) | data formatting | bytes 4194304 | tf_op jit(solution)/shard_map/reshape | solution.py:141
  61.9 5.3 %all-to-all-done.1 = f32[32,2,2176]{2,1,0:T(2,128)S(1)} async-done(((f32[32,2,2176]{2,1,0:T(2,128)}), f32[32,2,2176]{2,1,0:T(2,128)S(1)}, u32[]{:S(2)}, u32[]{:S(2)}) %all-to-all-start.1) | async-done | bytes 557088 | tf_op jit(solution)/shard_map/all_to_all | solution.py:79
  67.2 0.4 reshape.94
  67.6 1.1 %subtract_convert_fusion = (bf16[64,2048]{1,0:T(8,128)(2,1)S(1)}, bf16[64,2048]{1,0:T(8,128)(2,1)S(1)}) fusion(f32[64,2048]{1,0:T(8,128)} %param.18, f32[64,2176]{1,0:T(8,128)S(1)} %reshape.94), kind=kLoop, calls=%fused_computation.29 | loop fusion | flops 655360 | bytes 1572864 | tf_op jit(solution)/shard_map/convert_element_type | solution.py:16
  68.7 0.0 copy-start.5
  68.7 0.8 fusion.20
  69.6 3.9 %collective-permute-start = (f32[64,512]{1,0:T(8,128)S(1)}, f32[64,512]{1,0:T(8,128)S(1)}, u32[]{:S(2)}, u32[]{:S(2)}) collective-permute-start(f32[64,512]{1,0:T(8,128)S(1)} %slice_add_fusion.1), channel_id=1, source_target_pairs={{0,1},{1,0},{2,3},{3,2},{4,5},{5,4},{6,7},{7,6},{8,9},{9,8},{10,11... | collective-permute-start | bytes 393224 | tf_op jit(solution)/shard_map/ppermute | solution.py:102
  73.4 0.1 fusion.28
  73.6 0.1 copy.46.w_ref
  73.7 0.7 collective-permute-done
  74.5 1.4 %collective-permute-start.1 = (f32[64,512]{1,0:T(8,128)S(1)}, f32[64,512]{1,0:T(8,128)S(1)}, u32[]{:S(2)}, u32[]{:S(2)}) collective-permute-start(f32[64,512]{1,0:T(8,128)S(1)} %fusion.38.u0), channel_id=1, source_target_pairs={{0,2},{1,3},{2,4},{3,5},{4,6},{5,7},{6,0},{7,1},{8,10},{9,11},{10,... | collective-permute-start | bytes 393224 | tf_op jit(solution)/shard_map/ppermute | solution.py:104
  75.8 2.6 %collective-permute-start.2 = (f32[64,512]{1,0:T(8,128)S(1)}, f32[64,512]{1,0:T(8,128)S(1)}, u32[]{:S(2)}, u32[]{:S(2)}) collective-permute-start(f32[64,512]{1,0:T(8,128)S(1)} %fusion.38.u0), channel_id=1, source_target_pairs={{0,4},{1,5},{2,6},{3,7},{4,0},{5,1},{6,2},{7,3},{8,12},{9,13},{10,... | collective-permute-start | bytes 393224 | tf_op jit(solution)/shard_map/ppermute | solution.py:104
  78.5 1.1 %collective-permute-start.3 = (f32[64,512]{1,0:T(8,128)S(1)}, f32[64,512]{1,0:T(8,128)S(1)}, u32[]{:S(2)}, u32[]{:S(2)}) collective-permute-start(f32[64,512]{1,0:T(8,128)S(1)} %fusion.38.u0), channel_id=1, source_target_pairs={{0,6},{1,7},{2,0},{3,1},{4,2},{5,3},{6,4},{7,5},{8,14},{9,15},{10,... | collective-permute-start | bytes 393224 | tf_op jit(solution)/shard_map/ppermute | solution.py:104
  79.5 1.1 %collective-permute-done.1.u1 = f32[64,512]{1,0:T(8,128)S(1)} collective-permute-done((f32[64,512]{1,0:T(8,128)S(1)}, f32[64,512]{1,0:T(8,128)S(1)}, u32[]{:S(2)}, u32[]{:S(2)}) %collective-permute-start.1) | collective-permute-done | bytes 131104 | tf_op jit(solution)/shard_map/ppermute | solution.py:104
  80.6 3.9 %collective-permute-done.2.u2 = f32[64,512]{1,0:T(8,128)S(1)} collective-permute-done((f32[64,512]{1,0:T(8,128)S(1)}, f32[64,512]{1,0:T(8,128)S(1)}, u32[]{:S(2)}, u32[]{:S(2)}) %collective-permute-start.2) | collective-permute-done | bytes 131104 | tf_op jit(solution)/shard_map/ppermute | solution.py:104
  84.5 0.0 collective-permute-done.3.u3
  84.5 1.6 %copy-done.1 = f32[4,128,1024]{2,1,0:T(8,128)S(1)} copy-done((f32[4,128,1024]{2,1,0:T(8,128)S(1)}, f32[4,128,1024]{2,1,0:T(8,128)}, u32[]{:S(2)}) %copy-start.1) | copy-done | bytes 2097176
  86.1 0.9 copy-done.2
  87.1 3.0 %shard_map.109 = bf16[4,128,1024]{2,1,0:T(8,128)(2,1)} custom-call(f32[128,512]{1,0:T(8,128)S(1)} %copy-done.2, f32[64,512]{1,0:T(8,128)S(1)} %fusion.38.u0, f32[64,512]{1,0:T(8,128)S(1)} %collective-permute-done.1.u1, f32[64,512]{1,0:T(8,128)S(1)} %collective-permute-done.2.u2, f32[64,512]{1,0:T(8,128)S(1)} %collective-permute-done.3.u3, ...), custom_call_target="tpu_custom_call" | custom-call | tf_op jit(solution)/shard_map/pallas_call | solution.py:150
  (21 shorter events, 0.2 us)
Async XLA Ops:
  6.5 1.6 %copy-start = (bf16[4,128,2048]{2,1,0:T(8,128)(2,1)S(1)}, bf16[4,128,2048]{2,1,0:T(8,128)(2,1)}, u32[]{:S(2)}) copy-start(bf16[4,128,2048]{2,1,0:T(8,128)(2,1)} %param.11) | copy-start | bytes 6291460
  6.5 78.0 %reduce-scatter.2.cloned.1.call-start = ((), (), s32[]{:S(2)}) async-start(), calls=%async_computation.3 | async-start | bytes 2359296 | tf_op jit(solution)/shard_map/reduce_scatter | solution.py:85
  14.0 0.9 copy-start.4
  14.0 1.0 %copy-start.6 = (bf16[1,128,64]{1,2,0:T(8,128)(2,1)S(1)}, bf16[1,128,64]{1,2,0:T(8,128)(2,1)}, u32[]{:S(2)}) copy-start(bf16[1,128,64]{1,2,0:T(8,128)(2,1)} %param.21) | copy-start | bytes 49156
  15.1 14.7 %copy-start.7 = (s32[128]{0:T(128)S(1)}, s32[128]{0:T(128)}, u32[]{:S(2)}) copy-start(s32[128]{0:T(128)} %param.16) | copy-start | bytes 1540
  15.1 14.8 %copy-start.8 = (bf16[4,128,128]{2,1,0:T(8,128)(2,1)S(1)}, bf16[4,128,128]{2,1,0:T(8,128)(2,1)}, u32[]{:S(2)}) copy-start(bf16[4,128,128]{2,1,0:T(8,128)(2,1)} %param.13) | copy-start | bytes 393220
  16.2 28.7 %all-to-all-start = ((f32[32,2,2176]{2,1,0:T(2,128)}), f32[32,2,2176]{2,1,0:T(2,128)S(1)}, u32[]{:S(2)}, u32[]{:S(2)}) async-start(f32[32,2,2176]{2,1,0:T(2,128)} %reshape.93), calls=%async_computation.1 | async-start | bytes 1114112 | tf_op jit(solution)/shard_map/all_to_all | solution.py:78
  28.1 2.4 %copy-start.3 = (bf16[128,1,64,128]{3,2,1,0:T(8,128)(2,1)S(1)}, bf16[128,1,64,128]{3,2,1,0:T(8,128)(2,1)}, u32[]{:S(2)}) copy-start(bf16[128,1,64,128]{3,2,1,0:T(8,128)(2,1)} %param.14) | copy-start | bytes 6291460
  46.1 21.1 %all-to-all-start.1 = ((f32[32,2,2176]{2,1,0:T(2,128)}), f32[32,2,2176]{2,1,0:T(2,128)S(1)}, u32[]{:S(2)}, u32[]{:S(2)}) async-start(f32[32,2,2176]{2,1,0:T(2,128)} %broadcast_in_dim.56), calls=%async_computation.2 | async-start | bytes 1114112 | tf_op jit(solution)/shard_map/all_to_all | solution.py:79
  68.7 10.8 %copy-start.5 = (f32[128,64]{0,1:T(8,128)S(1)}, f32[128,64]{0,1:T(8,128)}, u32[]{:S(2)}) copy-start(f32[128,64]{0,1:T(8,128)} %param.20) | copy-start | bytes 98308
  69.6 4.8 %collective-permute-start = (f32[64,512]{1,0:T(8,128)S(1)}, f32[64,512]{1,0:T(8,128)S(1)}, u32[]{:S(2)}, u32[]{:S(2)}) collective-permute-start(f32[64,512]{1,0:T(8,128)S(1)} %slice_add_fusion.1), channel_id=1, source_target_pairs={{0,1},{1,0},{2,3},{3,2},{4,5},{5,4},{6,7},{7,6},{8,9},{9,8},{10,11... | collective-permute-start | bytes 393224 | tf_op jit(solution)/shard_map/ppermute | solution.py:102
  74.5 6.2 %collective-permute-start.1 = (f32[64,512]{1,0:T(8,128)S(1)}, f32[64,512]{1,0:T(8,128)S(1)}, u32[]{:S(2)}, u32[]{:S(2)}) collective-permute-start(f32[64,512]{1,0:T(8,128)S(1)} %fusion.38.u0), channel_id=1, source_target_pairs={{0,2},{1,3},{2,4},{3,5},{4,6},{5,7},{6,0},{7,1},{8,10},{9,11},{10,... | collective-permute-start | bytes 393224 | tf_op jit(solution)/shard_map/ppermute | solution.py:104
  75.8 8.7 %collective-permute-start.2 = (f32[64,512]{1,0:T(8,128)S(1)}, f32[64,512]{1,0:T(8,128)S(1)}, u32[]{:S(2)}, u32[]{:S(2)}) collective-permute-start(f32[64,512]{1,0:T(8,128)S(1)} %fusion.38.u0), channel_id=1, source_target_pairs={{0,4},{1,5},{2,6},{3,7},{4,0},{5,1},{6,2},{7,3},{8,12},{9,13},{10,... | collective-permute-start | bytes 393224 | tf_op jit(solution)/shard_map/ppermute | solution.py:104
  78.5 6.1 %collective-permute-start.3 = (f32[64,512]{1,0:T(8,128)S(1)}, f32[64,512]{1,0:T(8,128)S(1)}, u32[]{:S(2)}, u32[]{:S(2)}) collective-permute-start(f32[64,512]{1,0:T(8,128)S(1)} %fusion.38.u0), channel_id=1, source_target_pairs={{0,6},{1,7},{2,0},{3,1},{4,2},{5,3},{6,4},{7,5},{8,14},{9,15},{10,... | collective-permute-start | bytes 393224 | tf_op jit(solution)/shard_map/ppermute | solution.py:104
  84.5 1.6 %copy-start.1 = (f32[4,128,1024]{2,1,0:T(8,128)S(1)}, f32[4,128,1024]{2,1,0:T(8,128)}, u32[]{:S(2)}) copy-start(f32[4,128,1024]{2,1,0:T(8,128)} %reshape.100.cache_ref) | copy-start | bytes 6291460
  86.1 0.9 copy-start.2
Sparse Core Ops, SparseCore 0:
  14.2 37.9 reduce-scatter.1

commit v2 on v1

v2 whole, which is shorter than its diff:
```python
import functools

import jax
import jax.numpy as jnp
from jax import lax
from jax.experimental import pallas as pl
from jax.experimental.pallas import tpu as pltpu
from jax.sharding import PartitionSpec as P

LEARNING_RATE = 0.5
ADAPTER_SCALE = 0.5


def split_bf16(x):
    high = x.astype(jnp.bfloat16)
    low = (x - high.astype(jnp.float32)).astype(jnp.bfloat16)
    return high, low


def project_kernel(place_ref, hidden_ref, weight_ref, keep_ref, send_ref):
    dim = keep_ref.shape[2]
    both = jnp.dot(hidden_ref[...], weight_ref[...], preferred_element_type=jnp.float32)
    first, second = both[:, :dim], both[:, dim:]
    odd = place_ref[1] == 1
    keep_ref[0] = jnp.where(odd, second, first)
    send_ref[0] = jnp.where(odd, first, second)


def terms_kernel(a_ref, b_ref, out_ref):
    width = a_ref.shape[1]
    slices, depth = out_ref.shape[:2]
    a = -LEARNING_RATE * a_ref[...].astype(jnp.float32)
    b = -LEARNING_RATE * b_ref[...].astype(jnp.float32)
    for i in range(slices):
        at = slice(i * depth, (i + 1) * depth)
        out_ref[i, :, :width] = a[at]
        out_ref[i, :, width:] = b[at]


def sum_kernel(in_ref, out_ref):
    total = jnp.sum(in_ref[...], axis=0, keepdims=True)
    out_ref[...] = jnp.broadcast_to(total, out_ref.shape)


def inner_kernel(a_ref, b_ref, step_ref, hidden_ref, inner_ref, new_b_ref, held_ref, sems):
    rank, width = a_ref.shape
    chunks, tokens, part = held_ref.shape
    copies = [
        pltpu.make_async_copy(
            hidden_ref.at[:, pl.ds(k * part, part)], held_ref.at[k], sems.at[k]
        )
        for k in range(chunks)
    ]
    for copy in copies:
        copy.start()
    steps = jnp.concatenate([step_ref[i] for i in range(step_ref.shape[0])], axis=0)
    new_b_ref[...] = b_ref[...] + steps[:, width:]
    new_a = a_ref[...] + steps[:, :width]
    parts = jnp.concatenate(split_bf16(new_a), axis=0)
    total = jnp.zeros((tokens, 2 * rank), jnp.float32)
    for k in range(chunks):
        copies[k].wait()
        total = total + lax.dot_general(
            held_ref[k],
            parts[:, k * part : (k + 1) * part],
            (((1,), (1,)), ((), ())),
            preferred_element_type=jnp.float32,
        )
    total = total.T
    inner_ref[...] = total[:rank] + total[rank:]


def cache_kernel(length_ref, query_ref, fresh_ref, key_ref, value_ref, part_ref, weight_ref, rows_ref):
    block = pl.program_id(0)
    steps, rows, width = query_ref.shape
    first = block * rows
    ctx, dim = key_ref.shape[1:]
    heads = width // dim
    n_queries = steps * heads
    scale = 1.0 / (dim**0.5)
    for t in range(steps):
        for g in range(heads):
            at = (t * heads + g) * rows
            rows_ref[at : at + rows] = query_ref[t, :, g * dim : (g + 1) * dim].astype(jnp.float32)

    @pl.when(block == 0)
    def _():
        weight_ref[...] = jnp.zeros_like(weight_ref)

    fresh_keys = fresh_ref[...].astype(jnp.bfloat16)
    lane = lax.broadcasted_iota(jnp.int32, (n_queries, 2 * ctx), 1)
    step_of = lax.broadcasted_iota(jnp.int32, (n_queries, 2 * ctx), 0) >> 3
    by_lane = (((1,), (1,)), ((), ()))
    mm = functools.partial(
        lax.dot_general, dimension_numbers=by_lane, preferred_element_type=jnp.float32
    )
    for r in range(0, rows, 2):
        pair = [rows_ref[pl.ds(r + h, n_queries, stride=rows), :] for h in (0, 1)]
        pair = jnp.concatenate(pair, axis=0).astype(jnp.bfloat16)
        cached = mm(pair, key_ref[r : r + 2].reshape(2 * ctx, dim)) * scale
        fresh = mm(pair, fresh_keys) * scale
        weights = []
        for h in (0, 1):
            part = slice(h * n_queries, (h + 1) * n_queries)
            live = (lane >= h * ctx) & (lane < h * ctx + length_ref[first + r + h])
            at = steps * (r + h)
            causal = (lane >= at) & (lane <= at + step_of)
            old = jnp.where(live, cached[part], -jnp.inf)
            new = jnp.where(causal, fresh[part], -jnp.inf)
            top = jnp.max(jnp.maximum(old, new), axis=1, keepdims=True)
            old, new = jnp.exp(old - top), jnp.exp(new - top)
            inverse = 1.0 / jnp.sum(old + new, axis=1, keepdims=True)
            weights.append((old * inverse).astype(jnp.bfloat16))
            new = (new * inverse).astype(jnp.bfloat16).astype(jnp.float32)
            new = pltpu.roll(new, lax.rem(2 * ctx - at + steps * block, 2 * ctx), 1)
            row = pl.ds(r + h, n_queries, stride=rows)
            weight_ref[row, :] = weight_ref[row, :] + new
        part = jnp.dot(
            jnp.concatenate(weights, axis=0),
            value_ref[r : r + 2].reshape(2 * ctx, dim),
            preferred_element_type=jnp.float32,
        )
        for h in (0, 1):
            part_ref[pl.ds(r + h, n_queries, stride=rows), :] = part[
                h * n_queries : (h + 1) * n_queries
            ]


def finish_kernel(base_ref, u0, u1, u2, u3, b_ref, w_ref, cache_ref, out_ref, value_ref):
    t = pl.program_id(0)
    steps, rows, dim = value_ref.shape
    blocks, heads, block_rows = cache_ref.shape[:3]

    @pl.when(t == 0)
    def _():
        u = (u0[...] + u1[...]) + (u2[...] + u3[...])
        u_high, u_low = split_bf16(u)
        b_high, b_low = split_bf16(b_ref[...])
        dims = (((0,), (0,)), ((), ()))
        mm = functools.partial(
            lax.dot_general, dimension_numbers=dims, preferred_element_type=jnp.float32
        )
        delta = mm(u_high, b_high) + (mm(u_low, b_high) + mm(u_high, b_low))
        values = base_ref[...] + ADAPTER_SCALE * delta
        values = values.astype(jnp.bfloat16).astype(jnp.float32)
        for s in range(steps):
            value_ref[s] = values[s * rows : (s + 1) * rows]

    for step in range(steps):

        @pl.when(t == step)
        def _():
            for g in range(heads):
                for i in range(blocks):
                    at = slice(i * block_rows, (i + 1) * block_rows)
                    acc = cache_ref[i, g]
                    weight = w_ref[g]
                    for s in range(step + 1):
                        lane = i * steps + s
                        acc = acc + weight[:, lane : lane + 1] * value_ref[s, at]
                    out_ref[0, at, g * dim : (g + 1) * dim] = acc.astype(out_ref.dtype)


def shards(
    hidden,
    queries,
    rotated_token_keys,
    stored_key_cache,
    stored_value_cache,
    row_cache_length,
    value_weight_matrix,
    adapter_down_factor,
    learner_down_gradient,
    adapter_up_factor,
    learner_up_gradient,
):
    step_count, rows_dev, width_dev = hidden.shape
    heads_dev, ctx_len, head_dim = stored_key_cache.shape[1:]
    group_size = queries.shape[2] // (heads_dev * head_dim)
    rank = adapter_down_factor.shape[0]
    n_dp = lax.axis_size("dp")
    n_mp = lax.axis_size("mp")
    tokens = step_count * rows_dev
    flat_hidden = hidden.reshape(tokens, width_dev)

    small_vmem = pltpu.CompilerParams(vmem_limit_bytes=16 * 1024 * 1024)

    slices = jax.ShapeDtypeStruct((n_dp, rank // n_dp, width_dev + head_dim), jnp.float32)
    terms = pl.pallas_call(terms_kernel, out_shape=slices, compiler_params=small_vmem)(
        learner_down_gradient[0], learner_up_gradient[0].T
    )
    mine = lax.all_to_all(terms, "dp", 0, 0, tiled=True)
    mine = pl.pallas_call(sum_kernel, out_shape=slices, compiler_params=small_vmem)(mine)

    n_chips = n_mp // 2
    here = lax.axis_index("mp")
    place = jnp.stack([here // 2, here % 2]).astype(jnp.int32)
    chunk = jax.ShapeDtypeStruct((n_chips, tokens, head_dim), jnp.float32)
    chunk_spec = pl.BlockSpec((1, tokens, head_dim), lambda k, place: (k, 0, 0))
    keep, send = pl.pallas_call(
        project_kernel,
        grid_spec=pltpu.PrefetchScalarGridSpec(
            num_scalar_prefetch=1,
            grid=(n_chips,),
            in_specs=[
                pl.BlockSpec((tokens, width_dev), lambda k, place: (0, 0)),
                pl.BlockSpec(
                    (width_dev, 2 * head_dim), lambda k, place: (0, lax.rem(place[0] + k, n_chips))
                ),
            ],
            out_specs=[chunk_spec, chunk_spec],
        ),
        out_shape=[chunk, chunk],
        compiler_params=small_vmem,
        cost_estimate=pl.CostEstimate(
            flops=2 * tokens * width_dev * value_weight_matrix.shape[1],
            bytes_accessed=10 * 1024 * 1024,
            transcendentals=0,
        ),
    )(place, flat_hidden, value_weight_matrix)
    core_pairs = [(i, i ^ 1) for i in range(n_mp)]
    along_y = lambda k: [(i, (i + 2 * k) % n_mp) for i in range(n_mp)]
    paired = keep + lax.ppermute(send, "mp", core_pairs)
    mine, row_cache_length, paired = lax.optimization_barrier((mine, row_cache_length, paired))
    steps_ab = lax.all_to_all(mine, "dp", 0, 0, tiled=True)
    base_parts = [paired[0]] + [
        lax.ppermute(paired[k], "mp", along_y(k)) for k in range(1, n_chips)
    ]

    blocks = 4
    block_rows = rows_dev // blocks
    n_queries = step_count * group_size
    by_row = jax.ShapeDtypeStruct((rows_dev * n_queries, head_dim), jnp.float32)
    by_row_spec = pl.BlockSpec((block_rows * n_queries, head_dim), lambda i, _: (i, 0))
    cache_spec = pl.BlockSpec((block_rows, ctx_len, head_dim), lambda i, _: (i, 0, 0))
    keys_new = rotated_token_keys.astype(jnp.float32).transpose(1, 0, 2)
    cache_part, fresh_weights = pl.pallas_call(
        cache_kernel,
        grid_spec=pltpu.PrefetchScalarGridSpec(
            num_scalar_prefetch=1,
            grid=(blocks,),
            in_specs=[
                pl.BlockSpec(
                    (step_count, block_rows, group_size * head_dim), lambda i, _: (0, i, 0)
                ),
                pl.BlockSpec((block_rows * step_count, head_dim), lambda i, _: (i, 0)),
                cache_spec,
                cache_spec,
            ],
            out_specs=[
                by_row_spec,
                pl.BlockSpec((block_rows * n_queries, head_dim), lambda i, _: (0, 0)),
            ],
            scratch_shapes=[pltpu.VMEM((block_rows * n_queries, head_dim), jnp.float32)],
        ),
        out_shape=[
            by_row,
            jax.ShapeDtypeStruct((block_rows * n_queries, head_dim), jnp.float32),
        ],
        compiler_params=small_vmem,
        cost_estimate=pl.CostEstimate(
            flops=2 * 2 * 2 * rows_dev * n_queries * ctx_len * head_dim,
            bytes_accessed=10 * 1024 * 1024,
            transcendentals=rows_dev * n_queries * ctx_len,
        ),
    )(
        row_cache_length,
        queries,
        keys_new.reshape(rows_dev * step_count, head_dim),
        stored_key_cache[:, 0],
        stored_value_cache[:, 0],
    )

    base = (base_parts[0] + base_parts[1]) + (base_parts[2] + base_parts[3])
    steps_ab, cache_part, fresh_weights, base = lax.optimization_barrier(
        (steps_ab, cache_part, fresh_weights, base)
    )
    inner, new_b = pl.pallas_call(
        inner_kernel,
        out_shape=[
            jax.ShapeDtypeStruct((rank, tokens), jnp.float32),
            jax.ShapeDtypeStruct((rank, head_dim), jnp.float32),
        ],
        in_specs=[pl.BlockSpec(memory_space=pltpu.VMEM)] * 3
        + [pl.BlockSpec(memory_space=pltpu.HBM)],
        out_specs=[pl.BlockSpec(memory_space=pltpu.VMEM)] * 2,
        scratch_shapes=[
            pltpu.VMEM((8, tokens, width_dev // 8), jnp.bfloat16),
            pltpu.SemaphoreType.DMA((8,)),
        ],
        compiler_params=small_vmem,
        cost_estimate=pl.CostEstimate(
            flops=4 * tokens * width_dev * rank, bytes_accessed=1024 * 1024, transcendentals=0
        ),
    )(adapter_down_factor, adapter_up_factor.T, steps_ab, flat_hidden)
    inner = inner + lax.ppermute(inner, "mp", core_pairs)
    inner_parts = [inner] + [lax.ppermute(inner, "mp", along_y(k)) for k in range(1, n_chips)]

    by_query = (blocks, n_queries, block_rows, head_dim)

    whole = lambda a: pl.BlockSpec(a.shape, lambda t: (0,) * a.ndim)
    small = [base, *inner_parts, new_b]
    part_spec = pl.BlockSpec((blocks, group_size, block_rows, head_dim), lambda t: (0, t, 0, 0))
    weight_spec = pl.BlockSpec((group_size, block_rows, head_dim), lambda t: (t, 0, 0))
    return pl.pallas_call(
        finish_kernel,
        grid=(step_count,),
        out_shape=jax.ShapeDtypeStruct(queries.shape, jnp.bfloat16),
        in_specs=[whole(a) for a in small] + [weight_spec, part_spec],
        out_specs=pl.BlockSpec((1, rows_dev, group_size * head_dim), lambda t: (t, 0, 0)),
        scratch_shapes=[pltpu.VMEM((step_count, rows_dev, head_dim), jnp.float32)],
        compiler_params=small_vmem,
    )(*small, fresh_weights.reshape(by_query[1:]), cache_part.reshape(by_query))


def solution(mesh):
    placed = (
        P(None, "dp", "mp"),
        P(None, "dp", "mp"),
        P(None, "dp", "mp"),
        P("dp", "mp", None, None),
        P("dp", "mp", None, None),
        P("dp"),
        P("mp", None),
        P(None, "mp"),
        P("dp", None, "mp"),
        P("mp", None),
        P("dp", "mp", None),
    )
    return jax.shard_map(
        shards, mesh=mesh, in_specs=placed, out_specs=P(None, "dp", "mp"), check_vma=False
    )
```

time: 97.5 us -> 94.8 us (0.972)
  Pallas kernels: 3.04 us -> 35.9 us
  between operations: 13.6 us -> 0.19 us
  matrix products: 13 us -> 0 us
  waiting for transfers between devices: 22.9 us -> 15.7 us
  starting transfers between devices: 26.2 us -> 28.4 us
  other arithmetic: 4.4 us -> 2.25 us
  local copies, waits for them, and re-layouts: 13.9 us -> 11.9 us
    pallas_call x1 -> x6, Pallas kernels: 3.04 us -> 35.9 us  [the longest x1 24.1 us: shards(): pl.pallas_call(cache_kernel, grid_spec=pltpu.PrefetchScalarGridSpec(num_s...]
    dot_general x5 -> x0, matrix products: 13 us -> none  [the longest x1 5.89 us: shards(): lax.dot_general(value_weight_matrix, flat_hidden, (((0,), (1,)), ((), ())...]
    all_to_all x2, waiting for transfers between devices: 17.2 us -> 4.47 us  [the longest x1 4.47 us: shards(): mine = lax.all_to_all(terms, 'dp', 0, 0, tiled=True)]
    reshape x6 -> x1, local copies, waits for them, and re-layouts: 5.8 us -> 0.17 us  [shards(): keys_new.reshape(rows_dev * step_count, head_dim)]
    ppermute x4 -> x8, waiting for transfers between devices: 5.72 us -> 11.2 us  [the longest x3 7.97 us: shards(): lax.ppermute(inner, 'mp', along_y(k))]
    unnamed x19 -> x32, local copies, waits for them, and re-layouts: 6.74 us -> 10.4 us
    reduce_sum x3 -> x0, other arithmetic: 2.84 us -> none  [the longest x2 2.66 us: shards(): denominator = jnp.sum(cache_exp, axis=-1) + jnp.sum(fresh_exp, axis=-1)]
    ppermute x4 -> x8, starting transfers between devices: 8.93 us -> 11.1 us  [the longest x3 3.85 us: shards(): lax.ppermute(paired[k], 'mp', along_y(k))]
  transfers between devices with their start and end apart: 7 -> 10, of which waited for: 5 -> 6; matrix products, arithmetic and copies ran while one was open for 21% -> 4% of each run, Pallas kernels for 0% -> 30%
where the time goes in v2:
time: 94.8 us; the launch traced here: 94.3 us
  Pallas kernels  35.9 us (38%)
  starting transfers between devices  28.4 us (30%)
  waiting for transfers between devices  15.7 us (17%)
  local copies, waits for them, and re-layouts  11.9 us (13%)
  other arithmetic  2.25 us (2%)
    pallas_call x1, Pallas kernels, shards(): pl.pallas_call(cache_kernel, grid_spec=pltpu.PrefetchScalarGridSpec(num_s...  24.1 us
    all_to_all x1, starting transfers between devices, shards(): mine = lax.all_to_all(terms, 'dp', 0, 0, tiled=True)  11.9 us
    unnamed x32, local copies, waits for them, and re-layouts  10.4 us
    ppermute x3, waiting for transfers between devices, shards(): lax.ppermute(inner, 'mp', along_y(k))  7.97 us
    all_to_all x1, starting transfers between devices, shards(): steps_ab = lax.all_to_all(mine, 'dp', 0, 0, tiled=True)  5.36 us
    all_to_all x1, waiting for transfers between devices, shards(): mine = lax.all_to_all(terms, 'dp', 0, 0, tiled=True)  4.47 us
    pallas_call x1, Pallas kernels, shards(): pl.pallas_call(project_kernel, grid_spec=pltpu.PrefetchScalarGridSpec(num...  4.09 us
    ppermute x3, starting transfers between devices, shards(): lax.ppermute(paired[k], 'mp', along_y(k))  3.85 us
  transfers between devices with their start and end apart: 10, of which 6 were waited for; matrix products, arithmetic and copies ran while one was open for 4% of the time, Pallas kernels for 30%

profile of v2, /device:TPU:1, one launch (start us, length us, event | category | flops | bytes accessed | tf_op | source)
XLA Modules:
  0.0 94.3 jit_solution(14090530378701984937)
XLA Ops:
  0.0 0.9 %copy-done.10 = bf16[1,64,2048]{2,1,0:T(8,128)(2,1)S(1)} copy-done((bf16[1,64,2048]{2,1,0:T(8,128)(2,1)S(1)}, bf16[1,64,2048]{2,1,0:T(8,128)(2,1)}, u32[]{:S(2)}) %copy-start.10) | copy-done | bytes 262168
  1.0 0.7 copy-done.12
  1.7 0.9 shard_map.109
  2.6 11.9 %all-to-all-start = ((f32[32,2,2176]{2,1,0:T(2,128)}), f32[32,2,2176]{2,1,0:T(2,128)S(1)}, u32[]{:S(2)}, u32[]{:S(2)}) async-start(f32[32,2,2176]{2,1,0:T(2,128)} %shard_map.109), calls=%async_computation | async-start | bytes 1114112 | tf_op jit(solution)/shard_map/all_to_all | solution.py:192
  14.5 0.1 pad_add_fusion.place_ref
  14.5 1.6 %copy-done.2 = bf16[4,128,2048]{2,1,0:T(8,128)(2,1)S(1)} copy-done((bf16[4,128,2048]{2,1,0:T(8,128)(2,1)S(1)}, bf16[4,128,2048]{2,1,0:T(8,128)(2,1)}, u32[]{:S(2)}) %copy-start.2) | copy-done | bytes 2097176
  16.1 2.2 %copy-done.14 = bf16[2048,1024]{1,0:T(8,128)(2,1)S(1)} copy-done((bf16[2048,1024]{1,0:T(8,128)(2,1)S(1)}, bf16[2048,1024]{1,0:T(8,128)(2,1)}, u32[]{:S(2)}) %copy-start.14) | copy-done | bytes 4194328
  18.3 4.1 %shard_map.111 = (f32[4,512,128]{2,1,0:T(8,128)S(1)}, f32[4,512,128]{2,1,0:T(8,128)S(1)}) custom-call(s32[2]{0:T(128)S(1)} %pad_add_fusion.place_ref, bf16[512,2048]{1,0:T(8,128)(2,1)S(1)} %bitcast.27, bf16[2048,1024]{1,0:T(8,128)(2,1)S(1)} %copy-done.14), custom_call_target="tpu_custom_call" | custom-call | flops 2147483648 | bytes 10485760 | tf_op jit(solution)/shard_map/pallas_call | solution.py:200
  22.4 1.0 %collective-permute-start = (f32[4,512,128]{2,1,0:T(8,128)S(1)}, f32[4,512,128]{2,1,0:T(8,128)S(1)}, u32[]{:S(2)}, u32[]{:S(2)}) collective-permute-start(f32[4,512,128]{2,1,0:T(8,128)S(1)} %get-tuple-element.19), channel_id=1, source_target_pairs={{0,1},{1,0},{2,3},{3,2},{4,5},{5,4},{6,7},{7,6},{8,9},{9,8},{10,11... | collective-permute-start | bytes 3145736 | tf_op jit(solution)/shard_map/ppermute | solution.py:223
  23.5 2.3 %collective-permute-done = f32[4,512,128]{2,1,0:T(8,128)S(1)} collective-permute-done((f32[4,512,128]{2,1,0:T(8,128)S(1)}, f32[4,512,128]{2,1,0:T(8,128)S(1)}, u32[]{:S(2)}, u32[]{:S(2)}) %collective-permute-start) | collective-permute-done | bytes 1048608 | tf_op jit(solution)/shard_map/ppermute | solution.py:223
  25.7 1.1 %add.21 = f32[4,512,128]{2,1,0:T(8,128)} add(f32[4,512,128]{2,1,0:T(8,128)S(1)} %get-tuple-element.18, f32[4,512,128]{2,1,0:T(8,128)S(1)} %collective-permute-done) | non-fusion elementwise | flops 262144 | bytes 3145728 | tf_op jit(solution)/shard_map/add | solution.py:223
  26.8 4.5 %all-to-all-done.in_ref = f32[32,2,2176]{2,1,0:T(2,128)S(1)} async-done(((f32[32,2,2176]{2,1,0:T(2,128)}), f32[32,2,2176]{2,1,0:T(2,128)S(1)}, u32[]{:S(2)}, u32[]{:S(2)}) %all-to-all-start) | async-done | bytes 557088 | tf_op jit(solution)/shard_map/all_to_all | solution.py:192
  31.3 1.1 %shard_map.110 = f32[32,2,2176]{2,1,0:T(2,128)} custom-call(f32[32,2,2176]{2,1,0:T(2,128)S(1)} %all-to-all-done.in_ref), custom_call_target="tpu_custom_call" | custom-call | tf_op jit(solution)/shard_map/pallas_call | solution.py:193
  32.4 5.4 %all-to-all-start.1 = ((f32[32,2,2176]{2,1,0:T(2,128)}), f32[32,2,2176]{2,1,0:T(2,128)S(1)}, u32[]{:S(2)}, u32[]{:S(2)}) async-start(f32[32,2,2176]{2,1,0:T(2,128)} %shard_map.110), calls=%async_computation.1 | async-start | bytes 1114112 | tf_op jit(solution)/shard_map/all_to_all | solution.py:225
  37.8 0.0 copy-start.1
  37.8 1.3 %slice_bitcast_fusion = (f32[512,128]{1,0:T(8,128)S(1)}, f32[512,128]{1,0:T(8,128)S(1)}, f32[512,128]{1,0:T(8,128)S(1)}) fusion(f32[4,512,128]{2,1,0:T(8,128)} %add.21), kind=kLoop, calls=%fused_computation.3 | loop fusion | bytes 1572864 | tf_op jit(solution)/shard_map/squeeze | solution.py:227
  39.1 2.8 %collective-permute-start.3 = (f32[512,128]{1,0:T(8,128)S(1)}, f32[512,128]{1,0:T(8,128)S(1)}, u32[]{:S(2)}, u32[]{:S(2)}) collective-permute-start(f32[512,128]{1,0:T(8,128)S(1)} %get-tuple-element.31), channel_id=1, source_target_pairs={{0,6},{1,7},{2,0},{3,1},{4,2},{5,3},{6,4},{7,5},{8,14},{9,15},{10,... | collective-permute-start | bytes 786440 | tf_op jit(solution)/shard_map/ppermute | solution.py:227
  41.9 0.3 collective-permute-start.2
  42.3 0.7 collective-permute-start.1
  42.9 0.0 copy-done.15
  43.0 0.2 copy.12
  43.1 0.0 copy-done
  43.2 0.0 copy-done.13
  43.2 0.0 copy-done.1
  43.2 0.0 copy-start.6
  43.2 1.2 %copy-done.6 = bf16[4,128,1024]{2,1,0:T(8,128)(2,1)S(1)} copy-done((bf16[4,128,1024]{2,1,0:T(8,128)(2,1)S(1)}, bf16[4,128,1024]{2,1,0:T(8,128)(2,1)}, u32[]{:S(2)}) %copy-start.6) | copy-done | bytes 1048600
  44.4 24.1 %shard_map.112 = (f32[4096,128]{1,0:T(8,128)S(1)}, f32[1024,128]{1,0:T(8,128)S(1)}) custom-call(s32[128]{0:T(128)S(1)} %copy-done.13, bf16[4,128,1024]{2,1,0:T(8,128)(2,1)S(1)} %copy-done.6, f32[512,128]{1,0:T(8,128)S(1)} %bitcast.30, bf16[128,64,128]{2,1,0:T(8,128)(2,1)S(1)} %bitcast.25, bf16[128,64,128]{2,1,0:T(8,128)(2,1)S(1)} %bitcast.26), custom_call_target="tpu_custom_call" | custom-call | flops 268435456 | bytes 10485760 | tf_op jit(solution)/shard_map/pallas_call | solution.py:237
  68.5 0.0 copy-start.4
  68.5 1.3 %copy-done.4 = f32[4096,128]{1,0:T(8,128)} copy-done((f32[4096,128]{1,0:T(8,128)}, f32[4096,128]{1,0:T(8,128)S(1)}, u32[]{:S(2)}) %copy-start.4) | copy-done | bytes 2097176
  69.8 0.8 copy-done.8
  70.6 0.0 collective-permute-done.3
  70.6 0.0 collective-permute-done.2
  70.6 0.0 collective-permute-done.1
  70.6 0.0 copy-start.9
  70.6 1.1 %fusion.base_ref = f32[512,128]{1,0:T(8,128)S(1)} fusion(f32[512,128]{1,0:T(8,128)S(1)} %collective-permute-done.1, f32[512,128]{1,0:T(8,128)S(1)} %collective-permute-done.2, f32[512,128]{1,0:T(8,128)S(1)} %collective-permute-done.3, f32[4,512,128]{2,1,0:T(8,128)} %add.21), kind=kLoop, calls=%fused_computation.1 | loop fusion | flops 196608 | bytes 1310720 | tf_op jit(solution)/shard_map/add | solution.py:274
  71.7 0.0 all-to-all-done.1.step_ref
  71.7 0.0 copy-start.3
  71.8 1.6 %copy-done.3 = bf16[4,128,2048]{2,1,0:T(8,128)(2,1)S(1)} copy-done((bf16[4,128,2048]{2,1,0:T(8,128)(2,1)S(1)}, bf16[4,128,2048]{2,1,0:T(8,128)(2,1)}, u32[]{:S(2)}) %copy-start.3) | copy-done | bytes 2097176
  73.3 2.3 %shard_map.113 = (f32[64,512]{1,0:T(8,128)S(1)}, f32[64,128]{1,0:T(8,128)S(1)}) custom-call(f32[64,2048]{1,0:T(8,128)S(1)} %copy-done.7, f32[64,128]{1,0:T(8,128)S(1)} %bitcast.33, f32[32,2,2176]{2,1,0:T(2,128)S(1)} %all-to-all-done.1.step_ref, bf16[512,2048]{1,0:T(8,128)(2,1)S(1)} %bitcast.28), custom_call_target="tpu_custom_call" | custom-call | flops 268435456 | bytes 1048576 | tf_op jit(solution)/shard_map/pallas_call | solution.py:278
  75.6 2.8 %collective-permute-start.4 = (f32[64,512]{1,0:T(8,128)S(1)}, f32[64,512]{1,0:T(8,128)S(1)}, u32[]{:S(2)}, u32[]{:S(2)}) collective-permute-start(f32[64,512]{1,0:T(8,128)S(1)} %get-tuple-element.27), channel_id=1, source_target_pairs={{0,1},{1,0},{2,3},{3,2},{4,5},{5,4},{6,7},{7,6},{8,9},{9,8},{10,11... | collective-permute-start | bytes 393224 | tf_op jit(solution)/shard_map/ppermute | solution.py:296
  78.4 1.0 %collective-permute-done.4 = f32[64,512]{1,0:T(8,128)S(1)} collective-permute-done((f32[64,512]{1,0:T(8,128)S(1)}, f32[64,512]{1,0:T(8,128)S(1)}, u32[]{:S(2)}, u32[]{:S(2)}) %collective-permute-start.4) | collective-permute-done | bytes 131104 | tf_op jit(solution)/shard_map/ppermute | solution.py:296
  79.4 2.1 %collective-permute-start.7 = (f32[64,512]{1,0:T(8,128)S(1)}, f32[64,512]{1,0:T(8,128)S(1)}, u32[]{:S(2)}, u32[]{:S(2)}) collective-permute-start(f32[64,512]{1,0:T(8,128)S(1)} %add.25.u0), channel_id=1, source_target_pairs={{0,6},{1,7},{2,0},{3,1},{4,2},{5,3},{6,4},{7,5},{8,14},{9,15},{10,... | collective-permute-start | bytes 393224 | tf_op jit(solution)/shard_map/ppermute | solution.py:297
  81.5 1.4 %collective-permute-start.6 = (f32[64,512]{1,0:T(8,128)S(1)}, f32[64,512]{1,0:T(8,128)S(1)}, u32[]{:S(2)}, u32[]{:S(2)}) collective-permute-start(f32[64,512]{1,0:T(8,128)S(1)} %add.25.u0), channel_id=1, source_target_pairs={{0,4},{1,5},{2,6},{3,7},{4,0},{5,1},{6,2},{7,3},{8,12},{9,13},{10,... | collective-permute-start | bytes 393224 | tf_op jit(solution)/shard_map/ppermute | solution.py:297
  82.9 0.0 collective-permute-start.5
  82.9 1.6 %collective-permute-done.7.u3 = f32[64,512]{1,0:T(8,128)S(1)} collective-permute-done((f32[64,512]{1,0:T(8,128)S(1)}, f32[64,512]{1,0:T(8,128)S(1)}, u32[]{:S(2)}, u32[]{:S(2)}) %collective-permute-start.7) | collective-permute-done | bytes 131104 | tf_op jit(solution)/shard_map/ppermute | solution.py:297
  84.5 2.9 %collective-permute-done.6.u2 = f32[64,512]{1,0:T(8,128)S(1)} collective-permute-done((f32[64,512]{1,0:T(8,128)S(1)}, f32[64,512]{1,0:T(8,128)S(1)}, u32[]{:S(2)}, u32[]{:S(2)}) %collective-permute-start.6) | collective-permute-done | bytes 131104 | tf_op jit(solution)/shard_map/ppermute | solution.py:297
  87.4 3.5 %collective-permute-done.5.u1 = f32[64,512]{1,0:T(8,128)S(1)} collective-permute-done((f32[64,512]{1,0:T(8,128)S(1)}, f32[64,512]{1,0:T(8,128)S(1)}, u32[]{:S(2)}, u32[]{:S(2)}) %collective-permute-start.5) | collective-permute-done | bytes 131104 | tf_op jit(solution)/shard_map/ppermute | solution.py:297
  90.9 3.4 %shard_map.114 = bf16[4,128,1024]{2,1,0:T(8,128)(2,1)} custom-call(f32[512,128]{1,0:T(8,128)S(1)} %fusion.base_ref, f32[64,512]{1,0:T(8,128)S(1)} %add.25.u0, f32[64,512]{1,0:T(8,128)S(1)} %collective-permute-done.5.u1, f32[64,512]{1,0:T(8,128)S(1)} %collective-permute-done.6.u2, f32[64,512]{1,0:T(8,128)S(1)} %collective-permute-done.7.u3, ...), custom_call_target="tpu_custom_call" | custom-call | tf_op jit(solution)/shard_map/pallas_call | solution.py:305
  (17 shorter events, 0.1 us)
Async XLA Ops:
  0.0 0.9 %copy-start.10 = (bf16[1,64,2048]{2,1,0:T(8,128)(2,1)S(1)}, bf16[1,64,2048]{2,1,0:T(8,128)(2,1)}, u32[]{:S(2)}) copy-start(bf16[1,64,2048]{2,1,0:T(8,128)(2,1)} %param.19) | copy-start | bytes 786436
  1.0 0.7 copy-start.12
  2.6 28.7 %all-to-all-start = ((f32[32,2,2176]{2,1,0:T(2,128)}), f32[32,2,2176]{2,1,0:T(2,128)S(1)}, u32[]{:S(2)}, u32[]{:S(2)}) async-start(f32[32,2,2176]{2,1,0:T(2,128)} %shard_map.109), calls=%async_computation | async-start | bytes 1114112 | tf_op jit(solution)/shard_map/all_to_all | solution.py:192
  14.5 1.6 %copy-start.2 = (bf16[4,128,2048]{2,1,0:T(8,128)(2,1)S(1)}, bf16[4,128,2048]{2,1,0:T(8,128)(2,1)}, u32[]{:S(2)}) copy-start(bf16[4,128,2048]{2,1,0:T(8,128)(2,1)} %param.11) | copy-start | bytes 6291460
  16.1 2.2 %copy-start.14 = (bf16[2048,1024]{1,0:T(8,128)(2,1)S(1)}, bf16[2048,1024]{1,0:T(8,128)(2,1)}, u32[]{:S(2)}) copy-start(bf16[2048,1024]{1,0:T(8,128)(2,1)} %weight_ref.1) | copy-start | bytes 12582916
  22.4 3.3 %collective-permute-start = (f32[4,512,128]{2,1,0:T(8,128)S(1)}, f32[4,512,128]{2,1,0:T(8,128)S(1)}, u32[]{:S(2)}, u32[]{:S(2)}) collective-permute-start(f32[4,512,128]{2,1,0:T(8,128)S(1)} %get-tuple-element.19), channel_id=1, source_target_pairs={{0,1},{1,0},{2,3},{3,2},{4,5},{5,4},{6,7},{7,6},{8,9},{9,8},{10,11... | collective-permute-start | bytes 3145736 | tf_op jit(solution)/shard_map/ppermute | solution.py:223
  26.8 16.1 %copy-start.15 = (bf16[4,128,128]{2,1,0:T(8,128)(2,1)S(1)}, bf16[4,128,128]{2,1,0:T(8,128)(2,1)}, u32[]{:S(2)}) copy-start(bf16[4,128,128]{2,1,0:T(8,128)(2,1)} %param.13) | copy-start | bytes 393220
  26.8 16.3 %copy-start = (bf16[128,1,64,128]{3,2,1,0:T(8,128)(2,1)S(1)}, bf16[128,1,64,128]{3,2,1,0:T(8,128)(2,1)}, u32[]{:S(2)}) copy-start(bf16[128,1,64,128]{3,2,1,0:T(8,128)(2,1)} %param.14) | copy-start | bytes 6291460
  26.8 16.3 %copy-start.13 = (s32[128]{0:T(128)S(1)}, s32[128]{0:T(128)}, u32[]{:S(2)}) copy-start(s32[128]{0:T(128)} %length_ref) | copy-start | bytes 1540
  32.4 39.3 %all-to-all-start.1 = ((f32[32,2,2176]{2,1,0:T(2,128)}), f32[32,2,2176]{2,1,0:T(2,128)S(1)}, u32[]{:S(2)}, u32[]{:S(2)}) async-start(f32[32,2,2176]{2,1,0:T(2,128)} %shard_map.110), calls=%async_computation.1 | async-start | bytes 1114112 | tf_op jit(solution)/shard_map/all_to_all | solution.py:225
  37.8 5.4 %copy-start.1 = (bf16[128,1,64,128]{3,2,1,0:T(8,128)(2,1)S(1)}, bf16[128,1,64,128]{3,2,1,0:T(8,128)(2,1)}, u32[]{:S(2)}) copy-start(bf16[128,1,64,128]{3,2,1,0:T(8,128)(2,1)} %param.15) | copy-start | bytes 6291460
  39.1 31.5 %collective-permute-start.3 = (f32[512,128]{1,0:T(8,128)S(1)}, f32[512,128]{1,0:T(8,128)S(1)}, u32[]{:S(2)}, u32[]{:S(2)}) collective-permute-start(f32[512,128]{1,0:T(8,128)S(1)} %get-tuple-element.31), channel_id=1, source_target_pairs={{0,6},{1,7},{2,0},{3,1},{4,2},{5,3},{6,4},{7,5},{8,14},{9,15},{10,... | collective-permute-start | bytes 786440 | tf_op jit(solution)/shard_map/ppermute | solution.py:227
  41.9 28.7 %collective-permute-start.2 = (f32[512,128]{1,0:T(8,128)S(1)}, f32[512,128]{1,0:T(8,128)S(1)}, u32[]{:S(2)}, u32[]{:S(2)}) collective-permute-start(f32[512,128]{1,0:T(8,128)S(1)} %get-tuple-element.32), channel_id=1, source_target_pairs={{0,4},{1,5},{2,6},{3,7},{4,0},{5,1},{6,2},{7,3},{8,12},{9,13},{10,... | collective-permute-start | bytes 786440 | tf_op jit(solution)/shard_map/ppermute | solution.py:227
  42.3 28.4 %collective-permute-start.1 = (f32[512,128]{1,0:T(8,128)S(1)}, f32[512,128]{1,0:T(8,128)S(1)}, u32[]{:S(2)}, u32[]{:S(2)}) collective-permute-start(f32[512,128]{1,0:T(8,128)S(1)} %get-tuple-element.33), channel_id=1, source_target_pairs={{0,2},{1,3},{2,4},{3,5},{4,6},{5,7},{6,0},{7,1},{8,10},{9,11},{10,... | collective-permute-start | bytes 786440 | tf_op jit(solution)/shard_map/ppermute | solution.py:227
  43.2 1.2 %copy-start.6 = (bf16[4,128,1024]{2,1,0:T(8,128)(2,1)S(1)}, bf16[4,128,1024]{2,1,0:T(8,128)(2,1)}, u32[]{:S(2)}) copy-start(bf16[4,128,1024]{2,1,0:T(8,128)(2,1)} %query_ref.1) | copy-start | bytes 3145732
  44.4 27.3 %copy-start.7 = (f32[64,2048]{1,0:T(8,128)S(1)}, f32[64,2048]{1,0:T(8,128)}, u32[]{:S(2)}) copy-start(f32[64,2048]{1,0:T(8,128)} %a_ref.1) | copy-start | bytes 1572868
  44.4 27.3 %copy-start.11 = (f32[128,64]{0,1:T(8,128)S(1)}, f32[128,64]{0,1:T(8,128)}, u32[]{:S(2)}) copy-start(f32[128,64]{0,1:T(8,128)} %param.20) | copy-start | bytes 98308
  68.5 1.3 %copy-start.4 = (f32[4096,128]{1,0:T(8,128)}, f32[4096,128]{1,0:T(8,128)S(1)}, u32[]{:S(2)}) copy-start(f32[4096,128]{1,0:T(8,128)S(1)} %get-tuple-element.30) | copy-start | bytes 6291460
  69.8 0.8 copy-start.8
  70.6 20.2 %copy-start.9 = (f32[1024,128]{1,0:T(8,128)S(1)}, f32[1024,128]{1,0:T(8,128)}, u32[]{:S(2)}) copy-start(f32[1024,128]{1,0:T(8,128)} %copy-done.8) | copy-start | bytes 1572868
  71.7 1.6 %copy-start.3 = (bf16[4,128,2048]{2,1,0:T(8,128)(2,1)S(1)}, bf16[4,128,2048]{2,1,0:T(8,128)(2,1)}, u32[]{:S(2)}) copy-start(bf16[4,128,2048]{2,1,0:T(8,128)(2,1)} %param.11) | copy-start | bytes 6291460
  73.3 17.5 %copy-start.5 = (f32[4096,128]{1,0:T(8,128)S(1)}, f32[4096,128]{1,0:T(8,128)}, u32[]{:S(2)}) copy-start(f32[4096,128]{1,0:T(8,128)} %copy-done.4) | copy-start | bytes 6291460
  75.6 3.8 %collective-permute-start.4 = (f32[64,512]{1,0:T(8,128)S(1)}, f32[64,512]{1,0:T(8,128)S(1)}, u32[]{:S(2)}, u32[]{:S(2)}) collective-permute-start(f32[64,512]{1,0:T(8,128)S(1)} %get-tuple-element.27), channel_id=1, source_target_pairs={{0,1},{1,0},{2,3},{3,2},{4,5},{5,4},{6,7},{7,6},{8,9},{9,8},{10,11... | collective-permute-start | bytes 393224 | tf_op jit(solution)/shard_map/ppermute | solution.py:296
  79.4 5.1 %collective-permute-start.7 = (f32[64,512]{1,0:T(8,128)S(1)}, f32[64,512]{1,0:T(8,128)S(1)}, u32[]{:S(2)}, u32[]{:S(2)}) collective-permute-start(f32[64,512]{1,0:T(8,128)S(1)} %add.25.u0), channel_id=1, source_target_pairs={{0,6},{1,7},{2,0},{3,1},{4,2},{5,3},{6,4},{7,5},{8,14},{9,15},{10,... | collective-permute-start | bytes 393224 | tf_op jit(solution)/shard_map/ppermute | solution.py:297
  81.5 5.9 %collective-permute-start.6 = (f32[64,512]{1,0:T(8,128)S(1)}, f32[64,512]{1,0:T(8,128)S(1)}, u32[]{:S(2)}, u32[]{:S(2)}) collective-permute-start(f32[64,512]{1,0:T(8,128)S(1)} %add.25.u0), channel_id=1, source_target_pairs={{0,4},{1,5},{2,6},{3,7},{4,0},{5,1},{6,2},{7,3},{8,12},{9,13},{10,... | collective-permute-start | bytes 393224 | tf_op jit(solution)/shard_map/ppermute | solution.py:297
  82.9 8.0 %collective-permute-start.5 = (f32[64,512]{1,0:T(8,128)S(1)}, f32[64,512]{1,0:T(8,128)S(1)}, u32[]{:S(2)}, u32[]{:S(2)}) collective-permute-start(f32[64,512]{1,0:T(8,128)S(1)} %add.25.u0), channel_id=1, source_target_pairs={{0,2},{1,3},{2,4},{3,5},{4,6},{5,7},{6,0},{7,1},{8,10},{9,11},{10,... | collective-permute-start | bytes 393224 | tf_op jit(solution)/shard_map/ppermute | solution.py:297

commit v3 on v2

--- a/solution.py
+++ b/solution.py
@@ -42,35 +42,26 @@
     out_ref[...] = jnp.broadcast_to(total, out_ref.shape)
 
 
-def inner_kernel(a_ref, b_ref, step_ref, hidden_ref, inner_ref, new_b_ref, held_ref, sems):
+def inner_kernel(a_ref, b_ref, step_ref, hidden_ref, inner_ref, new_b_ref):
     rank, width = a_ref.shape
-    chunks, tokens, part = held_ref.shape
-    copies = [
-        pltpu.make_async_copy(
-            hidden_ref.at[:, pl.ds(k * part, part)], held_ref.at[k], sems.at[k]
-        )
-        for k in range(chunks)
-    ]
-    for copy in copies:
-        copy.start()
     steps = jnp.concatenate([step_ref[i] for i in range(step_ref.shape[0])], axis=0)
     new_b_ref[...] = b_ref[...] + steps[:, width:]
     new_a = a_ref[...] + steps[:, :width]
     parts = jnp.concatenate(split_bf16(new_a), axis=0)
-    total = jnp.zeros((tokens, 2 * rank), jnp.float32)
-    for k in range(chunks):
-        copies[k].wait()
-        total = total + lax.dot_general(
-            held_ref[k],
-            parts[:, k * part : (k + 1) * part],
-            (((1,), (1,)), ((), ())),
-            preferred_element_type=jnp.float32,
-        )
-    total = total.T
-    inner_ref[...] = total[:rank] + total[rank:]
-
-
-def cache_kernel(length_ref, query_ref, fresh_ref, key_ref, value_ref, part_ref, weight_ref, rows_ref):
+    both = lax.dot_general(
+        hidden_ref[...], parts, (((1,), (1,)), ((), ())), preferred_element_type=jnp.float32
+    )
+    both = both.T
+    inner_ref[...] = both[:rank] + both[rank:]
+
+
+def add_kernel(keep_ref, received_ref, *out_refs):
+    for k, out_ref in enumerate(out_refs):
+        out_ref[...] = keep_ref[k] + received_ref[k]
+
+
+def cache_kernel(length_ref, query_ref, fresh_ref, key_ref, value_ref, part_ref, weight_ref, rows_ref, *scratch):
+    pair_ref, old_ref, new_ref, old_weight_ref, new_weight_ref = scratch
     block = pl.program_id(0)
     steps, rows, width = query_ref.shape
     first = block * rows
@@ -87,49 +78,58 @@
     def _():
         weight_ref[...] = jnp.zeros_like(weight_ref)
 
-    fresh_keys = fresh_ref[...].astype(jnp.bfloat16)
-    lane = lax.broadcasted_iota(jnp.int32, (n_queries, 2 * ctx), 1)
-    step_of = lax.broadcasted_iota(jnp.int32, (n_queries, 2 * ctx), 0) >> 3
+    pairs = rows // 2
+    lanes = 2 * ctx
+    for r in range(rows):
+        row = rows_ref[pl.ds(r, n_queries, stride=rows), :]
+        pair_ref[r * n_queries : (r + 1) * n_queries] = row.astype(jnp.bfloat16)
     by_lane = (((1,), (1,)), ((), ()))
     mm = functools.partial(
         lax.dot_general, dimension_numbers=by_lane, preferred_element_type=jnp.float32
     )
-    for r in range(0, rows, 2):
-        pair = [rows_ref[pl.ds(r + h, n_queries, stride=rows), :] for h in (0, 1)]
-        pair = jnp.concatenate(pair, axis=0).astype(jnp.bfloat16)
-        cached = mm(pair, key_ref[r : r + 2].reshape(2 * ctx, dim)) * scale
-        fresh = mm(pair, fresh_keys) * scale
-        weights = []
-        for h in (0, 1):
-            part = slice(h * n_queries, (h + 1) * n_queries)
-            live = (lane >= h * ctx) & (lane < h * ctx + length_ref[first + r + h])
-            at = steps * (r + h)
-            causal = (lane >= at) & (lane <= at + step_of)
-            old = jnp.where(live, cached[part], -jnp.inf)
-            new = jnp.where(causal, fresh[part], -jnp.inf)
-            top = jnp.max(jnp.maximum(old, new), axis=1, keepdims=True)
-            old, new = jnp.exp(old - top), jnp.exp(new - top)
-            inverse = 1.0 / jnp.sum(old + new, axis=1, keepdims=True)
-            weights.append((old * inverse).astype(jnp.bfloat16))
-            new = (new * inverse).astype(jnp.bfloat16).astype(jnp.float32)
-            new = pltpu.roll(new, lax.rem(2 * ctx - at + steps * block, 2 * ctx), 1)
-            row = pl.ds(r + h, n_queries, stride=rows)
-            weight_ref[row, :] = weight_ref[row, :] + new
-        part = jnp.dot(
-            jnp.concatenate(weights, axis=0),
-            value_ref[r : r + 2].reshape(2 * ctx, dim),
-            preferred_element_type=jnp.float32,
-        )
-        for h in (0, 1):
-            part_ref[pl.ds(r + h, n_queries, stride=rows), :] = part[
-                h * n_queries : (h + 1) * n_queries
-            ]
+    fresh_keys = fresh_ref[...].astype(jnp.bfloat16)
+    both = 2 * n_queries
+    for p in range(pairs):
+        at = slice(p * both, (p + 1) * both)
+        keys = key_ref[2 * p : 2 * p + 2].reshape(lanes, dim)
+        old_ref[at] = mm(pair_ref[at], keys)
+        new_ref[at] = mm(pair_ref[at], fresh_keys)
+
+    lane = lax.broadcasted_iota(jnp.int32, (n_queries, lanes), 1)
+    step_of = lax.broadcasted_iota(jnp.int32, (n_queries, lanes), 0) >> 3
+    for r in range(rows):
+        half = r % 2
+        at = slice(r * n_queries, (r + 1) * n_queries)
+        live = (lane >= half * ctx) & (lane < half * ctx + length_ref[first + r])
+        causal = (lane >= steps * r) & (lane <= steps * r + step_of)
+        old = jnp.where(live, old_ref[at] * scale, -jnp.inf)
+        new = jnp.where(causal, new_ref[at] * scale, -jnp.inf)
+        top = jnp.max(jnp.maximum(old, new), axis=1, keepdims=True)
+        old, new = jnp.exp(old - top), jnp.exp(new - top)
+        inverse = 1.0 / jnp.sum(old + new, axis=1, keepdims=True)
+        old_weight_ref[at] = (old * inverse).astype(jnp.bfloat16)
+        new_weight_ref[at] = (new * inverse).astype(jnp.bfloat16)
+
+    source = lax.broadcasted_iota(jnp.int32, (lanes, lanes), 0)
+    target = lax.broadcasted_iota(jnp.int32, (lanes, lanes), 1)
+    move = (target - steps * block == source % steps).astype(jnp.bfloat16)
+    for p in range(pairs):
+        at = slice(p * both, (p + 1) * both)
+        values = value_ref[2 * p : 2 * p + 2].reshape(lanes, dim)
+        old_ref[at] = jnp.dot(old_weight_ref[at], values, preferred_element_type=jnp.float32)
+        new_ref[at] = jnp.dot(new_weight_ref[at], move, preferred_element_type=jnp.float32)
+    for q in range(n_queries):
+        at = slice(q * rows, (q + 1) * rows)
+        query = pl.ds(q, rows, stride=n_queries)
+        part_ref[at] = old_ref[query, :]
+        weight_ref[at] = weight_ref[at] + new_ref[query, :]
 
 
 def finish_kernel(base_ref, u0, u1, u2, u3, b_ref, w_ref, cache_ref, out_ref, value_ref):
     t = pl.program_id(0)
     steps, rows, dim = value_ref.shape
-    blocks, heads, block_rows = cache_ref.shape[:3]
+    blocks, queries, block_rows = cache_ref.shape[:3]
+    heads = queries // steps
 
     @pl.when(t == 0)
     def _():
@@ -153,8 +153,8 @@
             for g in range(heads):
                 for i in range(blocks):
                     at = slice(i * block_rows, (i + 1) * block_rows)
-                    acc = cache_ref[i, g]
-                    weight = w_ref[g]
+                    acc = cache_ref[i, step * heads + g]
+                    weight = w_ref[step * heads + g]
                     for s in range(step + 1):
                         lane = i * steps + s
                         acc = acc + weight[:, lane : lane + 1] * value_ref[s, at]
@@ -220,7 +220,11 @@
     )(place, flat_hidden, value_weight_matrix)
     core_pairs = [(i, i ^ 1) for i in range(n_mp)]
     along_y = lambda k: [(i, (i + 2 * k) % n_mp) for i in range(n_mp)]
-    paired = keep + lax.ppermute(send, "mp", core_pairs)
+    paired = pl.pallas_call(
+        add_kernel,
+        out_shape=[jax.ShapeDtypeStruct((tokens, head_dim), jnp.float32)] * n_chips,
+        compiler_params=small_vmem,
+    )(keep, lax.ppermute(send, "mp", core_pairs))
     mine, row_cache_length, paired = lax.optimization_barrier((mine, row_cache_length, paired))
     steps_ab = lax.all_to_all(mine, "dp", 0, 0, tiled=True)
     base_parts = [paired[0]] + [
@@ -228,6 +232,7 @@
     ]
 
     blocks = 4
+    f32, bf16 = jnp.float32, jnp.bfloat16
     block_rows = rows_dev // blocks
     n_queries = step_count * group_size
     by_row = jax.ShapeDtypeStruct((rows_dev * n_queries, head_dim), jnp.float32)
@@ -251,13 +256,16 @@
                 by_row_spec,
                 pl.BlockSpec((block_rows * n_queries, head_dim), lambda i, _: (0, 0)),
             ],
-            scratch_shapes=[pltpu.VMEM((block_rows * n_queries, head_dim), jnp.float32)],
+            scratch_shapes=[
+                pltpu.VMEM((block_rows * n_queries, head_dim), kind)
+                for kind in (f32, bf16, f32, f32, bf16, bf16)
+            ],
         ),
         out_shape=[
             by_row,
             jax.ShapeDtypeStruct((block_rows * n_queries, head_dim), jnp.float32),
         ],
-        compiler_params=small_vmem,
+        compiler_params=pltpu.CompilerParams(vmem_limit_bytes=60 * 1024 * 1024),
         cost_estimate=pl.CostEstimate(
             flops=2 * 2 * 2 * rows_dev * n_queries * ctx_len * head_dim,
             bytes_accessed=10 * 1024 * 1024,
@@ -281,13 +289,6 @@
             jax.ShapeDtypeStruct((rank, tokens), jnp.float32),
             jax.ShapeDtypeStruct((rank, head_dim), jnp.float32),
         ],
-        in_specs=[pl.BlockSpec(memory_space=pltpu.VMEM)] * 3
-        + [pl.BlockSpec(memory_space=pltpu.HBM)],
-        out_specs=[pl.BlockSpec(memory_space=pltpu.VMEM)] * 2,
-        scratch_shapes=[
-            pltpu.VMEM((8, tokens, width_dev // 8), jnp.bfloat16),
-            pltpu.SemaphoreType.DMA((8,)),
-        ],
         compiler_params=small_vmem,
         cost_estimate=pl.CostEstimate(
             flops=4 * tokens * width_dev * rank, bytes_accessed=1024 * 1024, transcendentals=0
@@ -298,19 +299,16 @@
 
     by_query = (blocks, n_queries, block_rows, head_dim)
 
-    whole = lambda a: pl.BlockSpec(a.shape, lambda t: (0,) * a.ndim)
-    small = [base, *inner_parts, new_b]
-    part_spec = pl.BlockSpec((blocks, group_size, block_rows, head_dim), lambda t: (0, t, 0, 0))
-    weight_spec = pl.BlockSpec((group_size, block_rows, head_dim), lambda t: (t, 0, 0))
+    operands = [base, *inner_parts, new_b, fresh_weights.reshape(by_query[1:]), cache_part.reshape(by_query)]
     return pl.pallas_call(
         finish_kernel,
         grid=(step_count,),
         out_shape=jax.ShapeDtypeStruct(queries.shape, jnp.bfloat16),
-        in_specs=[whole(a) for a in small] + [weight_spec, part_spec],
+        in_specs=[pl.BlockSpec(memory_space=pltpu.VMEM)] * len(operands),
         out_specs=pl.BlockSpec((1, rows_dev, group_size * head_dim), lambda t: (t, 0, 0)),
         scratch_shapes=[pltpu.VMEM((step_count, rows_dev, head_dim), jnp.float32)],
         compiler_params=small_vmem,
-    )(*small, fresh_weights.reshape(by_query[1:]), cache_part.reshape(by_query))
+    )(*operands)
 
 
 def solution(mesh):

time: 94.8 us -> 75.6 us (0.80)
  Pallas kernels: 35.9 us -> 21.7 us
  local copies, waits for them, and re-layouts: 11.9 us -> 7.04 us
  other arithmetic: 2.25 us -> 1.2 us
    pallas_call x1, Pallas kernels: 24.1 us -> 10.6 us  [shards(): pl.pallas_call(cache_kernel, grid_spec=pltpu.PrefetchScalarGridSpec(num_s...]
    unnamed x32 -> x24, local copies, waits for them, and re-layouts: 10.4 us -> 6.16 us
    pallas_call x1, Pallas kernels: 2.29 us -> 0.83 us  [shards(): pl.pallas_call(inner_kernel, out_shape=[jax.ShapeDtypeStruct((rank, token...]
    squeeze x1 -> x0, local copies, waits for them, and re-layouts: 1.31 us -> none  [shards(): paired[k]]
    ppermute x3, starting transfers between devices: 3.85 us -> 5.06 us  [shards(): lax.ppermute(paired[k], 'mp', along_y(k))]
    add x1 -> x0, other arithmetic: 1.07 us -> none  [shards(): paired = keep + lax.ppermute(send, 'mp', core_pairs)]
  transfers between devices with their start and end apart: 10 -> 10, of which waited for: 6 -> 6; matrix products, arithmetic and copies ran while one was open for 4% -> 3% of each run, Pallas kernels for 30% -> 21%
where the time goes in v3:
time: 75.6 us; the launch traced here: 75.1 us
  starting transfers between devices  29.1 us (38%)
  Pallas kernels  21.7 us (29%)
  waiting for transfers between devices  15.9 us (21%)
  local copies, waits for them, and re-layouts  7.04 us (9%)
  other arithmetic  1.2 us (2%)
    all_to_all x1, starting transfers between devices, shards(): mine = lax.all_to_all(terms, 'dp', 0, 0, tiled=True)  11.9 us
    pallas_call x1, Pallas kernels, shards(): pl.pallas_call(cache_kernel, grid_spec=pltpu.PrefetchScalarGridSpec(num_s...  10.6 us
    ppermute x3, waiting for transfers between devices, shards(): lax.ppermute(inner, 'mp', along_y(k))  8.69 us
    unnamed x24, local copies, waits for them, and re-layouts  6.16 us
    all_to_all x1, starting transfers between devices, shards(): steps_ab = lax.all_to_all(mine, 'dp', 0, 0, tiled=True)  5.54 us
    ppermute x3, starting transfers between devices, shards(): lax.ppermute(paired[k], 'mp', along_y(k))  5.06 us
    pallas_call x1, Pallas kernels, shards(): pl.pallas_call(project_kernel, grid_spec=pltpu.PrefetchScalarGridSpec(num...  4.09 us
    all_to_all x1, waiting for transfers between devices, shards(): mine = lax.all_to_all(terms, 'dp', 0, 0, tiled=True)  3.96 us
  transfers between devices with their start and end apart: 10, of which 6 were waited for; matrix products, arithmetic and copies ran while one was open for 3% of the time, Pallas kernels for 21%

profile of v3, /device:TPU:1, one launch (start us, length us, event | category | flops | bytes accessed | tf_op | source)
XLA Modules:
  0.0 75.1 jit_solution(3049216925039570100)
XLA Ops:
  0.0 0.0 copy-start.5
  0.0 0.9 %copy-done.5 = bf16[1,64,2048]{2,1,0:T(8,128)(2,1)S(1)} copy-done((bf16[1,64,2048]{2,1,0:T(8,128)(2,1)S(1)}, bf16[1,64,2048]{2,1,0:T(8,128)(2,1)}, u32[]{:S(2)}) %copy-start.5) | copy-done | bytes 262168
  1.0 0.7 copy-done.9
  1.7 0.9 %shard_map.109 = f32[32,2,2176]{2,1,0:T(2,128)} custom-call(bf16[64,2048]{1,0:T(8,128)(2,1)S(1)} %bitcast.19, bf16[64,128]{1,0:T(8,128)(2,1)S(1)} %bitcast.21), custom_call_target="tpu_custom_call" | custom-call | tf_op jit(solution)/shard_map/pallas_call | solution.py:189
  2.6 11.9 %all-to-all-start = ((f32[32,2,2176]{2,1,0:T(2,128)}), f32[32,2,2176]{2,1,0:T(2,128)S(1)}, u32[]{:S(2)}, u32[]{:S(2)}) async-start(f32[32,2,2176]{2,1,0:T(2,128)} %shard_map.109), calls=%async_computation | async-start | bytes 1114112 | tf_op jit(solution)/shard_map/all_to_all | solution.py:192
  14.5 0.1 pad_add_fusion.place_ref
  14.5 0.0 copy-start
  14.5 1.6 %copy-done = bf16[4,128,2048]{2,1,0:T(8,128)(2,1)S(1)} copy-done((bf16[4,128,2048]{2,1,0:T(8,128)(2,1)S(1)}, bf16[4,128,2048]{2,1,0:T(8,128)(2,1)}, u32[]{:S(2)}) %copy-start) | copy-done | bytes 2097176
  16.1 0.0 copy-start.10
  16.1 2.2 %copy-done.10 = bf16[2048,1024]{1,0:T(8,128)(2,1)S(1)} copy-done((bf16[2048,1024]{1,0:T(8,128)(2,1)S(1)}, bf16[2048,1024]{1,0:T(8,128)(2,1)}, u32[]{:S(2)}) %copy-start.10) | copy-done | bytes 4194328
  18.3 4.1 %shard_map.111 = (f32[4,512,128]{2,1,0:T(8,128)S(1)}, f32[4,512,128]{2,1,0:T(8,128)S(1)}) custom-call(s32[2]{0:T(128)S(1)} %pad_add_fusion.place_ref, bf16[512,2048]{1,0:T(8,128)(2,1)S(1)} %bitcast.15, bf16[2048,1024]{1,0:T(8,128)(2,1)S(1)} %copy-done.10), custom_call_target="tpu_custom_call" | custom-call | flops 2147483648 | bytes 10485760 | tf_op jit(solution)/shard_map/pallas_call | solution.py:200
  22.4 1.0 %collective-permute-start = (f32[4,512,128]{2,1,0:T(8,128)S(1)}, f32[4,512,128]{2,1,0:T(8,128)S(1)}, u32[]{:S(2)}, u32[]{:S(2)}) collective-permute-start(f32[4,512,128]{2,1,0:T(8,128)S(1)} %get-tuple-element.26), channel_id=1, source_target_pairs={{0,1},{1,0},{2,3},{3,2},{4,5},{5,4},{6,7},{7,6},{8,9},{9,8},{10,11... | collective-permute-start | bytes 3145736 | tf_op jit(solution)/shard_map/ppermute | solution.py:227
  23.5 2.3 %collective-permute-done.received_ref = f32[4,512,128]{2,1,0:T(8,128)S(1)} collective-permute-done((f32[4,512,128]{2,1,0:T(8,128)S(1)}, f32[4,512,128]{2,1,0:T(8,128)S(1)}, u32[]{:S(2)}, u32[]{:S(2)}) %collective-permute-start) | collective-permute-done | bytes 1048608 | tf_op jit(solution)/shard_map/ppermute | solution.py:227
  25.7 0.0 copy-start.11
  25.7 0.9 %shard_map.112 = (f32[512,128]{1,0:T(8,128)S(1)}, f32[512,128]{1,0:T(8,128)}, f32[512,128]{1,0:T(8,128)}, f32[512,128]{1,0:T(8,128)S(1)}) custom-call(f32[4,512,128]{2,1,0:T(8,128)S(1)} %get-tuple-element.25.keep_ref, f32[4,512,128]{2,1,0:T(8,128)S(1)} %collective-permute-done.received_ref), custom_call_target="tpu_custom_call" | custom-call | tf_op jit(solution)/shard_map/pallas_call | solution.py:223
  26.6 0.7 copy-done.6
  27.3 4.0 %all-to-all-done.in_ref = f32[32,2,2176]{2,1,0:T(2,128)S(1)} async-done(((f32[32,2,2176]{2,1,0:T(2,128)}), f32[32,2,2176]{2,1,0:T(2,128)S(1)}, u32[]{:S(2)}, u32[]{:S(2)}) %all-to-all-start) | async-done | bytes 557088 | tf_op jit(solution)/shard_map/all_to_all | solution.py:192
  31.3 1.1 %shard_map.110 = f32[32,2,2176]{2,1,0:T(2,128)} custom-call(f32[32,2,2176]{2,1,0:T(2,128)S(1)} %all-to-all-done.in_ref), custom_call_target="tpu_custom_call" | custom-call | tf_op jit(solution)/shard_map/pallas_call | solution.py:193
  32.4 5.5 %all-to-all-start.1 = ((f32[32,2,2176]{2,1,0:T(2,128)}), f32[32,2,2176]{2,1,0:T(2,128)S(1)}, u32[]{:S(2)}, u32[]{:S(2)}) async-start(f32[32,2,2176]{2,1,0:T(2,128)} %shard_map.110), calls=%async_computation.1 | async-start | bytes 1114112 | tf_op jit(solution)/shard_map/all_to_all | solution.py:229
  37.9 1.4 %collective-permute-start.1 = (f32[512,128]{1,0:T(8,128)}, f32[512,128]{1,0:T(8,128)S(1)}, u32[]{:S(2)}, u32[]{:S(2)}) collective-permute-start(f32[512,128]{1,0:T(8,128)} %get-tuple-element.36), channel_id=1, source_target_pairs={{0,2},{1,3},{2,4},{3,5},{4,6},{5,7},{6,0},{7,1},{8,10},{9,11},{10,... | collective-permute-start | bytes 786440 | tf_op jit(solution)/shard_map/ppermute | solution.py:231
  39.3 2.6 %collective-permute-start.2 = (f32[512,128]{1,0:T(8,128)}, f32[512,128]{1,0:T(8,128)}, u32[]{:S(2)}, u32[]{:S(2)}) collective-permute-start(f32[512,128]{1,0:T(8,128)} %get-tuple-element.37), channel_id=1, source_target_pairs={{0,4},{1,5},{2,6},{3,7},{4,0},{5,1},{6,2},{7,3},{8,12},{9,13},{10,... | collective-permute-start | bytes 786440 | tf_op jit(solution)/shard_map/ppermute | solution.py:231
  41.9 1.1 %collective-permute-start.3 = (f32[512,128]{1,0:T(8,128)S(1)}, f32[512,128]{1,0:T(8,128)}, u32[]{:S(2)}, u32[]{:S(2)}) collective-permute-start(f32[512,128]{1,0:T(8,128)S(1)} %get-tuple-element.38), channel_id=1, source_target_pairs={{0,6},{1,7},{2,0},{3,1},{4,2},{5,3},{6,4},{7,5},{8,14},{9,15},{10,... | collective-permute-start | bytes 786440 | tf_op jit(solution)/shard_map/ppermute | solution.py:231
  43.0 0.0 copy-done.11
  43.0 0.9 %copy.12 = f32[128,4,128]{2,1,0:T(4,128)} copy(f32[128,4,128]{2,0,1:T(8,128)S(1)} %convert_bitcast_fusion) | data formatting | bytes 524288 | tf_op jit(solution)/shard_map/reshape | solution.py:277
  43.9 10.6 %shard_map.113 = (f32[4096,128]{1,0:T(8,128)}, f32[1024,128]{1,0:T(8,128)}) custom-call(s32[128]{0:T(128)} %length_ref, bf16[4,128,1024]{2,1,0:T(8,128)(2,1)} %query_ref.1, f32[512,128]{1,0:T(8,128)} %bitcast.24, bf16[128,64,128]{2,1,0:T(8,128)(2,1)} %bitcast.22, bf16[128,64,128]{2,1,0:T(8,128)(2,1)} %bitcast.23), custom_call_target="tpu_custom_call" | custom-call | flops 268435456 | bytes 10485760 | tf_op jit(solution)/shard_map/pallas_call | solution.py:242
  54.5 0.0 collective-permute-done.1
  54.6 0.0 collective-permute-done.2
  54.6 0.0 collective-permute-done.3
  54.6 0.0 copy-done.7
  54.6 1.1 %add_add_fusion.base_ref = f32[512,128]{1,0:T(8,128)S(1)} fusion(f32[512,128]{1,0:T(8,128)} %collective-permute-done.2, f32[512,128]{1,0:T(8,128)} %collective-permute-done.3, f32[512,128]{1,0:T(8,128)S(1)} %copy-done.7, f32[512,128]{1,0:T(8,128)S(1)} %collective-permute-done.1), kind=kLoop, calls=%fused_computation.1 | loop fusion | flops 196608 | bytes 1310720 | tf_op jit(solution)/shard_map/add | solution.py:282
  55.7 0.0 all-to-all-done.1.step_ref
  55.7 0.0 copy-start.2
  55.7 0.0 copy-start.4
  55.7 0.0 copy-done.1
  55.7 0.0 copy-done.3
  55.7 0.0 copy-done.8
  55.7 0.8 %shard_map.114 = (f32[64,512]{1,0:T(8,128)S(1)}, f32[64,128]{1,0:T(8,128)S(1)}) custom-call(f32[64,2048]{1,0:T(8,128)S(1)} %copy-done.3, f32[64,128]{1,0:T(8,128)S(1)} %bitcast.20, f32[32,2,2176]{2,1,0:T(2,128)S(1)} %all-to-all-done.1.step_ref, bf16[512,2048]{1,0:T(8,128)(2,1)S(1)} %bitcast.16), custom_call_target="tpu_custom_call" | custom-call | flops 268435456 | bytes 1048576 | tf_op jit(solution)/shard_map/pallas_call | solution.py:286
  56.6 2.6 %collective-permute-start.4 = (f32[64,512]{1,0:T(8,128)S(1)}, f32[64,512]{1,0:T(8,128)S(1)}, u32[]{:S(2)}, u32[]{:S(2)}) collective-permute-start(f32[64,512]{1,0:T(8,128)S(1)} %get-tuple-element.41), channel_id=1, source_target_pairs={{0,1},{1,0},{2,3},{3,2},{4,5},{5,4},{6,7},{7,6},{8,9},{9,8},{10,11... | collective-permute-start | bytes 393224 | tf_op jit(solution)/shard_map/ppermute | solution.py:297
  59.2 1.0 %collective-permute-done.4 = f32[64,512]{1,0:T(8,128)S(1)} collective-permute-done((f32[64,512]{1,0:T(8,128)S(1)}, f32[64,512]{1,0:T(8,128)S(1)}, u32[]{:S(2)}, u32[]{:S(2)}) %collective-permute-start.4) | collective-permute-done | bytes 131104 | tf_op jit(solution)/shard_map/ppermute | solution.py:297
  60.2 1.9 %collective-permute-start.7 = (f32[64,512]{1,0:T(8,128)S(1)}, f32[64,512]{1,0:T(8,128)S(1)}, u32[]{:S(2)}, u32[]{:S(2)}) collective-permute-start(f32[64,512]{1,0:T(8,128)S(1)} %add.21.u0), channel_id=1, source_target_pairs={{0,6},{1,7},{2,0},{3,1},{4,2},{5,3},{6,4},{7,5},{8,14},{9,15},{10,... | collective-permute-start | bytes 393224 | tf_op jit(solution)/shard_map/ppermute | solution.py:298
  62.1 0.4 collective-permute-start.6
  62.5 0.7 collective-permute-start.5
  63.2 1.8 %collective-permute-done.7.u3 = f32[64,512]{1,0:T(8,128)S(1)} collective-permute-done((f32[64,512]{1,0:T(8,128)S(1)}, f32[64,512]{1,0:T(8,128)S(1)}, u32[]{:S(2)}, u32[]{:S(2)}) %collective-permute-start.7) | collective-permute-done | bytes 131104 | tf_op jit(solution)/shard_map/ppermute | solution.py:298
  65.0 3.1 %collective-permute-done.6.u2 = f32[64,512]{1,0:T(8,128)S(1)} collective-permute-done((f32[64,512]{1,0:T(8,128)S(1)}, f32[64,512]{1,0:T(8,128)S(1)}, u32[]{:S(2)}, u32[]{:S(2)}) %collective-permute-start.6) | collective-permute-done | bytes 131104 | tf_op jit(solution)/shard_map/ppermute | solution.py:298
  68.0 3.8 %collective-permute-done.5.u1 = f32[64,512]{1,0:T(8,128)S(1)} collective-permute-done((f32[64,512]{1,0:T(8,128)S(1)}, f32[64,512]{1,0:T(8,128)S(1)}, u32[]{:S(2)}, u32[]{:S(2)}) %collective-permute-start.5) | collective-permute-done | bytes 131104 | tf_op jit(solution)/shard_map/ppermute | solution.py:298
  71.8 0.0 copy-done.2
  71.8 0.0 copy-done.4
  71.8 3.3 %shard_map.115 = bf16[4,128,1024]{2,1,0:T(8,128)(2,1)} custom-call(f32[512,128]{1,0:T(8,128)S(1)} %add_add_fusion.base_ref, f32[64,512]{1,0:T(8,128)S(1)} %add.21.u0, f32[64,512]{1,0:T(8,128)S(1)} %collective-permute-done.5.u1, f32[64,512]{1,0:T(8,128)S(1)} %collective-permute-done.6.u2, f32[64,512]{1,0:T(8,128)S(1)} %collective-permute-done.7.u3, ...), custom_call_target="tpu_custom_call" | custom-call | tf_op jit(solution)/shard_map/pallas_call | solution.py:303
  (8 shorter events, 0.0 us)
Async XLA Ops:
  0.0 0.9 %copy-start.5 = (bf16[1,64,2048]{2,1,0:T(8,128)(2,1)S(1)}, bf16[1,64,2048]{2,1,0:T(8,128)(2,1)}, u32[]{:S(2)}) copy-start(bf16[1,64,2048]{2,1,0:T(8,128)(2,1)} %param.19) | copy-start | bytes 786436
  1.0 0.7 copy-start.9
  2.6 28.7 %all-to-all-start = ((f32[32,2,2176]{2,1,0:T(2,128)}), f32[32,2,2176]{2,1,0:T(2,128)S(1)}, u32[]{:S(2)}, u32[]{:S(2)}) async-start(f32[32,2,2176]{2,1,0:T(2,128)} %shard_map.109), calls=%async_computation | async-start | bytes 1114112 | tf_op jit(solution)/shard_map/all_to_all | solution.py:192
  14.5 1.6 %copy-start = (bf16[4,128,2048]{2,1,0:T(8,128)(2,1)S(1)}, bf16[4,128,2048]{2,1,0:T(8,128)(2,1)}, u32[]{:S(2)}) copy-start(bf16[4,128,2048]{2,1,0:T(8,128)(2,1)} %param.11) | copy-start | bytes 6291460
  16.1 2.2 %copy-start.10 = (bf16[2048,1024]{1,0:T(8,128)(2,1)S(1)}, bf16[2048,1024]{1,0:T(8,128)(2,1)}, u32[]{:S(2)}) copy-start(bf16[2048,1024]{1,0:T(8,128)(2,1)} %weight_ref.1) | copy-start | bytes 12582916
  22.4 3.3 %collective-permute-start = (f32[4,512,128]{2,1,0:T(8,128)S(1)}, f32[4,512,128]{2,1,0:T(8,128)S(1)}, u32[]{:S(2)}, u32[]{:S(2)}) collective-permute-start(f32[4,512,128]{2,1,0:T(8,128)S(1)} %get-tuple-element.26), channel_id=1, source_target_pairs={{0,1},{1,0},{2,3},{3,2},{4,5},{5,4},{6,7},{7,6},{8,9},{9,8},{10,11... | collective-permute-start | bytes 3145736 | tf_op jit(solution)/shard_map/ppermute | solution.py:227
  25.7 17.3 %copy-start.11 = (bf16[4,128,128]{2,1,0:T(8,128)(2,1)S(1)}, bf16[4,128,128]{2,1,0:T(8,128)(2,1)}, u32[]{:S(2)}) copy-start(bf16[4,128,128]{2,1,0:T(8,128)(2,1)} %param.13) | copy-start | bytes 393220
  26.6 0.7 copy-start.6
  32.4 23.3 %all-to-all-start.1 = ((f32[32,2,2176]{2,1,0:T(2,128)}), f32[32,2,2176]{2,1,0:T(2,128)S(1)}, u32[]{:S(2)}, u32[]{:S(2)}) async-start(f32[32,2,2176]{2,1,0:T(2,128)} %shard_map.110), calls=%async_computation.1 | async-start | bytes 1114112 | tf_op jit(solution)/shard_map/all_to_all | solution.py:229
  37.9 16.6 %collective-permute-start.1 = (f32[512,128]{1,0:T(8,128)}, f32[512,128]{1,0:T(8,128)S(1)}, u32[]{:S(2)}, u32[]{:S(2)}) collective-permute-start(f32[512,128]{1,0:T(8,128)} %get-tuple-element.36), channel_id=1, source_target_pairs={{0,2},{1,3},{2,4},{3,5},{4,6},{5,7},{6,0},{7,1},{8,10},{9,11},{10,... | collective-permute-start | bytes 786440 | tf_op jit(solution)/shard_map/ppermute | solution.py:231
  39.3 15.3 %collective-permute-start.2 = (f32[512,128]{1,0:T(8,128)}, f32[512,128]{1,0:T(8,128)}, u32[]{:S(2)}, u32[]{:S(2)}) collective-permute-start(f32[512,128]{1,0:T(8,128)} %get-tuple-element.37), channel_id=1, source_target_pairs={{0,4},{1,5},{2,6},{3,7},{4,0},{5,1},{6,2},{7,3},{8,12},{9,13},{10,... | collective-permute-start | bytes 786440 | tf_op jit(solution)/shard_map/ppermute | solution.py:231
  41.9 12.6 %collective-permute-start.3 = (f32[512,128]{1,0:T(8,128)S(1)}, f32[512,128]{1,0:T(8,128)}, u32[]{:S(2)}, u32[]{:S(2)}) collective-permute-start(f32[512,128]{1,0:T(8,128)S(1)} %get-tuple-element.38), channel_id=1, source_target_pairs={{0,6},{1,7},{2,0},{3,1},{4,2},{5,3},{6,4},{7,5},{8,14},{9,15},{10,... | collective-permute-start | bytes 786440 | tf_op jit(solution)/shard_map/ppermute | solution.py:231
  43.9 10.7 %copy-start.7 = (f32[512,128]{1,0:T(8,128)S(1)}, f32[512,128]{1,0:T(8,128)}, u32[]{:S(2)}) copy-start(f32[512,128]{1,0:T(8,128)} %copy-done.6) | copy-start | bytes 786436
  43.9 11.8 %copy-start.1 = (bf16[4,128,2048]{2,1,0:T(8,128)(2,1)S(1)}, bf16[4,128,2048]{2,1,0:T(8,128)(2,1)}, u32[]{:S(2)}) copy-start(bf16[4,128,2048]{2,1,0:T(8,128)(2,1)} %param.11) | copy-start | bytes 6291460
  43.9 11.8 %copy-start.3 = (f32[64,2048]{1,0:T(8,128)S(1)}, f32[64,2048]{1,0:T(8,128)}, u32[]{:S(2)}) copy-start(f32[64,2048]{1,0:T(8,128)} %a_ref.1) | copy-start | bytes 1572868
  43.9 11.8 %copy-start.8 = (f32[128,64]{0,1:T(8,128)S(1)}, f32[128,64]{0,1:T(8,128)}, u32[]{:S(2)}) copy-start(f32[128,64]{0,1:T(8,128)} %param.20) | copy-start | bytes 98308
  55.7 16.2 %copy-start.2 = (f32[4096,128]{1,0:T(8,128)S(1)}, f32[4096,128]{1,0:T(8,128)}, u32[]{:S(2)}) copy-start(f32[4096,128]{1,0:T(8,128)} %get-tuple-element.44) | copy-start | bytes 6291460
  55.7 16.2 %copy-start.4 = (f32[1024,128]{1,0:T(8,128)S(1)}, f32[1024,128]{1,0:T(8,128)}, u32[]{:S(2)}) copy-start(f32[1024,128]{1,0:T(8,128)} %get-tuple-element.43) | copy-start | bytes 1572868
  56.6 3.6 %collective-permute-start.4 = (f32[64,512]{1,0:T(8,128)S(1)}, f32[64,512]{1,0:T(8,128)S(1)}, u32[]{:S(2)}, u32[]{:S(2)}) collective-permute-start(f32[64,512]{1,0:T(8,128)S(1)} %get-tuple-element.41), channel_id=1, source_target_pairs={{0,1},{1,0},{2,3},{3,2},{4,5},{5,4},{6,7},{7,6},{8,9},{9,8},{10,11... | collective-permute-start | bytes 393224 | tf_op jit(solution)/shard_map/ppermute | solution.py:297
  60.2 4.8 %collective-permute-start.7 = (f32[64,512]{1,0:T(8,128)S(1)}, f32[64,512]{1,0:T(8,128)S(1)}, u32[]{:S(2)}, u32[]{:S(2)}) collective-permute-start(f32[64,512]{1,0:T(8,128)S(1)} %add.21.u0), channel_id=1, source_target_pairs={{0,6},{1,7},{2,0},{3,1},{4,2},{5,3},{6,4},{7,5},{8,14},{9,15},{10,... | collective-permute-start | bytes 393224 | tf_op jit(solution)/shard_map/ppermute | solution.py:298
  62.1 5.9 %collective-permute-start.6 = (f32[64,512]{1,0:T(8,128)S(1)}, f32[64,512]{1,0:T(8,128)S(1)}, u32[]{:S(2)}, u32[]{:S(2)}) collective-permute-start(f32[64,512]{1,0:T(8,128)S(1)} %add.21.u0), channel_id=1, source_target_pairs={{0,4},{1,5},{2,6},{3,7},{4,0},{5,1},{6,2},{7,3},{8,12},{9,13},{10,... | collective-permute-start | bytes 393224 | tf_op jit(solution)/shard_map/ppermute | solution.py:298
  62.5 9.4 %collective-permute-start.5 = (f32[64,512]{1,0:T(8,128)S(1)}, f32[64,512]{1,0:T(8,128)S(1)}, u32[]{:S(2)}, u32[]{:S(2)}) collective-permute-start(f32[64,512]{1,0:T(8,128)S(1)} %add.21.u0), channel_id=1, source_target_pairs={{0,2},{1,3},{2,4},{3,5},{4,6},{5,7},{6,0},{7,1},{8,10},{9,11},{10,... | collective-permute-start | bytes 393224 | tf_op jit(solution)/shard_map/ppermute | solution.py:298

commit v4 on v3

--- a/solution.py
+++ b/solution.py
@@ -60,11 +60,12 @@
         out_ref[...] = keep_ref[k] + received_ref[k]
 
 
-def cache_kernel(length_ref, query_ref, fresh_ref, key_ref, value_ref, part_ref, weight_ref, rows_ref, *scratch):
-    pair_ref, old_ref, new_ref, old_weight_ref, new_weight_ref = scratch
-    block = pl.program_id(0)
+def cache_kernel(
+    offset, length_ref, query_ref, fresh_ref, key_ref, value_ref, part_ref, weight_ref, *scratch
+):
+    rows_ref, pair_ref, old_ref, new_ref, old_weight_ref = scratch
     steps, rows, width = query_ref.shape
-    first = block * rows
+    first = (pl.program_id(0) + offset) * rows
     ctx, dim = key_ref.shape[1:]
     heads = width // dim
     n_queries = steps * heads
@@ -73,11 +74,6 @@
         for g in range(heads):
             at = (t * heads + g) * rows
             rows_ref[at : at + rows] = query_ref[t, :, g * dim : (g + 1) * dim].astype(jnp.float32)
-
-    @pl.when(block == 0)
-    def _():
-        weight_ref[...] = jnp.zeros_like(weight_ref)
-
     pairs = rows // 2
     lanes = 2 * ctx
     for r in range(rows):
@@ -87,7 +83,7 @@
     mm = functools.partial(
         lax.dot_general, dimension_numbers=by_lane, preferred_element_type=jnp.float32
     )
-    fresh_keys = fresh_ref[...].astype(jnp.bfloat16)
+    fresh_keys = fresh_ref[...].reshape(steps * rows, dim)
     both = 2 * n_queries
     for p in range(pairs):
         at = slice(p * both, (p + 1) * both)
@@ -96,40 +92,40 @@
         new_ref[at] = mm(pair_ref[at], fresh_keys)
 
     lane = lax.broadcasted_iota(jnp.int32, (n_queries, lanes), 1)
-    step_of = lax.broadcasted_iota(jnp.int32, (n_queries, lanes), 0) >> 3
+    step_of = lax.broadcasted_iota(jnp.int32, (n_queries, lanes), 0) // heads
+    row_of, reached = lane % rows, lane // rows <= step_of
     for r in range(rows):
         half = r % 2
         at = slice(r * n_queries, (r + 1) * n_queries)
         live = (lane >= half * ctx) & (lane < half * ctx + length_ref[first + r])
-        causal = (lane >= steps * r) & (lane <= steps * r + step_of)
+        causal = (row_of == r) & reached
         old = jnp.where(live, old_ref[at] * scale, -jnp.inf)
         new = jnp.where(causal, new_ref[at] * scale, -jnp.inf)
         top = jnp.max(jnp.maximum(old, new), axis=1, keepdims=True)
         old, new = jnp.exp(old - top), jnp.exp(new - top)
         inverse = 1.0 / jnp.sum(old + new, axis=1, keepdims=True)
         old_weight_ref[at] = (old * inverse).astype(jnp.bfloat16)
-        new_weight_ref[at] = (new * inverse).astype(jnp.bfloat16)
-
-    source = lax.broadcasted_iota(jnp.int32, (lanes, lanes), 0)
-    target = lax.broadcasted_iota(jnp.int32, (lanes, lanes), 1)
-    move = (target - steps * block == source % steps).astype(jnp.bfloat16)
+        new_ref[at] = new * inverse
+
     for p in range(pairs):
         at = slice(p * both, (p + 1) * both)
         values = value_ref[2 * p : 2 * p + 2].reshape(lanes, dim)
         old_ref[at] = jnp.dot(old_weight_ref[at], values, preferred_element_type=jnp.float32)
-        new_ref[at] = jnp.dot(new_weight_ref[at], move, preferred_element_type=jnp.float32)
     for q in range(n_queries):
         at = slice(q * rows, (q + 1) * rows)
         query = pl.ds(q, rows, stride=n_queries)
         part_ref[at] = old_ref[query, :]
-        weight_ref[at] = weight_ref[at] + new_ref[query, :]
-
-
-def finish_kernel(base_ref, u0, u1, u2, u3, b_ref, w_ref, cache_ref, out_ref, value_ref):
+        weight_ref[at] = new_ref[query, :].astype(jnp.bfloat16)
+
+
+def finish_kernel(v0, v1, v2, v3, u0, u1, u2, u3, b_ref, *refs):
+    *halves, out_ref, value_ref = refs
     t = pl.program_id(0)
-    steps, rows, dim = value_ref.shape
-    blocks, queries, block_rows = cache_ref.shape[:3]
-    heads = queries // steps
+    blocks, lanes, dim = value_ref.shape
+    steps = pl.num_programs(0)
+    rows = out_ref.shape[1]
+    block_rows = rows // blocks
+    heads = out_ref.shape[2] // dim
 
     @pl.when(t == 0)
     def _():
@@ -141,24 +137,26 @@
             lax.dot_general, dimension_numbers=dims, preferred_element_type=jnp.float32
         )
         delta = mm(u_high, b_high) + (mm(u_low, b_high) + mm(u_high, b_low))
-        values = base_ref[...] + ADAPTER_SCALE * delta
-        values = values.astype(jnp.bfloat16).astype(jnp.float32)
-        for s in range(steps):
-            value_ref[s] = values[s * rows : (s + 1) * rows]
-
-    for step in range(steps):
-
-        @pl.when(t == step)
-        def _():
-            for g in range(heads):
-                for i in range(blocks):
-                    at = slice(i * block_rows, (i + 1) * block_rows)
-                    acc = cache_ref[i, step * heads + g]
-                    weight = w_ref[step * heads + g]
-                    for s in range(step + 1):
-                        lane = i * steps + s
-                        acc = acc + weight[:, lane : lane + 1] * value_ref[s, at]
-                    out_ref[0, at, g * dim : (g + 1) * dim] = acc.astype(out_ref.dtype)
+        values = (v0[...] + v1[...]) + (v2[...] + v3[...]) + ADAPTER_SCALE * delta
+        values = values.astype(jnp.bfloat16)
+        for i in range(blocks):
+            for s in range(lanes // block_rows):
+                at = s * rows + i * block_rows
+                value_ref[i, s * block_rows : (s + 1) * block_rows] = values[at : at + block_rows]
+
+    size = heads * block_rows
+    start = pl.multiple_of(t * size, size)
+    half = blocks // 2
+    for i in range(blocks):
+        part_ref, weight_ref = halves[2 * (i // half) : 2 * (i // half) + 2]
+        fresh = jnp.dot(
+            weight_ref[i % half, pl.ds(start, size), :], value_ref[i], preferred_element_type=jnp.float32
+        )
+        context = part_ref[i % half, pl.ds(start, size), :] + fresh
+        for g in range(heads):
+            out_ref[0, i * block_rows : (i + 1) * block_rows, g * dim : (g + 1) * dim] = context[
+                g * block_rows : (g + 1) * block_rows
+            ].astype(out_ref.dtype)
 
 
 def shards(
@@ -186,7 +184,11 @@
     small_vmem = pltpu.CompilerParams(vmem_limit_bytes=16 * 1024 * 1024)
 
     slices = jax.ShapeDtypeStruct((n_dp, rank // n_dp, width_dev + head_dim), jnp.float32)
-    terms = pl.pallas_call(terms_kernel, out_shape=slices, compiler_params=small_vmem)(
+    terms = pl.pallas_call(
+        terms_kernel,
+        out_shape=slices,
+        compiler_params=pltpu.CompilerParams(vmem_limit_bytes=60 * 1024 * 1024),
+    )(
         learner_down_gradient[0], learner_up_gradient[0].T
     )
     mine = lax.all_to_all(terms, "dp", 0, 0, tiled=True)
@@ -232,57 +234,48 @@
     ]
 
     blocks = 4
-    f32, bf16 = jnp.float32, jnp.bfloat16
+    half = blocks // 2
     block_rows = rows_dev // blocks
     n_queries = step_count * group_size
-    by_row = jax.ShapeDtypeStruct((rows_dev * n_queries, head_dim), jnp.float32)
-    by_row_spec = pl.BlockSpec((block_rows * n_queries, head_dim), lambda i, _: (i, 0))
-    cache_spec = pl.BlockSpec((block_rows, ctx_len, head_dim), lambda i, _: (i, 0, 0))
-    keys_new = rotated_token_keys.astype(jnp.float32).transpose(1, 0, 2)
-    cache_part, fresh_weights = pl.pallas_call(
-        cache_kernel,
-        grid_spec=pltpu.PrefetchScalarGridSpec(
-            num_scalar_prefetch=1,
-            grid=(blocks,),
-            in_specs=[
-                pl.BlockSpec(
-                    (step_count, block_rows, group_size * head_dim), lambda i, _: (0, i, 0)
-                ),
-                pl.BlockSpec((block_rows * step_count, head_dim), lambda i, _: (i, 0)),
-                cache_spec,
-                cache_spec,
-            ],
-            out_specs=[
-                by_row_spec,
-                pl.BlockSpec((block_rows * n_queries, head_dim), lambda i, _: (0, 0)),
-            ],
-            scratch_shapes=[
-                pltpu.VMEM((block_rows * n_queries, head_dim), kind)
-                for kind in (f32, bf16, f32, f32, bf16, bf16)
-            ],
-        ),
-        out_shape=[
-            by_row,
-            jax.ShapeDtypeStruct((block_rows * n_queries, head_dim), jnp.float32),
-        ],
-        compiler_params=pltpu.CompilerParams(vmem_limit_bytes=60 * 1024 * 1024),
-        cost_estimate=pl.CostEstimate(
-            flops=2 * 2 * 2 * rows_dev * n_queries * ctx_len * head_dim,
-            bytes_accessed=10 * 1024 * 1024,
-            transcendentals=rows_dev * n_queries * ctx_len,
-        ),
-    )(
-        row_cache_length,
-        queries,
-        keys_new.reshape(rows_dev * step_count, head_dim),
-        stored_key_cache[:, 0],
-        stored_value_cache[:, 0],
-    )
-
-    base = (base_parts[0] + base_parts[1]) + (base_parts[2] + base_parts[3])
-    steps_ab, cache_part, fresh_weights, base = lax.optimization_barrier(
-        (steps_ab, cache_part, fresh_weights, base)
-    )
+    size = block_rows * n_queries
+
+    def attend(offset, lengths, vmem_mib):
+        by_row = lambda kind: jax.ShapeDtypeStruct((half * size, head_dim), kind)
+        by_row_spec = pl.BlockSpec((size, head_dim), lambda i, _: (i, 0))
+        cache_spec = pl.BlockSpec((block_rows, ctx_len, head_dim), lambda i, _: (i + offset, 0, 0))
+        token_spec = lambda width: pl.BlockSpec(
+            (step_count, block_rows, width), lambda i, _: (0, i + offset, 0)
+        )
+        f32, bf16 = jnp.float32, jnp.bfloat16
+        part, weights = pl.pallas_call(
+            functools.partial(cache_kernel, offset),
+            grid_spec=pltpu.PrefetchScalarGridSpec(
+                num_scalar_prefetch=1,
+                grid=(half,),
+                in_specs=[
+                    token_spec(group_size * head_dim),
+                    token_spec(head_dim),
+                    cache_spec,
+                    cache_spec,
+                ],
+                out_specs=[by_row_spec, by_row_spec],
+                scratch_shapes=[
+                    pltpu.VMEM((size, head_dim), kind) for kind in (f32, bf16, f32, f32, bf16)
+                ],
+            ),
+            out_shape=[by_row(f32), by_row(bf16)],
+            compiler_params=pltpu.CompilerParams(vmem_limit_bytes=vmem_mib * 1024 * 1024),
+            cost_estimate=pl.CostEstimate(
+                flops=2 * 2 * half * size * 2 * ctx_len * head_dim,
+                bytes_accessed=5 * 1024 * 1024,
+                transcendentals=2 * half * size * head_dim,
+            ),
+        )(lengths, queries, rotated_token_keys, stored_key_cache[:, 0], stored_value_cache[:, 0])
+        return part.reshape(half, size, head_dim), weights.reshape(half, size, head_dim)
+
+    first_half = attend(0, row_cache_length, 60)
+    steps_ab, first_half, base_parts = lax.optimization_barrier((steps_ab, first_half, base_parts))
+
     inner, new_b = pl.pallas_call(
         inner_kernel,
         out_shape=[
@@ -295,18 +288,18 @@
         ),
     )(adapter_down_factor, adapter_up_factor.T, steps_ab, flat_hidden)
     inner = inner + lax.ppermute(inner, "mp", core_pairs)
+    inner, row_cache_length = lax.optimization_barrier((inner, row_cache_length))
+    second_half = attend(half, row_cache_length, 52)
     inner_parts = [inner] + [lax.ppermute(inner, "mp", along_y(k)) for k in range(1, n_chips)]
 
-    by_query = (blocks, n_queries, block_rows, head_dim)
-
-    operands = [base, *inner_parts, new_b, fresh_weights.reshape(by_query[1:]), cache_part.reshape(by_query)]
+    operands = [*base_parts, *inner_parts, new_b, *first_half, *second_half]
     return pl.pallas_call(
         finish_kernel,
         grid=(step_count,),
         out_shape=jax.ShapeDtypeStruct(queries.shape, jnp.bfloat16),
         in_specs=[pl.BlockSpec(memory_space=pltpu.VMEM)] * len(operands),
         out_specs=pl.BlockSpec((1, rows_dev, group_size * head_dim), lambda t: (t, 0, 0)),
-        scratch_shapes=[pltpu.VMEM((step_count, rows_dev, head_dim), jnp.float32)],
+        scratch_shapes=[pltpu.VMEM((blocks, step_count * block_rows, head_dim), jnp.bfloat16)],
         compiler_params=small_vmem,
     )(*operands)
 

time: 75.6 us -> 75.1 us (level)
  waiting for transfers between devices: 15.9 us -> 13.8 us
  Pallas kernels: 21.7 us -> 23.7 us
  starting transfers between devices: 29.1 us -> 31 us
  local copies, waits for them, and re-layouts: 7.04 us -> 5.93 us
  other arithmetic: 1.2 us -> 0.09 us
    ppermute x3, waiting for transfers between devices: 8.69 us -> 3.48 us  [shards(): lax.ppermute(inner, 'mp', along_y(k))]
    ppermute x3, waiting for transfers between devices: 0.01 us -> 2.54 us  [shards(): lax.ppermute(paired[k], 'mp', along_y(k))]
    pallas_call x2 -> x3, Pallas kernels: 11.5 us -> 13.3 us  [the longest x2 11.4 us: attend(): pl.pallas_call(functools.partial(cache_kernel, offset), grid_spec=pltpu.P...]
    add x1 -> x0, other arithmetic: 1.08 us -> none  [shards(): base = base_parts[0] + base_parts[1] + (base_parts[2] + base_parts[3])]
    ppermute x1, starting transfers between devices: 2.59 us -> 3.56 us  [shards(): inner = inner + lax.ppermute(inner, 'mp', core_pairs)]
    reshape x1 -> x0, local copies, waits for them, and re-layouts: 0.88 us -> none  [shards(): keys_new.reshape(rows_dev * step_count, head_dim)]
    ppermute x3, starting transfers between devices: 2.98 us -> 3.85 us  [shards(): lax.ppermute(inner, 'mp', along_y(k))]
    unnamed x24 -> x30, local copies, waits for them, and re-layouts: 6.16 us -> 5.93 us
  transfers between devices with their start and end apart: 10 -> 10, of which waited for: 6 -> 6; matrix products, arithmetic and copies ran while one was open for 3% -> 0% of each run, Pallas kernels for 21% -> 22%
where the time goes in v4:
time: 75.1 us; the launch traced here: 74.6 us
  starting transfers between devices  31 us (41%)
  Pallas kernels  23.7 us (32%)
  waiting for transfers between devices  13.8 us (18%)
  local copies, waits for them, and re-layouts  5.93 us (8%)
    all_to_all x1, starting transfers between devices, shards(): mine = lax.all_to_all(terms, 'dp', 0, 0, tiled=True)  11.9 us
    pallas_call x2, Pallas kernels, attend(): pl.pallas_call(functools.partial(cache_kernel, offset), grid_spec=pltpu.P...  11.4 us
    unnamed x30, local copies, waits for them, and re-layouts  5.93 us
    all_to_all x1, starting transfers between devices, shards(): steps_ab = lax.all_to_all(mine, 'dp', 0, 0, tiled=True)  5.62 us
    ppermute x3, starting transfers between devices, shards(): lax.ppermute(paired[k], 'mp', along_y(k))  5.06 us
    pallas_call x1, Pallas kernels, shards(): pl.pallas_call(project_kernel, grid_spec=pltpu.PrefetchScalarGridSpec(num...  4.07 us
    all_to_all x1, waiting for transfers between devices, shards(): mine = lax.all_to_all(terms, 'dp', 0, 0, tiled=True)  3.87 us
    ppermute x3, starting transfers between devices, shards(): lax.ppermute(inner, 'mp', along_y(k))  3.85 us
  transfers between devices with their start and end apart: 10, of which 6 were waited for; matrix products, arithmetic and copies ran while one was open for 0% of the time, Pallas kernels for 22%

profile of v4, /device:TPU:1, one launch (start us, length us, event | category | flops | bytes accessed | tf_op | source)
XLA Modules:
  0.0 74.6 jit_solution(4844061210282974532)
XLA Ops:
  0.0 1.9 %shard_map.109 = f32[32,2,2176]{2,1,0:T(2,128)} custom-call(bf16[64,2048]{1,0:T(8,128)(2,1)} %bitcast.25, bf16[64,128]{1,0:T(8,128)(2,1)} %bitcast.26), custom_call_target="tpu_custom_call" | custom-call | tf_op jit(solution)/shard_map/pallas_call | solution.py:187
  1.9 11.9 %all-to-all-start = ((f32[32,2,2176]{2,1,0:T(2,128)}), f32[32,2,2176]{2,1,0:T(2,128)S(1)}, u32[]{:S(2)}, u32[]{:S(2)}) async-start(f32[32,2,2176]{2,1,0:T(2,128)} %shard_map.109), calls=%async_computation | async-start | bytes 1114112 | tf_op jit(solution)/shard_map/all_to_all | solution.py:194
  13.7 0.1 pad_add_fusion.place_ref
  13.8 1.6 %copy-done = bf16[4,128,2048]{2,1,0:T(8,128)(2,1)S(1)} copy-done((bf16[4,128,2048]{2,1,0:T(8,128)(2,1)S(1)}, bf16[4,128,2048]{2,1,0:T(8,128)(2,1)}, u32[]{:S(2)}) %copy-start) | copy-done | bytes 2097176
  15.4 2.2 %copy-done.14 = bf16[2048,1024]{1,0:T(8,128)(2,1)S(1)} copy-done((bf16[2048,1024]{1,0:T(8,128)(2,1)S(1)}, bf16[2048,1024]{1,0:T(8,128)(2,1)}, u32[]{:S(2)}) %copy-start.14) | copy-done | bytes 4194328
  17.6 4.1 %shard_map.111 = (f32[4,512,128]{2,1,0:T(8,128)S(1)}, f32[4,512,128]{2,1,0:T(8,128)S(1)}) custom-call(s32[2]{0:T(128)S(1)} %pad_add_fusion.place_ref, bf16[512,2048]{1,0:T(8,128)(2,1)S(1)} %bitcast.14, bf16[2048,1024]{1,0:T(8,128)(2,1)S(1)} %copy-done.14), custom_call_target="tpu_custom_call" | custom-call | flops 2147483648 | bytes 10485760 | tf_op jit(solution)/shard_map/pallas_call | solution.py:202
  21.7 1.0 %collective-permute-start = (f32[4,512,128]{2,1,0:T(8,128)S(1)}, f32[4,512,128]{2,1,0:T(8,128)S(1)}, u32[]{:S(2)}, u32[]{:S(2)}) collective-permute-start(f32[4,512,128]{2,1,0:T(8,128)S(1)} %get-tuple-element.33), channel_id=1, source_target_pairs={{0,1},{1,0},{2,3},{3,2},{4,5},{5,4},{6,7},{7,6},{8,9},{9,8},{10,11... | collective-permute-start | bytes 3145736 | tf_op jit(solution)/shard_map/ppermute | solution.py:229
  22.7 2.3 %collective-permute-done.received_ref = f32[4,512,128]{2,1,0:T(8,128)S(1)} collective-permute-done((f32[4,512,128]{2,1,0:T(8,128)S(1)}, f32[4,512,128]{2,1,0:T(8,128)S(1)}, u32[]{:S(2)}, u32[]{:S(2)}) %collective-permute-start) | collective-permute-done | bytes 1048608 | tf_op jit(solution)/shard_map/ppermute | solution.py:229
  25.0 1.0 %shard_map.112 = (f32[512,128]{1,0:T(8,128)S(1)}, f32[512,128]{1,0:T(8,128)}, f32[512,128]{1,0:T(8,128)}, f32[512,128]{1,0:T(8,128)}) custom-call(f32[4,512,128]{2,1,0:T(8,128)S(1)} %get-tuple-element.32.keep_ref, f32[4,512,128]{2,1,0:T(8,128)S(1)} %collective-permute-done.received_ref), custom_call_target="tpu_custom_call" | custom-call | tf_op jit(solution)/shard_map/pallas_call | solution.py:225
  26.0 0.7 copy-done.6
  26.7 3.9 %all-to-all-done.in_ref = f32[32,2,2176]{2,1,0:T(2,128)S(1)} async-done(((f32[32,2,2176]{2,1,0:T(2,128)}), f32[32,2,2176]{2,1,0:T(2,128)S(1)}, u32[]{:S(2)}, u32[]{:S(2)}) %all-to-all-start) | async-done | bytes 557088 | tf_op jit(solution)/shard_map/all_to_all | solution.py:194
  30.6 1.1 %shard_map.110 = f32[32,2,2176]{2,1,0:T(2,128)} custom-call(f32[32,2,2176]{2,1,0:T(2,128)S(1)} %all-to-all-done.in_ref), custom_call_target="tpu_custom_call" | custom-call | tf_op jit(solution)/shard_map/pallas_call | solution.py:195
  31.7 5.6 %all-to-all-start.1 = ((f32[32,2,2176]{2,1,0:T(2,128)}), f32[32,2,2176]{2,1,0:T(2,128)S(1)}, u32[]{:S(2)}, u32[]{:S(2)}) async-start(f32[32,2,2176]{2,1,0:T(2,128)} %shard_map.110), calls=%async_computation.1 | async-start | bytes 1114112 | tf_op jit(solution)/shard_map/all_to_all | solution.py:231
  37.3 1.4 %collective-permute-start.1 = (f32[512,128]{1,0:T(8,128)}, f32[512,128]{1,0:T(8,128)S(1)}, u32[]{:S(2)}, u32[]{:S(2)}) collective-permute-start(f32[512,128]{1,0:T(8,128)} %get-tuple-element.43), channel_id=1, source_target_pairs={{0,2},{1,3},{2,4},{3,5},{4,6},{5,7},{6,0},{7,1},{8,10},{9,11},{10,... | collective-permute-start | bytes 786440 | tf_op jit(solution)/shard_map/ppermute | solution.py:233
  38.7 2.6 %collective-permute-start.2 = (f32[512,128]{1,0:T(8,128)}, f32[512,128]{1,0:T(8,128)S(1)}, u32[]{:S(2)}, u32[]{:S(2)}) collective-permute-start(f32[512,128]{1,0:T(8,128)} %get-tuple-element.44), channel_id=1, source_target_pairs={{0,4},{1,5},{2,6},{3,7},{4,0},{5,1},{6,2},{7,3},{8,12},{9,13},{10,... | collective-permute-start | bytes 786440 | tf_op jit(solution)/shard_map/ppermute | solution.py:233
  41.3 1.1 %collective-permute-start.3 = (f32[512,128]{1,0:T(8,128)}, f32[512,128]{1,0:T(8,128)}, u32[]{:S(2)}, u32[]{:S(2)}) collective-permute-start(f32[512,128]{1,0:T(8,128)} %get-tuple-element.45), channel_id=1, source_target_pairs={{0,6},{1,7},{2,0},{3,1},{4,2},{5,3},{6,4},{7,5},{8,14},{9,15},{10,... | collective-permute-start | bytes 786440 | tf_op jit(solution)/shard_map/ppermute | solution.py:233
  42.4 6.2 %shard_map.113 = (f32[2048,128]{1,0:T(8,128)}, bf16[2048,128]{1,0:T(8,128)(2,1)}) custom-call(s32[128]{0:T(128)} %length_ref.1, bf16[4,128,1024]{2,1,0:T(8,128)(2,1)} %query_ref.3, bf16[4,128,128]{2,1,0:T(8,128)(2,1)} %fresh_ref.3, bf16[128,64,128]{2,1,0:T(8,128)(2,1)} %bitcast.21, bf16[128,64,128]{2,1,0:T(8,128)(2,1)} %bitcast.23), custom_call_target="tpu_custom_call" | custom-call | flops 134217728 | bytes 5242880 | tf_op jit(solution)/shard_map/pallas_call | solution.py:250
  48.6 0.0 collective-permute-done.1.v1
  48.6 0.0 copy-start.8
  48.6 0.7 copy-done.8
  49.3 2.5 %collective-permute-done.2.v2 = f32[512,128]{1,0:T(8,128)S(1)} collective-permute-done((f32[512,128]{1,0:T(8,128)}, f32[512,128]{1,0:T(8,128)S(1)}, u32[]{:S(2)}, u32[]{:S(2)}) %collective-permute-start.2) | collective-permute-done | bytes 262176 | tf_op jit(solution)/shard_map/ppermute | solution.py:233
  51.9 0.7 copy-done.10
  52.6 0.0 collective-permute-done.3.v3
  52.6 0.6 all-to-all-done.1.step_ref
  53.2 0.0 copy-done.1
  53.2 0.0 copy-done.3
  53.2 0.0 copy-done.12
  53.2 0.8 %shard_map.114 = (f32[64,512]{1,0:T(8,128)S(1)}, f32[64,128]{1,0:T(8,128)S(1)}) custom-call(f32[64,2048]{1,0:T(8,128)S(1)} %copy-done.3, f32[64,128]{1,0:T(8,128)S(1)} %bitcast.20, f32[32,2,2176]{2,1,0:T(2,128)S(1)} %all-to-all-done.1.step_ref, bf16[512,2048]{1,0:T(8,128)(2,1)S(1)} %bitcast.15), custom_call_target="tpu_custom_call" | custom-call | flops 268435456 | bytes 1048576 | tf_op jit(solution)/shard_map/pallas_call | solution.py:279
  54.1 3.6 %collective-permute-start.4 = (f32[64,512]{1,0:T(8,128)S(1)}, f32[64,512]{1,0:T(8,128)S(1)}, u32[]{:S(2)}, u32[]{:S(2)}) collective-permute-start(f32[64,512]{1,0:T(8,128)S(1)} %get-tuple-element.51), channel_id=1, source_target_pairs={{0,1},{1,0},{2,3},{3,2},{4,5},{5,4},{6,7},{7,6},{8,9},{9,8},{10,11... | collective-permute-start | bytes 393224 | tf_op jit(solution)/shard_map/ppermute | solution.py:290
  57.6 1.0 %collective-permute-done.4 = f32[64,512]{1,0:T(8,128)S(1)} collective-permute-done((f32[64,512]{1,0:T(8,128)S(1)}, f32[64,512]{1,0:T(8,128)S(1)}, u32[]{:S(2)}, u32[]{:S(2)}) %collective-permute-start.4) | collective-permute-done | bytes 131104 | tf_op jit(solution)/shard_map/ppermute | solution.py:290
  58.6 0.0 copy-start.2
  58.6 0.0 copy-start.5
  58.6 0.0 copy-start.7
  58.6 0.0 copy-start.9
  58.7 0.0 copy-start.11
  58.7 2.8 %collective-permute-start.7 = (f32[64,512]{1,0:T(8,128)S(1)}, f32[64,512]{1,0:T(8,128)S(1)}, u32[]{:S(2)}, u32[]{:S(2)}) collective-permute-start(f32[64,512]{1,0:T(8,128)S(1)} %add.9.u0), channel_id=1, source_target_pairs={{0,6},{1,7},{2,0},{3,1},{4,2},{5,3},{6,4},{7,5},{8,14},{9,15},{10,... | collective-permute-start | bytes 393224 | tf_op jit(solution)/shard_map/ppermute | solution.py:293
  61.5 0.3 collective-permute-start.6
  61.8 0.7 collective-permute-start.5
  62.5 0.0 copy-done.4
  62.5 0.0 copy-done.13
  62.5 5.2 %shard_map.115 = (f32[2048,128]{1,0:T(8,128)S(1)}, bf16[2048,128]{1,0:T(8,128)(2,1)S(1)}) custom-call(s32[128]{0:T(128)S(1)} %copy-done.13, bf16[4,128,1024]{2,1,0:T(8,128)(2,1)} %query_ref.3, bf16[4,128,128]{2,1,0:T(8,128)(2,1)S(1)} %copy-done.4, bf16[128,64,128]{2,1,0:T(8,128)(2,1)} %bitcast.22, bf16[128,64,128]{2,1,0:T(8,128)(2,1)} %bitcast.24), custom_call_target="tpu_custom_call" | custom-call | flops 134217728 | bytes 5242880 | tf_op jit(solution)/shard_map/pallas_call | solution.py:250
  67.7 0.0 collective-permute-done.7.u3
  67.7 0.0 collective-permute-done.6.u2
  67.7 3.5 %collective-permute-done.5.u1 = f32[64,512]{1,0:T(8,128)S(1)} collective-permute-done((f32[64,512]{1,0:T(8,128)S(1)}, f32[64,512]{1,0:T(8,128)S(1)}, u32[]{:S(2)}, u32[]{:S(2)}) %collective-permute-start.5) | collective-permute-done | bytes 131104 | tf_op jit(solution)/shard_map/ppermute | solution.py:293
  71.2 0.0 copy-done.7
  71.2 0.0 copy-done.9
  71.2 0.0 copy-done.11
  71.2 3.4 %shard_map.116 = bf16[4,128,1024]{2,1,0:T(8,128)(2,1)} custom-call(f32[512,128]{1,0:T(8,128)S(1)} %copy-done.7, f32[512,128]{1,0:T(8,128)S(1)} %copy-done.9, f32[512,128]{1,0:T(8,128)S(1)} %copy-done.11, f32[512,128]{1,0:T(8,128)} %collective-permute-done.3.v3, f32[64,512]{1,0:T(8,128)S(1)} %add.9.u0, f32[64,512]{1,0:T(8,128)S(1)} %collective-permute-done.5.u1, ...), custom_call_target="tpu_custom_call" | custom-call | tf_op jit(solution)/shard_map/pallas_call | solution.py:296
  (12 shorter events, 0.0 us)
Async XLA Ops:
  1.9 28.7 %all-to-all-start = ((f32[32,2,2176]{2,1,0:T(2,128)}), f32[32,2,2176]{2,1,0:T(2,128)S(1)}, u32[]{:S(2)}, u32[]{:S(2)}) async-start(f32[32,2,2176]{2,1,0:T(2,128)} %shard_map.109), calls=%async_computation | async-start | bytes 1114112 | tf_op jit(solution)/shard_map/all_to_all | solution.py:194
  13.8 1.6 %copy-start = (bf16[4,128,2048]{2,1,0:T(8,128)(2,1)S(1)}, bf16[4,128,2048]{2,1,0:T(8,128)(2,1)}, u32[]{:S(2)}) copy-start(bf16[4,128,2048]{2,1,0:T(8,128)(2,1)} %param.11) | copy-start | bytes 6291460
  15.4 2.2 %copy-start.14 = (bf16[2048,1024]{1,0:T(8,128)(2,1)S(1)}, bf16[2048,1024]{1,0:T(8,128)(2,1)}, u32[]{:S(2)}) copy-start(bf16[2048,1024]{1,0:T(8,128)(2,1)} %weight_ref.1) | copy-start | bytes 12582916
  21.7 3.3 %collective-permute-start = (f32[4,512,128]{2,1,0:T(8,128)S(1)}, f32[4,512,128]{2,1,0:T(8,128)S(1)}, u32[]{:S(2)}, u32[]{:S(2)}) collective-permute-start(f32[4,512,128]{2,1,0:T(8,128)S(1)} %get-tuple-element.33), channel_id=1, source_target_pairs={{0,1},{1,0},{2,3},{3,2},{4,5},{5,4},{6,7},{7,6},{8,9},{9,8},{10,11... | collective-permute-start | bytes 3145736 | tf_op jit(solution)/shard_map/ppermute | solution.py:229
  26.0 0.7 copy-start.6
  31.7 21.5 %all-to-all-start.1 = ((f32[32,2,2176]{2,1,0:T(2,128)}), f32[32,2,2176]{2,1,0:T(2,128)S(1)}, u32[]{:S(2)}, u32[]{:S(2)}) async-start(f32[32,2,2176]{2,1,0:T(2,128)} %shard_map.110), calls=%async_computation.1 | async-start | bytes 1114112 | tf_op jit(solution)/shard_map/all_to_all | solution.py:231
  37.3 11.3 %collective-permute-start.1 = (f32[512,128]{1,0:T(8,128)}, f32[512,128]{1,0:T(8,128)S(1)}, u32[]{:S(2)}, u32[]{:S(2)}) collective-permute-start(f32[512,128]{1,0:T(8,128)} %get-tuple-element.43), channel_id=1, source_target_pairs={{0,2},{1,3},{2,4},{3,5},{4,6},{5,7},{6,0},{7,1},{8,10},{9,11},{10,... | collective-permute-start | bytes 786440 | tf_op jit(solution)/shard_map/ppermute | solution.py:233
  38.7 13.2 %collective-permute-start.2 = (f32[512,128]{1,0:T(8,128)}, f32[512,128]{1,0:T(8,128)S(1)}, u32[]{:S(2)}, u32[]{:S(2)}) collective-permute-start(f32[512,128]{1,0:T(8,128)} %get-tuple-element.44), channel_id=1, source_target_pairs={{0,4},{1,5},{2,6},{3,7},{4,0},{5,1},{6,2},{7,3},{8,12},{9,13},{10,... | collective-permute-start | bytes 786440 | tf_op jit(solution)/shard_map/ppermute | solution.py:233
  41.3 11.3 %collective-permute-start.3 = (f32[512,128]{1,0:T(8,128)}, f32[512,128]{1,0:T(8,128)}, u32[]{:S(2)}, u32[]{:S(2)}) collective-permute-start(f32[512,128]{1,0:T(8,128)} %get-tuple-element.45), channel_id=1, source_target_pairs={{0,6},{1,7},{2,0},{3,1},{4,2},{5,3},{6,4},{7,5},{8,14},{9,15},{10,... | collective-permute-start | bytes 786440 | tf_op jit(solution)/shard_map/ppermute | solution.py:233
  42.4 10.8 %copy-start.1 = (bf16[4,128,2048]{2,1,0:T(8,128)(2,1)S(1)}, bf16[4,128,2048]{2,1,0:T(8,128)(2,1)}, u32[]{:S(2)}) copy-start(bf16[4,128,2048]{2,1,0:T(8,128)(2,1)} %param.11) | copy-start | bytes 6291460
  42.4 10.8 %copy-start.3 = (f32[64,2048]{1,0:T(8,128)S(1)}, f32[64,2048]{1,0:T(8,128)}, u32[]{:S(2)}) copy-start(f32[64,2048]{1,0:T(8,128)} %a_ref.1) | copy-start | bytes 1572868
  42.4 10.8 %copy-start.12 = (f32[128,64]{0,1:T(8,128)S(1)}, f32[128,64]{0,1:T(8,128)}, u32[]{:S(2)}) copy-start(f32[128,64]{0,1:T(8,128)} %param.20) | copy-start | bytes 98308
  48.6 13.9 %copy-start.4 = (bf16[4,128,128]{2,1,0:T(8,128)(2,1)S(1)}, bf16[4,128,128]{2,1,0:T(8,128)(2,1)}, u32[]{:S(2)}) copy-start(bf16[4,128,128]{2,1,0:T(8,128)(2,1)} %fresh_ref.3) | copy-start | bytes 393220
  48.6 13.9 %copy-start.13 = (s32[128]{0:T(128)S(1)}, s32[128]{0:T(128)}, u32[]{:S(2)}) copy-start(s32[128]{0:T(128)} %length_ref.1) | copy-start | bytes 1540
  48.6 0.7 copy-start.8
  51.9 0.7 copy-start.10
  54.1 4.5 %collective-permute-start.4 = (f32[64,512]{1,0:T(8,128)S(1)}, f32[64,512]{1,0:T(8,128)S(1)}, u32[]{:S(2)}, u32[]{:S(2)}) collective-permute-start(f32[64,512]{1,0:T(8,128)S(1)} %get-tuple-element.51), channel_id=1, source_target_pairs={{0,1},{1,0},{2,3},{3,2},{4,5},{5,4},{6,7},{7,6},{8,9},{9,8},{10,11... | collective-permute-start | bytes 393224 | tf_op jit(solution)/shard_map/ppermute | solution.py:290
  58.6 12.6 %copy-start.2 = (f32[2048,128]{1,0:T(8,128)S(1)}, f32[2048,128]{1,0:T(8,128)}, u32[]{:S(2)}) copy-start(f32[2048,128]{1,0:T(8,128)} %get-tuple-element.40) | copy-start | bytes 3145732
  58.6 12.6 %copy-start.5 = (bf16[2048,128]{1,0:T(8,128)(2,1)S(1)}, bf16[2048,128]{1,0:T(8,128)(2,1)}, u32[]{:S(2)}) copy-start(bf16[2048,128]{1,0:T(8,128)(2,1)} %get-tuple-element.41) | copy-start | bytes 1572868
  58.6 12.6 %copy-start.7 = (f32[512,128]{1,0:T(8,128)S(1)}, f32[512,128]{1,0:T(8,128)}, u32[]{:S(2)}) copy-start(f32[512,128]{1,0:T(8,128)} %copy-done.6) | copy-start | bytes 786436
  58.6 12.6 %copy-start.9 = (f32[512,128]{1,0:T(8,128)S(1)}, f32[512,128]{1,0:T(8,128)}, u32[]{:S(2)}) copy-start(f32[512,128]{1,0:T(8,128)} %copy-done.8) | copy-start | bytes 786436
  58.7 12.6 %copy-start.11 = (f32[512,128]{1,0:T(8,128)S(1)}, f32[512,128]{1,0:T(8,128)}, u32[]{:S(2)}) copy-start(f32[512,128]{1,0:T(8,128)} %copy-done.10) | copy-start | bytes 786436
  58.7 9.0 %collective-permute-start.7 = (f32[64,512]{1,0:T(8,128)S(1)}, f32[64,512]{1,0:T(8,128)S(1)}, u32[]{:S(2)}, u32[]{:S(2)}) collective-permute-start(f32[64,512]{1,0:T(8,128)S(1)} %add.9.u0), channel_id=1, source_target_pairs={{0,6},{1,7},{2,0},{3,1},{4,2},{5,3},{6,4},{7,5},{8,14},{9,15},{10,... | collective-permute-start | bytes 393224 | tf_op jit(solution)/shard_map/ppermute | solution.py:293
  61.5 6.3 %collective-permute-start.6 = (f32[64,512]{1,0:T(8,128)S(1)}, f32[64,512]{1,0:T(8,128)S(1)}, u32[]{:S(2)}, u32[]{:S(2)}) collective-permute-start(f32[64,512]{1,0:T(8,128)S(1)} %add.9.u0), channel_id=1, source_target_pairs={{0,4},{1,5},{2,6},{3,7},{4,0},{5,1},{6,2},{7,3},{8,12},{9,13},{10,... | collective-permute-start | bytes 393224 | tf_op jit(solution)/shard_map/ppermute | solution.py:293
  61.8 9.4 %collective-permute-start.5 = (f32[64,512]{1,0:T(8,128)S(1)}, f32[64,512]{1,0:T(8,128)S(1)}, u32[]{:S(2)}, u32[]{:S(2)}) collective-permute-start(f32[64,512]{1,0:T(8,128)S(1)} %add.9.u0), channel_id=1, source_target_pairs={{0,2},{1,3},{2,4},{3,5},{4,6},{5,7},{6,0},{7,1},{8,10},{9,11},{10,... | collective-permute-start | bytes 393224 | tf_op jit(solution)/shard_map/ppermute | solution.py:293

commit v5 on v4

--- a/solution.py
+++ b/solution.py
@@ -227,7 +227,7 @@
         out_shape=[jax.ShapeDtypeStruct((tokens, head_dim), jnp.float32)] * n_chips,
         compiler_params=small_vmem,
     )(keep, lax.ppermute(send, "mp", core_pairs))
-    mine, row_cache_length, paired = lax.optimization_barrier((mine, row_cache_length, paired))
+    mine, row_cache_length, _ = lax.optimization_barrier((mine, row_cache_length, paired))
     steps_ab = lax.all_to_all(mine, "dp", 0, 0, tiled=True)
     base_parts = [paired[0]] + [
         lax.ppermute(paired[k], "mp", along_y(k)) for k in range(1, n_chips)
@@ -274,7 +274,7 @@
         return part.reshape(half, size, head_dim), weights.reshape(half, size, head_dim)
 
     first_half = attend(0, row_cache_length, 60)
-    steps_ab, first_half, base_parts = lax.optimization_barrier((steps_ab, first_half, base_parts))
+    steps_ab, first_half = lax.optimization_barrier((steps_ab, first_half))
 
     inner, new_b = pl.pallas_call(
         inner_kernel,
@@ -283,11 +283,10 @@
             jax.ShapeDtypeStruct((rank, head_dim), jnp.float32),
         ],
         compiler_params=small_vmem,
-        cost_estimate=pl.CostEstimate(
-            flops=4 * tokens * width_dev * rank, bytes_accessed=1024 * 1024, transcendentals=0
-        ),
+        cost_estimate=pl.CostEstimate(flops=0, bytes_accessed=0, transcendentals=0),
     )(adapter_down_factor, adapter_up_factor.T, steps_ab, flat_hidden)
     inner = inner + lax.ppermute(inner, "mp", core_pairs)
+    inner, base_parts = lax.optimization_barrier((inner, base_parts))
     inner, row_cache_length = lax.optimization_barrier((inner, row_cache_length))
     second_half = attend(half, row_cache_length, 52)
     inner_parts = [inner] + [lax.ppermute(inner, "mp", along_y(k)) for k in range(1, n_chips)]

time: 75.1 us -> 75.2 us (level)
  local copies, waits for them, and re-layouts: 5.93 us -> 4.51 us
  waiting for transfers between devices: 13.8 us -> 15.2 us
    all_to_all x1, waiting for transfers between devices: 0.61 us -> 4.52 us  [shards(): steps_ab = lax.all_to_all(mine, 'dp', 0, 0, tiled=True)]
    ppermute x3, waiting for transfers between devices: 2.54 us -> 0.01 us  [shards(): lax.ppermute(paired[k], 'mp', along_y(k))]
    unnamed x30 -> x22, local copies, waits for them, and re-layouts: 5.93 us -> 4.51 us
  transfers between devices with their start and end apart: 10 -> 10, of which waited for: 6 -> 5; matrix products, arithmetic and copies ran while one was open for 0% -> 0% of each run, Pallas kernels for 22% -> 23%
where the time goes in v5:
time: 75.2 us; the launch traced here: 74.8 us
  starting transfers between devices  31 us (41%)
  Pallas kernels  23.8 us (32%)
  waiting for transfers between devices  15.2 us (20%)
  local copies, waits for them, and re-layouts  4.51 us (6%)
    all_to_all x1, starting transfers between devices, shards(): mine = lax.all_to_all(terms, 'dp', 0, 0, tiled=True)  11.9 us
    pallas_call x2, Pallas kernels, attend(): pl.pallas_call(functools.partial(cache_kernel, offset), grid_spec=pltpu.P...  11.4 us
    all_to_all x1, starting transfers between devices, shards(): steps_ab = lax.all_to_all(mine, 'dp', 0, 0, tiled=True)  5.59 us
    ppermute x3, starting transfers between devices, shards(): lax.ppermute(paired[k], 'mp', along_y(k))  5.06 us
    all_to_all x1, waiting for transfers between devices, shards(): steps_ab = lax.all_to_all(mine, 'dp', 0, 0, tiled=True)  4.52 us
    unnamed x22, local copies, waits for them, and re-layouts  4.51 us
    pallas_call x1, Pallas kernels, shards(): pl.pallas_call(project_kernel, grid_spec=pltpu.PrefetchScalarGridSpec(num...  4.07 us
    all_to_all x1, waiting for transfers between devices, shards(): mine = lax.all_to_all(terms, 'dp', 0, 0, tiled=True)  3.91 us
  transfers between devices with their start and end apart: 10, of which 5 were waited for; matrix products, arithmetic and copies ran while one was open for 0% of the time, Pallas kernels for 23%

profile of v5, /device:TPU:1, one launch (start us, length us, event | category | flops | bytes accessed | tf_op | source)
XLA Modules:
  0.0 74.8 jit_solution(7989587865531925788)
XLA Ops:
  0.0 1.9 %shard_map.109 = f32[32,2,2176]{2,1,0:T(2,128)} custom-call(bf16[64,2048]{1,0:T(8,128)(2,1)} %bitcast.25, bf16[64,128]{1,0:T(8,128)(2,1)} %bitcast.26), custom_call_target="tpu_custom_call" | custom-call | tf_op jit(solution)/shard_map/pallas_call | solution.py:187
  1.9 11.9 %all-to-all-start = ((f32[32,2,2176]{2,1,0:T(2,128)}), f32[32,2,2176]{2,1,0:T(2,128)S(1)}, u32[]{:S(2)}, u32[]{:S(2)}) async-start(f32[32,2,2176]{2,1,0:T(2,128)} %shard_map.109), calls=%async_computation | async-start | bytes 1114112 | tf_op jit(solution)/shard_map/all_to_all | solution.py:194
  13.7 0.1 pad_add_fusion.place_ref
  13.8 0.0 copy-start
  13.8 1.6 %copy-done = bf16[4,128,2048]{2,1,0:T(8,128)(2,1)S(1)} copy-done((bf16[4,128,2048]{2,1,0:T(8,128)(2,1)S(1)}, bf16[4,128,2048]{2,1,0:T(8,128)(2,1)}, u32[]{:S(2)}) %copy-start) | copy-done | bytes 2097176
  15.4 0.0 copy-start.10
  15.4 2.2 %copy-done.10 = bf16[2048,1024]{1,0:T(8,128)(2,1)S(1)} copy-done((bf16[2048,1024]{1,0:T(8,128)(2,1)S(1)}, bf16[2048,1024]{1,0:T(8,128)(2,1)}, u32[]{:S(2)}) %copy-start.10) | copy-done | bytes 4194328
  17.6 4.1 %shard_map.111 = (f32[4,512,128]{2,1,0:T(8,128)S(1)}, f32[4,512,128]{2,1,0:T(8,128)S(1)}) custom-call(s32[2]{0:T(128)S(1)} %pad_add_fusion.place_ref, bf16[512,2048]{1,0:T(8,128)(2,1)S(1)} %bitcast.14, bf16[2048,1024]{1,0:T(8,128)(2,1)S(1)} %copy-done.10), custom_call_target="tpu_custom_call" | custom-call | flops 2147483648 | bytes 10485760 | tf_op jit(solution)/shard_map/pallas_call | solution.py:202
  21.7 1.0 %collective-permute-start = (f32[4,512,128]{2,1,0:T(8,128)S(1)}, f32[4,512,128]{2,1,0:T(8,128)S(1)}, u32[]{:S(2)}, u32[]{:S(2)}) collective-permute-start(f32[4,512,128]{2,1,0:T(8,128)S(1)} %get-tuple-element.30), channel_id=1, source_target_pairs={{0,1},{1,0},{2,3},{3,2},{4,5},{5,4},{6,7},{7,6},{8,9},{9,8},{10,11... | collective-permute-start | bytes 3145736 | tf_op jit(solution)/shard_map/ppermute | solution.py:229
  22.7 2.3 %collective-permute-done.received_ref = f32[4,512,128]{2,1,0:T(8,128)S(1)} collective-permute-done((f32[4,512,128]{2,1,0:T(8,128)S(1)}, f32[4,512,128]{2,1,0:T(8,128)S(1)}, u32[]{:S(2)}, u32[]{:S(2)}) %collective-permute-start) | collective-permute-done | bytes 1048608 | tf_op jit(solution)/shard_map/ppermute | solution.py:229
  25.0 1.0 %shard_map.112 = (f32[512,128]{1,0:T(8,128)S(1)}, f32[512,128]{1,0:T(8,128)}, f32[512,128]{1,0:T(8,128)}, f32[512,128]{1,0:T(8,128)}) custom-call(f32[4,512,128]{2,1,0:T(8,128)S(1)} %get-tuple-element.29.keep_ref, f32[4,512,128]{2,1,0:T(8,128)S(1)} %collective-permute-done.received_ref), custom_call_target="tpu_custom_call" | custom-call | tf_op jit(solution)/shard_map/pallas_call | solution.py:225
  26.0 0.0 copy-start.6
  26.0 0.7 copy-done.6
  26.7 3.9 %all-to-all-done.in_ref = f32[32,2,2176]{2,1,0:T(2,128)S(1)} async-done(((f32[32,2,2176]{2,1,0:T(2,128)}), f32[32,2,2176]{2,1,0:T(2,128)S(1)}, u32[]{:S(2)}, u32[]{:S(2)}) %all-to-all-start) | async-done | bytes 557088 | tf_op jit(solution)/shard_map/all_to_all | solution.py:194
  30.6 1.1 %shard_map.110 = f32[32,2,2176]{2,1,0:T(2,128)} custom-call(f32[32,2,2176]{2,1,0:T(2,128)S(1)} %all-to-all-done.in_ref), custom_call_target="tpu_custom_call" | custom-call | tf_op jit(solution)/shard_map/pallas_call | solution.py:195
  31.7 5.6 %all-to-all-start.1 = ((f32[32,2,2176]{2,1,0:T(2,128)}), f32[32,2,2176]{2,1,0:T(2,128)S(1)}, u32[]{:S(2)}, u32[]{:S(2)}) async-start(f32[32,2,2176]{2,1,0:T(2,128)} %shard_map.110), calls=%async_computation.1 | async-start | bytes 1114112 | tf_op jit(solution)/shard_map/all_to_all | solution.py:231
  37.3 1.4 %collective-permute-start.2 = (f32[512,128]{1,0:T(8,128)}, f32[512,128]{1,0:T(8,128)}, u32[]{:S(2)}, u32[]{:S(2)}) collective-permute-start(f32[512,128]{1,0:T(8,128)} %get-tuple-element.32), channel_id=1, source_target_pairs={{0,2},{1,3},{2,4},{3,5},{4,6},{5,7},{6,0},{7,1},{8,10},{9,11},{10,... | collective-permute-start | bytes 786440 | tf_op jit(solution)/shard_map/ppermute | solution.py:233
  38.7 2.6 %collective-permute-start.3 = (f32[512,128]{1,0:T(8,128)}, f32[512,128]{1,0:T(8,128)}, u32[]{:S(2)}, u32[]{:S(2)}) collective-permute-start(f32[512,128]{1,0:T(8,128)} %get-tuple-element.33), channel_id=1, source_target_pairs={{0,4},{1,5},{2,6},{3,7},{4,0},{5,1},{6,2},{7,3},{8,12},{9,13},{10,... | collective-permute-start | bytes 786440 | tf_op jit(solution)/shard_map/ppermute | solution.py:233
  41.3 1.1 %collective-permute-start.4 = (f32[512,128]{1,0:T(8,128)}, f32[512,128]{1,0:T(8,128)}, u32[]{:S(2)}, u32[]{:S(2)}) collective-permute-start(f32[512,128]{1,0:T(8,128)} %get-tuple-element.34), channel_id=1, source_target_pairs={{0,6},{1,7},{2,0},{3,1},{4,2},{5,3},{6,4},{7,5},{8,14},{9,15},{10,... | collective-permute-start | bytes 786440 | tf_op jit(solution)/shard_map/ppermute | solution.py:233
  42.4 0.0 copy-start.1
  42.4 0.0 copy-start.3
  42.4 6.2 %shard_map.113 = (f32[2048,128]{1,0:T(8,128)}, bf16[2048,128]{1,0:T(8,128)(2,1)}) custom-call(s32[128]{0:T(128)} %length_ref.1, bf16[4,128,1024]{2,1,0:T(8,128)(2,1)} %query_ref.3, bf16[4,128,128]{2,1,0:T(8,128)(2,1)} %fresh_ref.3, bf16[128,64,128]{2,1,0:T(8,128)(2,1)} %bitcast.21, bf16[128,64,128]{2,1,0:T(8,128)(2,1)} %bitcast.23), custom_call_target="tpu_custom_call" | custom-call | flops 134217728 | bytes 5242880 | tf_op jit(solution)/shard_map/pallas_call | solution.py:250
  48.6 4.5 %all-to-all-done.1.step_ref = f32[32,2,2176]{2,1,0:T(2,128)S(1)} async-done(((f32[32,2,2176]{2,1,0:T(2,128)}), f32[32,2,2176]{2,1,0:T(2,128)S(1)}, u32[]{:S(2)}, u32[]{:S(2)}) %all-to-all-start.1) | async-done | bytes 557088 | tf_op jit(solution)/shard_map/all_to_all | solution.py:231
  53.1 0.0 copy-done.1
  53.1 0.0 copy-done.3
  53.1 0.0 copy-done.8
  53.1 0.8 %shard_map.114 = (f32[64,512]{1,0:T(8,128)S(1)}, f32[64,128]{1,0:T(8,128)S(1)}) custom-call(f32[64,2048]{1,0:T(8,128)S(1)} %copy-done.3, f32[64,128]{1,0:T(8,128)S(1)} %bitcast.20, f32[32,2,2176]{2,1,0:T(2,128)S(1)} %all-to-all-done.1.step_ref, bf16[512,2048]{1,0:T(8,128)(2,1)S(1)} %bitcast.15), custom_call_target="tpu_custom_call" | custom-call | tf_op jit(solution)/shard_map/pallas_call | solution.py:279
  54.0 3.6 %collective-permute-start.1 = (f32[64,512]{1,0:T(8,128)S(1)}, f32[64,512]{1,0:T(8,128)S(1)}, u32[]{:S(2)}, u32[]{:S(2)}) collective-permute-start(f32[64,512]{1,0:T(8,128)S(1)} %get-tuple-element.40), channel_id=1, source_target_pairs={{0,1},{1,0},{2,3},{3,2},{4,5},{5,4},{6,7},{7,6},{8,9},{9,8},{10,11... | collective-permute-start | bytes 393224 | tf_op jit(solution)/shard_map/ppermute | solution.py:288
  57.6 1.0 %collective-permute-done.1 = f32[64,512]{1,0:T(8,128)S(1)} collective-permute-done((f32[64,512]{1,0:T(8,128)S(1)}, f32[64,512]{1,0:T(8,128)S(1)}, u32[]{:S(2)}, u32[]{:S(2)}) %collective-permute-start.1) | collective-permute-done | bytes 131104 | tf_op jit(solution)/shard_map/ppermute | solution.py:288
  58.6 0.0 copy-start.2
  58.6 0.0 copy-start.5
  58.6 0.0 copy-start.7
  58.6 0.0 collective-permute-done.2.v1
  58.6 0.0 collective-permute-done.3.v2
  58.7 0.0 collective-permute-done.4.v3
  58.7 2.8 %collective-permute-start.7 = (f32[64,512]{1,0:T(8,128)S(1)}, f32[64,512]{1,0:T(8,128)S(1)}, u32[]{:S(2)}, u32[]{:S(2)}) collective-permute-start(f32[64,512]{1,0:T(8,128)S(1)} %add.9.u0), channel_id=1, source_target_pairs={{0,6},{1,7},{2,0},{3,1},{4,2},{5,3},{6,4},{7,5},{8,14},{9,15},{10,... | collective-permute-start | bytes 393224 | tf_op jit(solution)/shard_map/ppermute | solution.py:292
  61.5 0.3 collective-permute-start.6
  61.8 0.7 collective-permute-start.5
  62.5 0.0 copy-done.4
  62.5 0.0 copy-done.9
  62.5 5.2 %shard_map.115 = (f32[2048,128]{1,0:T(8,128)S(1)}, bf16[2048,128]{1,0:T(8,128)(2,1)S(1)}) custom-call(s32[128]{0:T(128)S(1)} %copy-done.9, bf16[4,128,1024]{2,1,0:T(8,128)(2,1)} %query_ref.3, bf16[4,128,128]{2,1,0:T(8,128)(2,1)S(1)} %copy-done.4, bf16[128,64,128]{2,1,0:T(8,128)(2,1)} %bitcast.22, bf16[128,64,128]{2,1,0:T(8,128)(2,1)} %bitcast.24), custom_call_target="tpu_custom_call" | custom-call | flops 134217728 | bytes 5242880 | tf_op jit(solution)/shard_map/pallas_call | solution.py:250
  67.7 0.0 collective-permute-done.7.u3
  67.7 0.0 collective-permute-done.6.u2
  67.8 3.5 %collective-permute-done.5.u1 = f32[64,512]{1,0:T(8,128)S(1)} collective-permute-done((f32[64,512]{1,0:T(8,128)S(1)}, f32[64,512]{1,0:T(8,128)S(1)}, u32[]{:S(2)}, u32[]{:S(2)}) %collective-permute-start.5) | collective-permute-done | bytes 131104 | tf_op jit(solution)/shard_map/ppermute | solution.py:292
  71.2 0.0 copy-done.2
  71.2 0.0 copy-done.5
  71.2 0.0 copy-done.7
  71.2 3.6 %shard_map.116 = bf16[4,128,1024]{2,1,0:T(8,128)(2,1)} custom-call(f32[512,128]{1,0:T(8,128)S(1)} %copy-done.7, f32[512,128]{1,0:T(8,128)} %collective-permute-done.2.v1, f32[512,128]{1,0:T(8,128)} %collective-permute-done.3.v2, f32[512,128]{1,0:T(8,128)} %collective-permute-done.4.v3, f32[64,512]{1,0:T(8,128)S(1)} %add.9.u0, ...), custom_call_target="tpu_custom_call" | custom-call | tf_op jit(solution)/shard_map/pallas_call | solution.py:295
  (4 shorter events, 0.0 us)
Async XLA Ops:
  1.9 28.7 %all-to-all-start = ((f32[32,2,2176]{2,1,0:T(2,128)}), f32[32,2,2176]{2,1,0:T(2,128)S(1)}, u32[]{:S(2)}, u32[]{:S(2)}) async-start(f32[32,2,2176]{2,1,0:T(2,128)} %shard_map.109), calls=%async_computation | async-start | bytes 1114112 | tf_op jit(solution)/shard_map/all_to_all | solution.py:194
  13.8 1.6 %copy-start = (bf16[4,128,2048]{2,1,0:T(8,128)(2,1)S(1)}, bf16[4,128,2048]{2,1,0:T(8,128)(2,1)}, u32[]{:S(2)}) copy-start(bf16[4,128,2048]{2,1,0:T(8,128)(2,1)} %param.11) | copy-start | bytes 6291460
  15.4 2.2 %copy-start.10 = (bf16[2048,1024]{1,0:T(8,128)(2,1)S(1)}, bf16[2048,1024]{1,0:T(8,128)(2,1)}, u32[]{:S(2)}) copy-start(bf16[2048,1024]{1,0:T(8,128)(2,1)} %weight_ref.1) | copy-start | bytes 12582916
  21.7 3.3 %collective-permute-start = (f32[4,512,128]{2,1,0:T(8,128)S(1)}, f32[4,512,128]{2,1,0:T(8,128)S(1)}, u32[]{:S(2)}, u32[]{:S(2)}) collective-permute-start(f32[4,512,128]{2,1,0:T(8,128)S(1)} %get-tuple-element.30), channel_id=1, source_target_pairs={{0,1},{1,0},{2,3},{3,2},{4,5},{5,4},{6,7},{7,6},{8,9},{9,8},{10,11... | collective-permute-start | bytes 3145736 | tf_op jit(solution)/shard_map/ppermute | solution.py:229
  26.0 0.7 copy-start.6
  31.7 21.4 %all-to-all-start.1 = ((f32[32,2,2176]{2,1,0:T(2,128)}), f32[32,2,2176]{2,1,0:T(2,128)S(1)}, u32[]{:S(2)}, u32[]{:S(2)}) async-start(f32[32,2,2176]{2,1,0:T(2,128)} %shard_map.110), calls=%async_computation.1 | async-start | bytes 1114112 | tf_op jit(solution)/shard_map/all_to_all | solution.py:231
  37.3 21.4 %collective-permute-start.2 = (f32[512,128]{1,0:T(8,128)}, f32[512,128]{1,0:T(8,128)}, u32[]{:S(2)}, u32[]{:S(2)}) collective-permute-start(f32[512,128]{1,0:T(8,128)} %get-tuple-element.32), channel_id=1, source_target_pairs={{0,2},{1,3},{2,4},{3,5},{4,6},{5,7},{6,0},{7,1},{8,10},{9,11},{10,... | collective-permute-start | bytes 786440 | tf_op jit(solution)/shard_map/ppermute | solution.py:233
  38.7 20.0 %collective-permute-start.3 = (f32[512,128]{1,0:T(8,128)}, f32[512,128]{1,0:T(8,128)}, u32[]{:S(2)}, u32[]{:S(2)}) collective-permute-start(f32[512,128]{1,0:T(8,128)} %get-tuple-element.33), channel_id=1, source_target_pairs={{0,4},{1,5},{2,6},{3,7},{4,0},{5,1},{6,2},{7,3},{8,12},{9,13},{10,... | collective-permute-start | bytes 786440 | tf_op jit(solution)/shard_map/ppermute | solution.py:233
  41.3 17.4 %collective-permute-start.4 = (f32[512,128]{1,0:T(8,128)}, f32[512,128]{1,0:T(8,128)}, u32[]{:S(2)}, u32[]{:S(2)}) collective-permute-start(f32[512,128]{1,0:T(8,128)} %get-tuple-element.34), channel_id=1, source_target_pairs={{0,6},{1,7},{2,0},{3,1},{4,2},{5,3},{6,4},{7,5},{8,14},{9,15},{10,... | collective-permute-start | bytes 786440 | tf_op jit(solution)/shard_map/ppermute | solution.py:233
  42.4 10.8 %copy-start.1 = (bf16[4,128,2048]{2,1,0:T(8,128)(2,1)S(1)}, bf16[4,128,2048]{2,1,0:T(8,128)(2,1)}, u32[]{:S(2)}) copy-start(bf16[4,128,2048]{2,1,0:T(8,128)(2,1)} %param.11) | copy-start | bytes 6291460
  42.4 10.8 %copy-start.3 = (f32[64,2048]{1,0:T(8,128)S(1)}, f32[64,2048]{1,0:T(8,128)}, u32[]{:S(2)}) copy-start(f32[64,2048]{1,0:T(8,128)} %a_ref.1) | copy-start | bytes 1572868
  42.4 10.8 %copy-start.8 = (f32[128,64]{0,1:T(8,128)S(1)}, f32[128,64]{0,1:T(8,128)}, u32[]{:S(2)}) copy-start(f32[128,64]{0,1:T(8,128)} %param.20) | copy-start | bytes 98308
  48.6 13.9 %copy-start.4 = (bf16[4,128,128]{2,1,0:T(8,128)(2,1)S(1)}, bf16[4,128,128]{2,1,0:T(8,128)(2,1)}, u32[]{:S(2)}) copy-start(bf16[4,128,128]{2,1,0:T(8,128)(2,1)} %fresh_ref.3) | copy-start | bytes 393220
  48.6 13.9 %copy-start.9 = (s32[128]{0:T(128)S(1)}, s32[128]{0:T(128)}, u32[]{:S(2)}) copy-start(s32[128]{0:T(128)} %length_ref.1) | copy-start | bytes 1540
  54.0 4.6 %collective-permute-start.1 = (f32[64,512]{1,0:T(8,128)S(1)}, f32[64,512]{1,0:T(8,128)S(1)}, u32[]{:S(2)}, u32[]{:S(2)}) collective-permute-start(f32[64,512]{1,0:T(8,128)S(1)} %get-tuple-element.40), channel_id=1, source_target_pairs={{0,1},{1,0},{2,3},{3,2},{4,5},{5,4},{6,7},{7,6},{8,9},{9,8},{10,11... | collective-permute-start | bytes 393224 | tf_op jit(solution)/shard_map/ppermute | solution.py:288
  58.6 12.6 %copy-start.2 = (f32[2048,128]{1,0:T(8,128)S(1)}, f32[2048,128]{1,0:T(8,128)}, u32[]{:S(2)}) copy-start(f32[2048,128]{1,0:T(8,128)} %get-tuple-element.37) | copy-start | bytes 3145732
  58.6 12.6 %copy-start.5 = (bf16[2048,128]{1,0:T(8,128)(2,1)S(1)}, bf16[2048,128]{1,0:T(8,128)(2,1)}, u32[]{:S(2)}) copy-start(bf16[2048,128]{1,0:T(8,128)(2,1)} %get-tuple-element.38) | copy-start | bytes 1572868
  58.6 12.6 %copy-start.7 = (f32[512,128]{1,0:T(8,128)S(1)}, f32[512,128]{1,0:T(8,128)}, u32[]{:S(2)}) copy-start(f32[512,128]{1,0:T(8,128)} %copy-done.6) | copy-start | bytes 786436
  58.7 9.1 %collective-permute-start.7 = (f32[64,512]{1,0:T(8,128)S(1)}, f32[64,512]{1,0:T(8,128)S(1)}, u32[]{:S(2)}, u32[]{:S(2)}) collective-permute-start(f32[64,512]{1,0:T(8,128)S(1)} %add.9.u0), channel_id=1, source_target_pairs={{0,6},{1,7},{2,0},{3,1},{4,2},{5,3},{6,4},{7,5},{8,14},{9,15},{10,... | collective-permute-start | bytes 393224 | tf_op jit(solution)/shard_map/ppermute | solution.py:292
  61.5 6.3 %collective-permute-start.6 = (f32[64,512]{1,0:T(8,128)S(1)}, f32[64,512]{1,0:T(8,128)S(1)}, u32[]{:S(2)}, u32[]{:S(2)}) collective-permute-start(f32[64,512]{1,0:T(8,128)S(1)} %add.9.u0), channel_id=1, source_target_pairs={{0,4},{1,5},{2,6},{3,7},{4,0},{5,1},{6,2},{7,3},{8,12},{9,13},{10,... | collective-permute-start | bytes 393224 | tf_op jit(solution)/shard_map/ppermute | solution.py:292
  61.8 9.4 %collective-permute-start.5 = (f32[64,512]{1,0:T(8,128)S(1)}, f32[64,512]{1,0:T(8,128)S(1)}, u32[]{:S(2)}, u32[]{:S(2)}) collective-permute-start(f32[64,512]{1,0:T(8,128)S(1)} %add.9.u0), channel_id=1, source_target_pairs={{0,2},{1,3},{2,4},{3,5},{4,6},{5,7},{6,0},{7,1},{8,10},{9,11},{10,... | collective-permute-start | bytes 393224 | tf_op jit(solution)/shard_map/ppermute | solution.py:292

commit v6 on v5

--- a/solution.py
+++ b/solution.py
@@ -119,44 +119,45 @@
 
 
 def finish_kernel(v0, v1, v2, v3, u0, u1, u2, u3, b_ref, *refs):
-    *halves, out_ref, value_ref = refs
-    t = pl.program_id(0)
+    *halves, out_ref, value_ref, held_ref, sems = refs
     blocks, lanes, dim = value_ref.shape
-    steps = pl.num_programs(0)
-    rows = out_ref.shape[1]
+    steps, rows, width = held_ref.shape
     block_rows = rows // blocks
-    heads = out_ref.shape[2] // dim
-
-    @pl.when(t == 0)
-    def _():
-        u = (u0[...] + u1[...]) + (u2[...] + u3[...])
-        u_high, u_low = split_bf16(u)
-        b_high, b_low = split_bf16(b_ref[...])
-        dims = (((0,), (0,)), ((), ()))
-        mm = functools.partial(
-            lax.dot_general, dimension_numbers=dims, preferred_element_type=jnp.float32
-        )
-        delta = mm(u_high, b_high) + (mm(u_low, b_high) + mm(u_high, b_low))
-        values = (v0[...] + v1[...]) + (v2[...] + v3[...]) + ADAPTER_SCALE * delta
-        values = values.astype(jnp.bfloat16)
+    heads = width // dim
+    u = (u0[...] + u1[...]) + (u2[...] + u3[...])
+    u_high, u_low = split_bf16(u)
+    b_high, b_low = split_bf16(b_ref[...])
+    dims = (((0,), (0,)), ((), ()))
+    mm = functools.partial(
+        lax.dot_general, dimension_numbers=dims, preferred_element_type=jnp.float32
+    )
+    delta = mm(u_high, b_high) + (mm(u_low, b_high) + mm(u_high, b_low))
+    values = (v0[...] + v1[...]) + (v2[...] + v3[...]) + ADAPTER_SCALE * delta
+    values = values.astype(jnp.bfloat16)
+    for i in range(blocks):
+        for s in range(steps):
+            at = s * rows + i * block_rows
+            value_ref[i, s * block_rows : (s + 1) * block_rows] = values[at : at + block_rows]
+
+    size = heads * block_rows
+    half = blocks // 2
+    copies = []
+    for t in range(steps):
+        at = slice(t * size, (t + 1) * size)
         for i in range(blocks):
-            for s in range(lanes // block_rows):
-                at = s * rows + i * block_rows
-                value_ref[i, s * block_rows : (s + 1) * block_rows] = values[at : at + block_rows]
-
-    size = heads * block_rows
-    start = pl.multiple_of(t * size, size)
-    half = blocks // 2
-    for i in range(blocks):
-        part_ref, weight_ref = halves[2 * (i // half) : 2 * (i // half) + 2]
-        fresh = jnp.dot(
-            weight_ref[i % half, pl.ds(start, size), :], value_ref[i], preferred_element_type=jnp.float32
-        )
-        context = part_ref[i % half, pl.ds(start, size), :] + fresh
-        for g in range(heads):
-            out_ref[0, i * block_rows : (i + 1) * block_rows, g * dim : (g + 1) * dim] = context[
-                g * block_rows : (g + 1) * block_rows
-            ].astype(out_ref.dtype)
+            part_ref, weight_ref = halves[2 * (i // half) : 2 * (i // half) + 2]
+            fresh = jnp.dot(
+                weight_ref[i % half, at], value_ref[i], preferred_element_type=jnp.float32
+            )
+            context = part_ref[i % half, at] + fresh
+            for g in range(heads):
+                held_ref[t, i * block_rows : (i + 1) * block_rows, g * dim : (g + 1) * dim] = (
+                    context[g * block_rows : (g + 1) * block_rows].astype(held_ref.dtype)
+                )
+        copies.append(pltpu.make_async_copy(held_ref.at[t], out_ref.at[t], sems.at[t]))
+        copies[-1].start()
+    for copy in copies:
+        copy.wait()
 
 
 def shards(
@@ -294,11 +295,14 @@
     operands = [*base_parts, *inner_parts, new_b, *first_half, *second_half]
     return pl.pallas_call(
         finish_kernel,
-        grid=(step_count,),
         out_shape=jax.ShapeDtypeStruct(queries.shape, jnp.bfloat16),
         in_specs=[pl.BlockSpec(memory_space=pltpu.VMEM)] * len(operands),
-        out_specs=pl.BlockSpec((1, rows_dev, group_size * head_dim), lambda t: (t, 0, 0)),
-        scratch_shapes=[pltpu.VMEM((blocks, step_count * block_rows, head_dim), jnp.bfloat16)],
+        out_specs=pl.BlockSpec(memory_space=pl.ANY),
+        scratch_shapes=[
+            pltpu.VMEM((blocks, step_count * block_rows, head_dim), jnp.bfloat16),
+            pltpu.VMEM(queries.shape, jnp.bfloat16),
+            pltpu.SemaphoreType.DMA((step_count,)),
+        ],
         compiler_params=small_vmem,
     )(*operands)
 

time: 75.2 us -> 74.4 us (0.989)
    pallas_call x1, Pallas kernels: 3.56 us -> 2.8 us  [shards(): pl.pallas_call(finish_kernel, out_shape=jax.ShapeDtypeStruct(queries.shap...]
where the time goes in v6:
time: 74.4 us; the launch traced here: 74 us
  starting transfers between devices  31 us (42%)
  Pallas kernels  23.1 us (31%)
  waiting for transfers between devices  15.2 us (20%)
  local copies, waits for them, and re-layouts  4.51 us (6%)
    all_to_all x1, starting transfers between devices, shards(): mine = lax.all_to_all(terms, 'dp', 0, 0, tiled=True)  11.9 us
    pallas_call x2, Pallas kernels, attend(): pl.pallas_call(functools.partial(cache_kernel, offset), grid_spec=pltpu.P...  11.4 us
    all_to_all x1, starting transfers between devices, shards(): steps_ab = lax.all_to_all(mine, 'dp', 0, 0, tiled=True)  5.59 us
    ppermute x3, starting transfers between devices, shards(): lax.ppermute(paired[k], 'mp', along_y(k))  5.06 us
    all_to_all x1, waiting for transfers between devices, shards(): steps_ab = lax.all_to_all(mine, 'dp', 0, 0, tiled=True)  4.52 us
    unnamed x22, local copies, waits for them, and re-layouts  4.51 us
    pallas_call x1, Pallas kernels, shards(): pl.pallas_call(project_kernel, grid_spec=pltpu.PrefetchScalarGridSpec(num...  4.07 us
    all_to_all x1, waiting for transfers between devices, shards(): mine = lax.all_to_all(terms, 'dp', 0, 0, tiled=True)  3.91 us
  transfers between devices with their start and end apart: 10, of which 5 were waited for; matrix products, arithmetic and copies ran while one was open for 0% of the time, Pallas kernels for 23%

profile of v6, /device:TPU:1, one launch (start us, length us, event | category | flops | bytes accessed | tf_op | source)
XLA Modules:
  0.0 74.0 jit_solution(10033487659432199317)
XLA Ops:
  0.0 1.9 %shard_map.109 = f32[32,2,2176]{2,1,0:T(2,128)} custom-call(bf16[64,2048]{1,0:T(8,128)(2,1)} %bitcast.25, bf16[64,128]{1,0:T(8,128)(2,1)} %bitcast.26), custom_call_target="tpu_custom_call" | custom-call | tf_op jit(solution)/shard_map/pallas_call | solution.py:188
  1.9 11.9 %all-to-all-start = ((f32[32,2,2176]{2,1,0:T(2,128)}), f32[32,2,2176]{2,1,0:T(2,128)S(1)}, u32[]{:S(2)}, u32[]{:S(2)}) async-start(f32[32,2,2176]{2,1,0:T(2,128)} %shard_map.109), calls=%async_computation | async-start | bytes 1114112 | tf_op jit(solution)/shard_map/all_to_all | solution.py:195
  13.7 0.1 pad_add_fusion.place_ref
  13.8 0.0 copy-start
  13.8 1.6 %copy-done = bf16[4,128,2048]{2,1,0:T(8,128)(2,1)S(1)} copy-done((bf16[4,128,2048]{2,1,0:T(8,128)(2,1)S(1)}, bf16[4,128,2048]{2,1,0:T(8,128)(2,1)}, u32[]{:S(2)}) %copy-start) | copy-done | bytes 2097176
  15.4 0.0 copy-start.10
  15.4 2.2 %copy-done.10 = bf16[2048,1024]{1,0:T(8,128)(2,1)S(1)} copy-done((bf16[2048,1024]{1,0:T(8,128)(2,1)S(1)}, bf16[2048,1024]{1,0:T(8,128)(2,1)}, u32[]{:S(2)}) %copy-start.10) | copy-done | bytes 4194328
  17.6 4.1 %shard_map.111 = (f32[4,512,128]{2,1,0:T(8,128)S(1)}, f32[4,512,128]{2,1,0:T(8,128)S(1)}) custom-call(s32[2]{0:T(128)S(1)} %pad_add_fusion.place_ref, bf16[512,2048]{1,0:T(8,128)(2,1)S(1)} %bitcast.14, bf16[2048,1024]{1,0:T(8,128)(2,1)S(1)} %copy-done.10), custom_call_target="tpu_custom_call" | custom-call | flops 2147483648 | bytes 10485760 | tf_op jit(solution)/shard_map/pallas_call | solution.py:203
  21.7 1.0 %collective-permute-start = (f32[4,512,128]{2,1,0:T(8,128)S(1)}, f32[4,512,128]{2,1,0:T(8,128)S(1)}, u32[]{:S(2)}, u32[]{:S(2)}) collective-permute-start(f32[4,512,128]{2,1,0:T(8,128)S(1)} %get-tuple-element.30), channel_id=1, source_target_pairs={{0,1},{1,0},{2,3},{3,2},{4,5},{5,4},{6,7},{7,6},{8,9},{9,8},{10,11... | collective-permute-start | bytes 3145736 | tf_op jit(solution)/shard_map/ppermute | solution.py:230
  22.7 2.3 %collective-permute-done.received_ref = f32[4,512,128]{2,1,0:T(8,128)S(1)} collective-permute-done((f32[4,512,128]{2,1,0:T(8,128)S(1)}, f32[4,512,128]{2,1,0:T(8,128)S(1)}, u32[]{:S(2)}, u32[]{:S(2)}) %collective-permute-start) | collective-permute-done | bytes 1048608 | tf_op jit(solution)/shard_map/ppermute | solution.py:230
  25.0 1.0 %shard_map.112 = (f32[512,128]{1,0:T(8,128)S(1)}, f32[512,128]{1,0:T(8,128)}, f32[512,128]{1,0:T(8,128)}, f32[512,128]{1,0:T(8,128)}) custom-call(f32[4,512,128]{2,1,0:T(8,128)S(1)} %get-tuple-element.29.keep_ref, f32[4,512,128]{2,1,0:T(8,128)S(1)} %collective-permute-done.received_ref), custom_call_target="tpu_custom_call" | custom-call | tf_op jit(solution)/shard_map/pallas_call | solution.py:226
  26.0 0.0 copy-start.6
  26.0 0.7 copy-done.6
  26.7 3.9 %all-to-all-done.in_ref = f32[32,2,2176]{2,1,0:T(2,128)S(1)} async-done(((f32[32,2,2176]{2,1,0:T(2,128)}), f32[32,2,2176]{2,1,0:T(2,128)S(1)}, u32[]{:S(2)}, u32[]{:S(2)}) %all-to-all-start) | async-done | bytes 557088 | tf_op jit(solution)/shard_map/all_to_all | solution.py:195
  30.6 1.1 %shard_map.110 = f32[32,2,2176]{2,1,0:T(2,128)} custom-call(f32[32,2,2176]{2,1,0:T(2,128)S(1)} %all-to-all-done.in_ref), custom_call_target="tpu_custom_call" | custom-call | tf_op jit(solution)/shard_map/pallas_call | solution.py:196
  31.7 5.6 %all-to-all-start.1 = ((f32[32,2,2176]{2,1,0:T(2,128)}), f32[32,2,2176]{2,1,0:T(2,128)S(1)}, u32[]{:S(2)}, u32[]{:S(2)}) async-start(f32[32,2,2176]{2,1,0:T(2,128)} %shard_map.110), calls=%async_computation.1 | async-start | bytes 1114112 | tf_op jit(solution)/shard_map/all_to_all | solution.py:232
  37.3 1.4 %collective-permute-start.2 = (f32[512,128]{1,0:T(8,128)}, f32[512,128]{1,0:T(8,128)}, u32[]{:S(2)}, u32[]{:S(2)}) collective-permute-start(f32[512,128]{1,0:T(8,128)} %get-tuple-element.32), channel_id=1, source_target_pairs={{0,2},{1,3},{2,4},{3,5},{4,6},{5,7},{6,0},{7,1},{8,10},{9,11},{10,... | collective-permute-start | bytes 786440 | tf_op jit(solution)/shard_map/ppermute | solution.py:234
  38.7 2.6 %collective-permute-start.3 = (f32[512,128]{1,0:T(8,128)}, f32[512,128]{1,0:T(8,128)}, u32[]{:S(2)}, u32[]{:S(2)}) collective-permute-start(f32[512,128]{1,0:T(8,128)} %get-tuple-element.33), channel_id=1, source_target_pairs={{0,4},{1,5},{2,6},{3,7},{4,0},{5,1},{6,2},{7,3},{8,12},{9,13},{10,... | collective-permute-start | bytes 786440 | tf_op jit(solution)/shard_map/ppermute | solution.py:234
  41.3 1.1 %collective-permute-start.4 = (f32[512,128]{1,0:T(8,128)}, f32[512,128]{1,0:T(8,128)}, u32[]{:S(2)}, u32[]{:S(2)}) collective-permute-start(f32[512,128]{1,0:T(8,128)} %get-tuple-element.34), channel_id=1, source_target_pairs={{0,6},{1,7},{2,0},{3,1},{4,2},{5,3},{6,4},{7,5},{8,14},{9,15},{10,... | collective-permute-start | bytes 786440 | tf_op jit(solution)/shard_map/ppermute | solution.py:234
  42.4 0.0 copy-start.1
  42.4 0.0 copy-start.3
  42.4 6.2 %shard_map.113 = (f32[2048,128]{1,0:T(8,128)}, bf16[2048,128]{1,0:T(8,128)(2,1)}) custom-call(s32[128]{0:T(128)} %length_ref.1, bf16[4,128,1024]{2,1,0:T(8,128)(2,1)} %query_ref.3, bf16[4,128,128]{2,1,0:T(8,128)(2,1)} %fresh_ref.3, bf16[128,64,128]{2,1,0:T(8,128)(2,1)} %bitcast.21, bf16[128,64,128]{2,1,0:T(8,128)(2,1)} %bitcast.23), custom_call_target="tpu_custom_call" | custom-call | flops 134217728 | bytes 5242880 | tf_op jit(solution)/shard_map/pallas_call | solution.py:251
  48.6 4.5 %all-to-all-done.1.step_ref = f32[32,2,2176]{2,1,0:T(2,128)S(1)} async-done(((f32[32,2,2176]{2,1,0:T(2,128)}), f32[32,2,2176]{2,1,0:T(2,128)S(1)}, u32[]{:S(2)}, u32[]{:S(2)}) %all-to-all-start.1) | async-done | bytes 557088 | tf_op jit(solution)/shard_map/all_to_all | solution.py:232
  53.1 0.0 copy-done.1
  53.1 0.0 copy-done.3
  53.1 0.0 copy-done.8
  53.1 0.8 %shard_map.114 = (f32[64,512]{1,0:T(8,128)S(1)}, f32[64,128]{1,0:T(8,128)S(1)}) custom-call(f32[64,2048]{1,0:T(8,128)S(1)} %copy-done.3, f32[64,128]{1,0:T(8,128)S(1)} %bitcast.20, f32[32,2,2176]{2,1,0:T(2,128)S(1)} %all-to-all-done.1.step_ref, bf16[512,2048]{1,0:T(8,128)(2,1)S(1)} %bitcast.15), custom_call_target="tpu_custom_call" | custom-call | tf_op jit(solution)/shard_map/pallas_call | solution.py:280
  54.0 3.6 %collective-permute-start.1 = (f32[64,512]{1,0:T(8,128)S(1)}, f32[64,512]{1,0:T(8,128)S(1)}, u32[]{:S(2)}, u32[]{:S(2)}) collective-permute-start(f32[64,512]{1,0:T(8,128)S(1)} %get-tuple-element.40), channel_id=1, source_target_pairs={{0,1},{1,0},{2,3},{3,2},{4,5},{5,4},{6,7},{7,6},{8,9},{9,8},{10,11... | collective-permute-start | bytes 393224 | tf_op jit(solution)/shard_map/ppermute | solution.py:289
  57.6 1.0 %collective-permute-done.1 = f32[64,512]{1,0:T(8,128)S(1)} collective-permute-done((f32[64,512]{1,0:T(8,128)S(1)}, f32[64,512]{1,0:T(8,128)S(1)}, u32[]{:S(2)}, u32[]{:S(2)}) %collective-permute-start.1) | collective-permute-done | bytes 131104 | tf_op jit(solution)/shard_map/ppermute | solution.py:289
  58.6 0.0 copy-start.2
  58.6 0.0 copy-start.5
  58.6 0.0 copy-start.7
  58.6 0.0 collective-permute-done.2.v1
  58.6 0.0 collective-permute-done.3.v2
  58.7 0.0 collective-permute-done.4.v3
  58.7 2.8 %collective-permute-start.7 = (f32[64,512]{1,0:T(8,128)S(1)}, f32[64,512]{1,0:T(8,128)S(1)}, u32[]{:S(2)}, u32[]{:S(2)}) collective-permute-start(f32[64,512]{1,0:T(8,128)S(1)} %add.9.u0), channel_id=1, source_target_pairs={{0,6},{1,7},{2,0},{3,1},{4,2},{5,3},{6,4},{7,5},{8,14},{9,15},{10,... | collective-permute-start | bytes 393224 | tf_op jit(solution)/shard_map/ppermute | solution.py:293
  61.5 0.3 collective-permute-start.6
  61.8 0.7 collective-permute-start.5
  62.5 0.0 copy-done.4
  62.5 0.0 copy-done.9
  62.5 5.2 %shard_map.115 = (f32[2048,128]{1,0:T(8,128)S(1)}, bf16[2048,128]{1,0:T(8,128)(2,1)S(1)}) custom-call(s32[128]{0:T(128)S(1)} %copy-done.9, bf16[4,128,1024]{2,1,0:T(8,128)(2,1)} %query_ref.3, bf16[4,128,128]{2,1,0:T(8,128)(2,1)S(1)} %copy-done.4, bf16[128,64,128]{2,1,0:T(8,128)(2,1)} %bitcast.22, bf16[128,64,128]{2,1,0:T(8,128)(2,1)} %bitcast.24), custom_call_target="tpu_custom_call" | custom-call | flops 134217728 | bytes 5242880 | tf_op jit(solution)/shard_map/pallas_call | solution.py:251
  67.7 0.0 collective-permute-done.7.u3
  67.7 0.0 collective-permute-done.6.u2
  67.8 3.5 %collective-permute-done.5.u1 = f32[64,512]{1,0:T(8,128)S(1)} collective-permute-done((f32[64,512]{1,0:T(8,128)S(1)}, f32[64,512]{1,0:T(8,128)S(1)}, u32[]{:S(2)}, u32[]{:S(2)}) %collective-permute-start.5) | collective-permute-done | bytes 131104 | tf_op jit(solution)/shard_map/ppermute | solution.py:293
  71.2 0.0 copy-done.2
  71.2 0.0 copy-done.5
  71.2 0.0 copy-done.7
  71.2 2.8 %shard_map.116 = bf16[4,128,1024]{2,1,0:T(8,128)(2,1)} custom-call(f32[512,128]{1,0:T(8,128)S(1)} %copy-done.7, f32[512,128]{1,0:T(8,128)} %collective-permute-done.2.v1, f32[512,128]{1,0:T(8,128)} %collective-permute-done.3.v2, f32[512,128]{1,0:T(8,128)} %collective-permute-done.4.v3, f32[64,512]{1,0:T(8,128)S(1)} %add.9.u0, ...), custom_call_target="tpu_custom_call" | custom-call | tf_op jit(solution)/shard_map/pallas_call | solution.py:296
  (4 shorter events, 0.0 us)
Async XLA Ops:
  1.9 28.7 %all-to-all-start = ((f32[32,2,2176]{2,1,0:T(2,128)}), f32[32,2,2176]{2,1,0:T(2,128)S(1)}, u32[]{:S(2)}, u32[]{:S(2)}) async-start(f32[32,2,2176]{2,1,0:T(2,128)} %shard_map.109), calls=%async_computation | async-start | bytes 1114112 | tf_op jit(solution)/shard_map/all_to_all | solution.py:195
  13.8 1.6 %copy-start = (bf16[4,128,2048]{2,1,0:T(8,128)(2,1)S(1)}, bf16[4,128,2048]{2,1,0:T(8,128)(2,1)}, u32[]{:S(2)}) copy-start(bf16[4,128,2048]{2,1,0:T(8,128)(2,1)} %param.11) | copy-start | bytes 6291460
  15.4 2.2 %copy-start.10 = (bf16[2048,1024]{1,0:T(8,128)(2,1)S(1)}, bf16[2048,1024]{1,0:T(8,128)(2,1)}, u32[]{:S(2)}) copy-start(bf16[2048,1024]{1,0:T(8,128)(2,1)} %weight_ref.1) | copy-start | bytes 12582916
  21.7 3.3 %collective-permute-start = (f32[4,512,128]{2,1,0:T(8,128)S(1)}, f32[4,512,128]{2,1,0:T(8,128)S(1)}, u32[]{:S(2)}, u32[]{:S(2)}) collective-permute-start(f32[4,512,128]{2,1,0:T(8,128)S(1)} %get-tuple-element.30), channel_id=1, source_target_pairs={{0,1},{1,0},{2,3},{3,2},{4,5},{5,4},{6,7},{7,6},{8,9},{9,8},{10,11... | collective-permute-start | bytes 3145736 | tf_op jit(solution)/shard_map/ppermute | solution.py:230
  26.0 0.7 copy-start.6
  31.7 21.4 %all-to-all-start.1 = ((f32[32,2,2176]{2,1,0:T(2,128)}), f32[32,2,2176]{2,1,0:T(2,128)S(1)}, u32[]{:S(2)}, u32[]{:S(2)}) async-start(f32[32,2,2176]{2,1,0:T(2,128)} %shard_map.110), calls=%async_computation.1 | async-start | bytes 1114112 | tf_op jit(solution)/shard_map/all_to_all | solution.py:232
  37.3 21.4 %collective-permute-start.2 = (f32[512,128]{1,0:T(8,128)}, f32[512,128]{1,0:T(8,128)}, u32[]{:S(2)}, u32[]{:S(2)}) collective-permute-start(f32[512,128]{1,0:T(8,128)} %get-tuple-element.32), channel_id=1, source_target_pairs={{0,2},{1,3},{2,4},{3,5},{4,6},{5,7},{6,0},{7,1},{8,10},{9,11},{10,... | collective-permute-start | bytes 786440 | tf_op jit(solution)/shard_map/ppermute | solution.py:234
  38.7 20.0 %collective-permute-start.3 = (f32[512,128]{1,0:T(8,128)}, f32[512,128]{1,0:T(8,128)}, u32[]{:S(2)}, u32[]{:S(2)}) collective-permute-start(f32[512,128]{1,0:T(8,128)} %get-tuple-element.33), channel_id=1, source_target_pairs={{0,4},{1,5},{2,6},{3,7},{4,0},{5,1},{6,2},{7,3},{8,12},{9,13},{10,... | collective-permute-start | bytes 786440 | tf_op jit(solution)/shard_map/ppermute | solution.py:234
  41.3 17.4 %collective-permute-start.4 = (f32[512,128]{1,0:T(8,128)}, f32[512,128]{1,0:T(8,128)}, u32[]{:S(2)}, u32[]{:S(2)}) collective-permute-start(f32[512,128]{1,0:T(8,128)} %get-tuple-element.34), channel_id=1, source_target_pairs={{0,6},{1,7},{2,0},{3,1},{4,2},{5,3},{6,4},{7,5},{8,14},{9,15},{10,... | collective-permute-start | bytes 786440 | tf_op jit(solution)/shard_map/ppermute | solution.py:234
  42.4 10.8 %copy-start.1 = (bf16[4,128,2048]{2,1,0:T(8,128)(2,1)S(1)}, bf16[4,128,2048]{2,1,0:T(8,128)(2,1)}, u32[]{:S(2)}) copy-start(bf16[4,128,2048]{2,1,0:T(8,128)(2,1)} %param.11) | copy-start | bytes 6291460
  42.4 10.8 %copy-start.3 = (f32[64,2048]{1,0:T(8,128)S(1)}, f32[64,2048]{1,0:T(8,128)}, u32[]{:S(2)}) copy-start(f32[64,2048]{1,0:T(8,128)} %a_ref.1) | copy-start | bytes 1572868
  42.4 10.8 %copy-start.8 = (f32[128,64]{0,1:T(8,128)S(1)}, f32[128,64]{0,1:T(8,128)}, u32[]{:S(2)}) copy-start(f32[128,64]{0,1:T(8,128)} %param.20) | copy-start | bytes 98308
  48.6 13.9 %copy-start.4 = (bf16[4,128,128]{2,1,0:T(8,128)(2,1)S(1)}, bf16[4,128,128]{2,1,0:T(8,128)(2,1)}, u32[]{:S(2)}) copy-start(bf16[4,128,128]{2,1,0:T(8,128)(2,1)} %fresh_ref.3) | copy-start | bytes 393220
  48.6 13.9 %copy-start.9 = (s32[128]{0:T(128)S(1)}, s32[128]{0:T(128)}, u32[]{:S(2)}) copy-start(s32[128]{0:T(128)} %length_ref.1) | copy-start | bytes 1540
  54.0 4.6 %collective-permute-start.1 = (f32[64,512]{1,0:T(8,128)S(1)}, f32[64,512]{1,0:T(8,128)S(1)}, u32[]{:S(2)}, u32[]{:S(2)}) collective-permute-start(f32[64,512]{1,0:T(8,128)S(1)} %get-tuple-element.40), channel_id=1, source_target_pairs={{0,1},{1,0},{2,3},{3,2},{4,5},{5,4},{6,7},{7,6},{8,9},{9,8},{10,11... | collective-permute-start | bytes 393224 | tf_op jit(solution)/shard_map/ppermute | solution.py:289
  58.6 12.6 %copy-start.2 = (f32[2048,128]{1,0:T(8,128)S(1)}, f32[2048,128]{1,0:T(8,128)}, u32[]{:S(2)}) copy-start(f32[2048,128]{1,0:T(8,128)} %get-tuple-element.37) | copy-start | bytes 3145732
  58.6 12.6 %copy-start.5 = (bf16[2048,128]{1,0:T(8,128)(2,1)S(1)}, bf16[2048,128]{1,0:T(8,128)(2,1)}, u32[]{:S(2)}) copy-start(bf16[2048,128]{1,0:T(8,128)(2,1)} %get-tuple-element.38) | copy-start | bytes 1572868
  58.6 12.6 %copy-start.7 = (f32[512,128]{1,0:T(8,128)S(1)}, f32[512,128]{1,0:T(8,128)}, u32[]{:S(2)}) copy-start(f32[512,128]{1,0:T(8,128)} %copy-done.6) | copy-start | bytes 786436
  58.7 9.1 %collective-permute-start.7 = (f32[64,512]{1,0:T(8,128)S(1)}, f32[64,512]{1,0:T(8,128)S(1)}, u32[]{:S(2)}, u32[]{:S(2)}) collective-permute-start(f32[64,512]{1,0:T(8,128)S(1)} %add.9.u0), channel_id=1, source_target_pairs={{0,6},{1,7},{2,0},{3,1},{4,2},{5,3},{6,4},{7,5},{8,14},{9,15},{10,... | collective-permute-start | bytes 393224 | tf_op jit(solution)/shard_map/ppermute | solution.py:293
  61.5 6.3 %collective-permute-start.6 = (f32[64,512]{1,0:T(8,128)S(1)}, f32[64,512]{1,0:T(8,128)S(1)}, u32[]{:S(2)}, u32[]{:S(2)}) collective-permute-start(f32[64,512]{1,0:T(8,128)S(1)} %add.9.u0), channel_id=1, source_target_pairs={{0,4},{1,5},{2,6},{3,7},{4,0},{5,1},{6,2},{7,3},{8,12},{9,13},{10,... | collective-permute-start | bytes 393224 | tf_op jit(solution)/shard_map/ppermute | solution.py:293
  61.8 9.4 %collective-permute-start.5 = (f32[64,512]{1,0:T(8,128)S(1)}, f32[64,512]{1,0:T(8,128)S(1)}, u32[]{:S(2)}, u32[]{:S(2)}) collective-permute-start(f32[64,512]{1,0:T(8,128)S(1)} %add.9.u0), channel_id=1, source_target_pairs={{0,2},{1,3},{2,4},{3,5},{4,6},{5,7},{6,0},{7,1},{8,10},{9,11},{10,... | collective-permute-start | bytes 393224 | tf_op jit(solution)/shard_map/ppermute | solution.py:293

commit v7 on v6

--- a/solution.py
+++ b/solution.py
@@ -141,23 +141,28 @@
 
     size = heads * block_rows
     half = blocks // 2
-    copies = []
-    for t in range(steps):
-        at = slice(t * size, (t + 1) * size)
+
+    def written(t):
+        return pltpu.make_async_copy(held_ref.at[t], out_ref.at[t], sems.at[t])
+
+    def one_step(t, carry):
+        at = pl.ds(pl.multiple_of(t * size, size), size)
         for i in range(blocks):
             part_ref, weight_ref = halves[2 * (i // half) : 2 * (i // half) + 2]
             fresh = jnp.dot(
-                weight_ref[i % half, at], value_ref[i], preferred_element_type=jnp.float32
+                weight_ref[i % half, at, :], value_ref[i], preferred_element_type=jnp.float32
             )
-            context = part_ref[i % half, at] + fresh
+            context = part_ref[i % half, at, :] + fresh
             for g in range(heads):
                 held_ref[t, i * block_rows : (i + 1) * block_rows, g * dim : (g + 1) * dim] = (
                     context[g * block_rows : (g + 1) * block_rows].astype(held_ref.dtype)
                 )
-        copies.append(pltpu.make_async_copy(held_ref.at[t], out_ref.at[t], sems.at[t]))
-        copies[-1].start()
-    for copy in copies:
-        copy.wait()
+        written(t).start()
+        return carry
+
+    lax.fori_loop(0, steps, one_step, 0)
+    for t in range(steps):
+        written(t).wait()
 
 
 def shards(
@@ -290,7 +295,8 @@
     inner, base_parts = lax.optimization_barrier((inner, base_parts))
     inner, row_cache_length = lax.optimization_barrier((inner, row_cache_length))
     second_half = attend(half, row_cache_length, 52)
-    inner_parts = [inner] + [lax.ppermute(inner, "mp", along_y(k)) for k in range(1, n_chips)]
+    distances = sorted(range(1, n_chips), key=lambda k: min(k, n_chips - k))
+    inner_parts = [inner] + [lax.ppermute(inner, "mp", along_y(k)) for k in distances]
 
     operands = [*base_parts, *inner_parts, new_b, *first_half, *second_half]
     return pl.pallas_call(

time: 74.4 us -> 71.9 us (0.966)
  waiting for transfers between devices: 15.2 us -> 11.7 us
    ppermute x3, waiting for transfers between devices: 3.47 us -> 0.01 us  [shards(): lax.ppermute(inner, 'mp', along_y(k))]
  transfers between devices with their start and end apart: 10 -> 10, of which waited for: 5 -> 4; matrix products, arithmetic and copies ran while one was open for 0% -> 0% of each run, Pallas kernels for 23% -> 24%
where the time goes in v7:
time: 71.9 us; the launch traced here: 71.5 us
  starting transfers between devices  31.7 us (44%)
  Pallas kernels  23.3 us (32%)
  waiting for transfers between devices  11.7 us (16%)
  local copies, waits for them, and re-layouts  4.51 us (6%)
    all_to_all x1, starting transfers between devices, shards(): mine = lax.all_to_all(terms, 'dp', 0, 0, tiled=True)  11.9 us
    pallas_call x2, Pallas kernels, attend(): pl.pallas_call(functools.partial(cache_kernel, offset), grid_spec=pltpu.P...  11.4 us
    all_to_all x1, starting transfers between devices, shards(): steps_ab = lax.all_to_all(mine, 'dp', 0, 0, tiled=True)  5.59 us
    ppermute x3, starting transfers between devices, shards(): lax.ppermute(paired[k], 'mp', along_y(k))  5.06 us
    all_to_all x1, waiting for transfers between devices, shards(): steps_ab = lax.all_to_all(mine, 'dp', 0, 0, tiled=True)  4.52 us
    unnamed x22, local copies, waits for them, and re-layouts  4.51 us
    ppermute x3, starting transfers between devices, shards(): lax.ppermute(inner, 'mp', along_y(k))  4.48 us
    pallas_call x1, Pallas kernels, shards(): pl.pallas_call(project_kernel, grid_spec=pltpu.PrefetchScalarGridSpec(num...  4.07 us
  transfers between devices with their start and end apart: 10, of which 4 were waited for; matrix products, arithmetic and copies ran while one was open for 0% of the time, Pallas kernels for 24%

profile of v7, /device:TPU:1, one launch (start us, length us, event | category | flops | bytes accessed | tf_op | source)
XLA Modules:
  0.0 71.5 jit_solution(13636223903613669527)
XLA Ops:
  0.0 1.9 %shard_map.109 = f32[32,2,2176]{2,1,0:T(2,128)} custom-call(bf16[64,2048]{1,0:T(8,128)(2,1)} %bitcast.25, bf16[64,128]{1,0:T(8,128)(2,1)} %bitcast.26), custom_call_target="tpu_custom_call" | custom-call | tf_op jit(solution)/shard_map/pallas_call | solution.py:193
  1.9 11.9 %all-to-all-start = ((f32[32,2,2176]{2,1,0:T(2,128)}), f32[32,2,2176]{2,1,0:T(2,128)S(1)}, u32[]{:S(2)}, u32[]{:S(2)}) async-start(f32[32,2,2176]{2,1,0:T(2,128)} %shard_map.109), calls=%async_computation | async-start | bytes 1114112 | tf_op jit(solution)/shard_map/all_to_all | solution.py:200
  13.7 0.1 pad_add_fusion.place_ref
  13.8 0.0 copy-start
  13.8 1.6 %copy-done = bf16[4,128,2048]{2,1,0:T(8,128)(2,1)S(1)} copy-done((bf16[4,128,2048]{2,1,0:T(8,128)(2,1)S(1)}, bf16[4,128,2048]{2,1,0:T(8,128)(2,1)}, u32[]{:S(2)}) %copy-start) | copy-done | bytes 2097176
  15.4 0.0 copy-start.10
  15.4 2.2 %copy-done.10 = bf16[2048,1024]{1,0:T(8,128)(2,1)S(1)} copy-done((bf16[2048,1024]{1,0:T(8,128)(2,1)S(1)}, bf16[2048,1024]{1,0:T(8,128)(2,1)}, u32[]{:S(2)}) %copy-start.10) | copy-done | bytes 4194328
  17.6 4.1 %shard_map.111 = (f32[4,512,128]{2,1,0:T(8,128)S(1)}, f32[4,512,128]{2,1,0:T(8,128)S(1)}) custom-call(s32[2]{0:T(128)S(1)} %pad_add_fusion.place_ref, bf16[512,2048]{1,0:T(8,128)(2,1)S(1)} %bitcast.14, bf16[2048,1024]{1,0:T(8,128)(2,1)S(1)} %copy-done.10), custom_call_target="tpu_custom_call" | custom-call | flops 2147483648 | bytes 10485760 | tf_op jit(solution)/shard_map/pallas_call | solution.py:208
  21.7 1.0 %collective-permute-start = (f32[4,512,128]{2,1,0:T(8,128)S(1)}, f32[4,512,128]{2,1,0:T(8,128)S(1)}, u32[]{:S(2)}, u32[]{:S(2)}) collective-permute-start(f32[4,512,128]{2,1,0:T(8,128)S(1)} %get-tuple-element.30), channel_id=1, source_target_pairs={{0,1},{1,0},{2,3},{3,2},{4,5},{5,4},{6,7},{7,6},{8,9},{9,8},{10,11... | collective-permute-start | bytes 3145736 | tf_op jit(solution)/shard_map/ppermute | solution.py:235
  22.7 2.3 %collective-permute-done.received_ref = f32[4,512,128]{2,1,0:T(8,128)S(1)} collective-permute-done((f32[4,512,128]{2,1,0:T(8,128)S(1)}, f32[4,512,128]{2,1,0:T(8,128)S(1)}, u32[]{:S(2)}, u32[]{:S(2)}) %collective-permute-start) | collective-permute-done | bytes 1048608 | tf_op jit(solution)/shard_map/ppermute | solution.py:235
  25.0 1.0 %shard_map.112 = (f32[512,128]{1,0:T(8,128)S(1)}, f32[512,128]{1,0:T(8,128)}, f32[512,128]{1,0:T(8,128)}, f32[512,128]{1,0:T(8,128)}) custom-call(f32[4,512,128]{2,1,0:T(8,128)S(1)} %get-tuple-element.29.keep_ref, f32[4,512,128]{2,1,0:T(8,128)S(1)} %collective-permute-done.received_ref), custom_call_target="tpu_custom_call" | custom-call | tf_op jit(solution)/shard_map/pallas_call | solution.py:231
  26.0 0.0 copy-start.6
  26.0 0.7 copy-done.6
  26.7 3.9 %all-to-all-done.in_ref = f32[32,2,2176]{2,1,0:T(2,128)S(1)} async-done(((f32[32,2,2176]{2,1,0:T(2,128)}), f32[32,2,2176]{2,1,0:T(2,128)S(1)}, u32[]{:S(2)}, u32[]{:S(2)}) %all-to-all-start) | async-done | bytes 557088 | tf_op jit(solution)/shard_map/all_to_all | solution.py:200
  30.6 1.1 %shard_map.110 = f32[32,2,2176]{2,1,0:T(2,128)} custom-call(f32[32,2,2176]{2,1,0:T(2,128)S(1)} %all-to-all-done.in_ref), custom_call_target="tpu_custom_call" | custom-call | tf_op jit(solution)/shard_map/pallas_call | solution.py:201
  31.7 5.6 %all-to-all-start.1 = ((f32[32,2,2176]{2,1,0:T(2,128)}), f32[32,2,2176]{2,1,0:T(2,128)S(1)}, u32[]{:S(2)}, u32[]{:S(2)}) async-start(f32[32,2,2176]{2,1,0:T(2,128)} %shard_map.110), calls=%async_computation.1 | async-start | bytes 1114112 | tf_op jit(solution)/shard_map/all_to_all | solution.py:237
  37.3 1.4 %collective-permute-start.2 = (f32[512,128]{1,0:T(8,128)}, f32[512,128]{1,0:T(8,128)}, u32[]{:S(2)}, u32[]{:S(2)}) collective-permute-start(f32[512,128]{1,0:T(8,128)} %get-tuple-element.32), channel_id=1, source_target_pairs={{0,2},{1,3},{2,4},{3,5},{4,6},{5,7},{6,0},{7,1},{8,10},{9,11},{10,... | collective-permute-start | bytes 786440 | tf_op jit(solution)/shard_map/ppermute | solution.py:239
  38.7 2.6 %collective-permute-start.3 = (f32[512,128]{1,0:T(8,128)}, f32[512,128]{1,0:T(8,128)}, u32[]{:S(2)}, u32[]{:S(2)}) collective-permute-start(f32[512,128]{1,0:T(8,128)} %get-tuple-element.33), channel_id=1, source_target_pairs={{0,4},{1,5},{2,6},{3,7},{4,0},{5,1},{6,2},{7,3},{8,12},{9,13},{10,... | collective-permute-start | bytes 786440 | tf_op jit(solution)/shard_map/ppermute | solution.py:239
  41.3 1.1 %collective-permute-start.4 = (f32[512,128]{1,0:T(8,128)}, f32[512,128]{1,0:T(8,128)}, u32[]{:S(2)}, u32[]{:S(2)}) collective-permute-start(f32[512,128]{1,0:T(8,128)} %get-tuple-element.34), channel_id=1, source_target_pairs={{0,6},{1,7},{2,0},{3,1},{4,2},{5,3},{6,4},{7,5},{8,14},{9,15},{10,... | collective-permute-start | bytes 786440 | tf_op jit(solution)/shard_map/ppermute | solution.py:239
  42.4 0.0 copy-start.1
  42.4 0.0 copy-start.3
  42.4 6.2 %shard_map.113 = (f32[2048,128]{1,0:T(8,128)}, bf16[2048,128]{1,0:T(8,128)(2,1)}) custom-call(s32[128]{0:T(128)} %length_ref.1, bf16[4,128,1024]{2,1,0:T(8,128)(2,1)} %query_ref.3, bf16[4,128,128]{2,1,0:T(8,128)(2,1)} %fresh_ref.3, bf16[128,64,128]{2,1,0:T(8,128)(2,1)} %bitcast.21, bf16[128,64,128]{2,1,0:T(8,128)(2,1)} %bitcast.23), custom_call_target="tpu_custom_call" | custom-call | flops 134217728 | bytes 5242880 | tf_op jit(solution)/shard_map/pallas_call | solution.py:256
  48.6 4.5 %all-to-all-done.1.step_ref = f32[32,2,2176]{2,1,0:T(2,128)S(1)} async-done(((f32[32,2,2176]{2,1,0:T(2,128)}), f32[32,2,2176]{2,1,0:T(2,128)S(1)}, u32[]{:S(2)}, u32[]{:S(2)}) %all-to-all-start.1) | async-done | bytes 557088 | tf_op jit(solution)/shard_map/all_to_all | solution.py:237
  53.1 0.0 copy-done.1
  53.1 0.0 copy-done.3
  53.1 0.0 copy-done.8
  53.1 0.8 %shard_map.114 = (f32[64,512]{1,0:T(8,128)S(1)}, f32[64,128]{1,0:T(8,128)S(1)}) custom-call(f32[64,2048]{1,0:T(8,128)S(1)} %copy-done.3, f32[64,128]{1,0:T(8,128)S(1)} %bitcast.20, f32[32,2,2176]{2,1,0:T(2,128)S(1)} %all-to-all-done.1.step_ref, bf16[512,2048]{1,0:T(8,128)(2,1)S(1)} %bitcast.15), custom_call_target="tpu_custom_call" | custom-call | tf_op jit(solution)/shard_map/pallas_call | solution.py:285
  54.0 3.6 %collective-permute-start.1 = (f32[64,512]{1,0:T(8,128)S(1)}, f32[64,512]{1,0:T(8,128)S(1)}, u32[]{:S(2)}, u32[]{:S(2)}) collective-permute-start(f32[64,512]{1,0:T(8,128)S(1)} %get-tuple-element.40), channel_id=1, source_target_pairs={{0,1},{1,0},{2,3},{3,2},{4,5},{5,4},{6,7},{7,6},{8,9},{9,8},{10,11... | collective-permute-start | bytes 393224 | tf_op jit(solution)/shard_map/ppermute | solution.py:294
  57.6 1.0 %collective-permute-done.1 = f32[64,512]{1,0:T(8,128)S(1)} collective-permute-done((f32[64,512]{1,0:T(8,128)S(1)}, f32[64,512]{1,0:T(8,128)S(1)}, u32[]{:S(2)}, u32[]{:S(2)}) %collective-permute-start.1) | collective-permute-done | bytes 131104 | tf_op jit(solution)/shard_map/ppermute | solution.py:294
  58.6 0.0 copy-start.2
  58.6 0.0 copy-start.5
  58.6 0.0 copy-start.7
  58.6 0.0 collective-permute-done.2.v1
  58.6 0.0 collective-permute-done.3.v2
  58.7 0.0 collective-permute-done.4.v3
  58.7 3.0 %collective-permute-start.7 = (f32[64,512]{1,0:T(8,128)S(1)}, f32[64,512]{1,0:T(8,128)S(1)}, u32[]{:S(2)}, u32[]{:S(2)}) collective-permute-start(f32[64,512]{1,0:T(8,128)S(1)} %add.9.u0), channel_id=1, source_target_pairs={{0,4},{1,5},{2,6},{3,7},{4,0},{5,1},{6,2},{7,3},{8,12},{9,13},{10,... | collective-permute-start | bytes 393224 | tf_op jit(solution)/shard_map/ppermute | solution.py:299
  61.7 0.8 %collective-permute-start.6 = (f32[64,512]{1,0:T(8,128)S(1)}, f32[64,512]{1,0:T(8,128)S(1)}, u32[]{:S(2)}, u32[]{:S(2)}) collective-permute-start(f32[64,512]{1,0:T(8,128)S(1)} %add.9.u0), channel_id=1, source_target_pairs={{0,6},{1,7},{2,0},{3,1},{4,2},{5,3},{6,4},{7,5},{8,14},{9,15},{10,... | collective-permute-start | bytes 393224 | tf_op jit(solution)/shard_map/ppermute | solution.py:299
  62.4 0.7 collective-permute-start.5
  63.1 0.0 copy-done.4
  63.2 0.0 copy-done.9
  63.2 5.2 %shard_map.115 = (f32[2048,128]{1,0:T(8,128)S(1)}, bf16[2048,128]{1,0:T(8,128)(2,1)S(1)}) custom-call(s32[128]{0:T(128)S(1)} %copy-done.9, bf16[4,128,1024]{2,1,0:T(8,128)(2,1)} %query_ref.3, bf16[4,128,128]{2,1,0:T(8,128)(2,1)S(1)} %copy-done.4, bf16[128,64,128]{2,1,0:T(8,128)(2,1)} %bitcast.22, bf16[128,64,128]{2,1,0:T(8,128)(2,1)} %bitcast.24), custom_call_target="tpu_custom_call" | custom-call | flops 134217728 | bytes 5242880 | tf_op jit(solution)/shard_map/pallas_call | solution.py:256
  68.3 0.0 collective-permute-done.7.u3
  68.4 0.0 collective-permute-done.6.u2
  68.4 0.0 collective-permute-done.5.u1
  68.4 0.0 copy-done.2
  68.4 0.0 copy-done.5
  68.4 0.0 copy-done.7
  68.4 3.1 %shard_map.116 = bf16[4,128,1024]{2,1,0:T(8,128)(2,1)} custom-call(f32[512,128]{1,0:T(8,128)S(1)} %copy-done.7, f32[512,128]{1,0:T(8,128)} %collective-permute-done.2.v1, f32[512,128]{1,0:T(8,128)} %collective-permute-done.3.v2, f32[512,128]{1,0:T(8,128)} %collective-permute-done.4.v3, f32[64,512]{1,0:T(8,128)S(1)} %add.9.u0, ...), custom_call_target="tpu_custom_call" | custom-call | tf_op jit(solution)/shard_map/pallas_call | solution.py:302
  (4 shorter events, 0.0 us)
Async XLA Ops:
  1.9 28.7 %all-to-all-start = ((f32[32,2,2176]{2,1,0:T(2,128)}), f32[32,2,2176]{2,1,0:T(2,128)S(1)}, u32[]{:S(2)}, u32[]{:S(2)}) async-start(f32[32,2,2176]{2,1,0:T(2,128)} %shard_map.109), calls=%async_computation | async-start | bytes 1114112 | tf_op jit(solution)/shard_map/all_to_all | solution.py:200
  13.8 1.6 %copy-start = (bf16[4,128,2048]{2,1,0:T(8,128)(2,1)S(1)}, bf16[4,128,2048]{2,1,0:T(8,128)(2,1)}, u32[]{:S(2)}) copy-start(bf16[4,128,2048]{2,1,0:T(8,128)(2,1)} %param.11) | copy-start | bytes 6291460
  15.4 2.2 %copy-start.10 = (bf16[2048,1024]{1,0:T(8,128)(2,1)S(1)}, bf16[2048,1024]{1,0:T(8,128)(2,1)}, u32[]{:S(2)}) copy-start(bf16[2048,1024]{1,0:T(8,128)(2,1)} %weight_ref.1) | copy-start | bytes 12582916
  21.7 3.3 %collective-permute-start = (f32[4,512,128]{2,1,0:T(8,128)S(1)}, f32[4,512,128]{2,1,0:T(8,128)S(1)}, u32[]{:S(2)}, u32[]{:S(2)}) collective-permute-start(f32[4,512,128]{2,1,0:T(8,128)S(1)} %get-tuple-element.30), channel_id=1, source_target_pairs={{0,1},{1,0},{2,3},{3,2},{4,5},{5,4},{6,7},{7,6},{8,9},{9,8},{10,11... | collective-permute-start | bytes 3145736 | tf_op jit(solution)/shard_map/ppermute | solution.py:235
  26.0 0.7 copy-start.6
  31.7 21.4 %all-to-all-start.1 = ((f32[32,2,2176]{2,1,0:T(2,128)}), f32[32,2,2176]{2,1,0:T(2,128)S(1)}, u32[]{:S(2)}, u32[]{:S(2)}) async-start(f32[32,2,2176]{2,1,0:T(2,128)} %shard_map.110), calls=%async_computation.1 | async-start | bytes 1114112 | tf_op jit(solution)/shard_map/all_to_all | solution.py:237
  37.3 21.4 %collective-permute-start.2 = (f32[512,128]{1,0:T(8,128)}, f32[512,128]{1,0:T(8,128)}, u32[]{:S(2)}, u32[]{:S(2)}) collective-permute-start(f32[512,128]{1,0:T(8,128)} %get-tuple-element.32), channel_id=1, source_target_pairs={{0,2},{1,3},{2,4},{3,5},{4,6},{5,7},{6,0},{7,1},{8,10},{9,11},{10,... | collective-permute-start | bytes 786440 | tf_op jit(solution)/shard_map/ppermute | solution.py:239
  38.7 20.0 %collective-permute-start.3 = (f32[512,128]{1,0:T(8,128)}, f32[512,128]{1,0:T(8,128)}, u32[]{:S(2)}, u32[]{:S(2)}) collective-permute-start(f32[512,128]{1,0:T(8,128)} %get-tuple-element.33), channel_id=1, source_target_pairs={{0,4},{1,5},{2,6},{3,7},{4,0},{5,1},{6,2},{7,3},{8,12},{9,13},{10,... | collective-permute-start | bytes 786440 | tf_op jit(solution)/shard_map/ppermute | solution.py:239
  41.3 17.4 %collective-permute-start.4 = (f32[512,128]{1,0:T(8,128)}, f32[512,128]{1,0:T(8,128)}, u32[]{:S(2)}, u32[]{:S(2)}) collective-permute-start(f32[512,128]{1,0:T(8,128)} %get-tuple-element.34), channel_id=1, source_target_pairs={{0,6},{1,7},{2,0},{3,1},{4,2},{5,3},{6,4},{7,5},{8,14},{9,15},{10,... | collective-permute-start | bytes 786440 | tf_op jit(solution)/shard_map/ppermute | solution.py:239
  42.4 10.8 %copy-start.1 = (bf16[4,128,2048]{2,1,0:T(8,128)(2,1)S(1)}, bf16[4,128,2048]{2,1,0:T(8,128)(2,1)}, u32[]{:S(2)}) copy-start(bf16[4,128,2048]{2,1,0:T(8,128)(2,1)} %param.11) | copy-start | bytes 6291460
  42.4 10.8 %copy-start.3 = (f32[64,2048]{1,0:T(8,128)S(1)}, f32[64,2048]{1,0:T(8,128)}, u32[]{:S(2)}) copy-start(f32[64,2048]{1,0:T(8,128)} %a_ref.1) | copy-start | bytes 1572868
  42.4 10.8 %copy-start.8 = (f32[128,64]{0,1:T(8,128)S(1)}, f32[128,64]{0,1:T(8,128)}, u32[]{:S(2)}) copy-start(f32[128,64]{0,1:T(8,128)} %param.20) | copy-start | bytes 98308
  48.6 14.6 %copy-start.4 = (bf16[4,128,128]{2,1,0:T(8,128)(2,1)S(1)}, bf16[4,128,128]{2,1,0:T(8,128)(2,1)}, u32[]{:S(2)}) copy-start(bf16[4,128,128]{2,1,0:T(8,128)(2,1)} %fresh_ref.3) | copy-start | bytes 393220
  48.6 14.6 %copy-start.9 = (s32[128]{0:T(128)S(1)}, s32[128]{0:T(128)}, u32[]{:S(2)}) copy-start(s32[128]{0:T(128)} %length_ref.1) | copy-start | bytes 1540
  54.0 4.6 %collective-permute-start.1 = (f32[64,512]{1,0:T(8,128)S(1)}, f32[64,512]{1,0:T(8,128)S(1)}, u32[]{:S(2)}, u32[]{:S(2)}) collective-permute-start(f32[64,512]{1,0:T(8,128)S(1)} %get-tuple-element.40), channel_id=1, source_target_pairs={{0,1},{1,0},{2,3},{3,2},{4,5},{5,4},{6,7},{7,6},{8,9},{9,8},{10,11... | collective-permute-start | bytes 393224 | tf_op jit(solution)/shard_map/ppermute | solution.py:294
  58.6 9.8 %copy-start.2 = (f32[2048,128]{1,0:T(8,128)S(1)}, f32[2048,128]{1,0:T(8,128)}, u32[]{:S(2)}) copy-start(f32[2048,128]{1,0:T(8,128)} %get-tuple-element.37) | copy-start | bytes 3145732
  58.6 9.8 %copy-start.5 = (bf16[2048,128]{1,0:T(8,128)(2,1)S(1)}, bf16[2048,128]{1,0:T(8,128)(2,1)}, u32[]{:S(2)}) copy-start(bf16[2048,128]{1,0:T(8,128)(2,1)} %get-tuple-element.38) | copy-start | bytes 1572868
  58.6 9.8 %copy-start.7 = (f32[512,128]{1,0:T(8,128)S(1)}, f32[512,128]{1,0:T(8,128)}, u32[]{:S(2)}) copy-start(f32[512,128]{1,0:T(8,128)} %copy-done.6) | copy-start | bytes 786436
  58.7 9.7 %collective-permute-start.7 = (f32[64,512]{1,0:T(8,128)S(1)}, f32[64,512]{1,0:T(8,128)S(1)}, u32[]{:S(2)}, u32[]{:S(2)}) collective-permute-start(f32[64,512]{1,0:T(8,128)S(1)} %add.9.u0), channel_id=1, source_target_pairs={{0,4},{1,5},{2,6},{3,7},{4,0},{5,1},{6,2},{7,3},{8,12},{9,13},{10,... | collective-permute-start | bytes 393224 | tf_op jit(solution)/shard_map/ppermute | solution.py:299
  61.7 6.7 %collective-permute-start.6 = (f32[64,512]{1,0:T(8,128)S(1)}, f32[64,512]{1,0:T(8,128)S(1)}, u32[]{:S(2)}, u32[]{:S(2)}) collective-permute-start(f32[64,512]{1,0:T(8,128)S(1)} %add.9.u0), channel_id=1, source_target_pairs={{0,6},{1,7},{2,0},{3,1},{4,2},{5,3},{6,4},{7,5},{8,14},{9,15},{10,... | collective-permute-start | bytes 393224 | tf_op jit(solution)/shard_map/ppermute | solution.py:299
  62.4 5.9 %collective-permute-start.5 = (f32[64,512]{1,0:T(8,128)S(1)}, f32[64,512]{1,0:T(8,128)S(1)}, u32[]{:S(2)}, u32[]{:S(2)}) collective-permute-start(f32[64,512]{1,0:T(8,128)S(1)} %add.9.u0), channel_id=1, source_target_pairs={{0,2},{1,3},{2,4},{3,5},{4,6},{5,7},{6,0},{7,1},{8,10},{9,11},{10,... | collective-permute-start | bytes 393224 | tf_op jit(solution)/shard_map/ppermute | solution.py:299

commit v8 on v6

--- a/solution.py
+++ b/solution.py
@@ -119,7 +119,7 @@
 
 
 def finish_kernel(v0, v1, v2, v3, u0, u1, u2, u3, b_ref, *refs):
-    *halves, out_ref, value_ref, held_ref, sems = refs
+    *parts, out_ref, value_ref, held_ref, sems = refs
     blocks, lanes, dim = value_ref.shape
     steps, rows, width = held_ref.shape
     block_rows = rows // blocks
@@ -140,16 +140,17 @@
             value_ref[i, s * block_rows : (s + 1) * block_rows] = values[at : at + block_rows]
 
     size = heads * block_rows
-    half = blocks // 2
+    split = parts[0].shape[0]
     copies = []
     for t in range(steps):
         at = slice(t * size, (t + 1) * size)
         for i in range(blocks):
-            part_ref, weight_ref = halves[2 * (i // half) : 2 * (i // half) + 2]
+            part_ref, weight_ref = parts[:2] if i < split else parts[2:]
+            k = i if i < split else i - split
             fresh = jnp.dot(
-                weight_ref[i % half, at], value_ref[i], preferred_element_type=jnp.float32
+                weight_ref[k, at], value_ref[i], preferred_element_type=jnp.float32
             )
-            context = part_ref[i % half, at] + fresh
+            context = part_ref[k, at] + fresh
             for g in range(heads):
                 held_ref[t, i * block_rows : (i + 1) * block_rows, g * dim : (g + 1) * dim] = (
                     context[g * block_rows : (g + 1) * block_rows].astype(held_ref.dtype)
@@ -235,13 +236,13 @@
     ]
 
     blocks = 4
-    half = blocks // 2
+    early_blocks = 3
     block_rows = rows_dev // blocks
     n_queries = step_count * group_size
     size = block_rows * n_queries
 
-    def attend(offset, lengths, vmem_mib):
-        by_row = lambda kind: jax.ShapeDtypeStruct((half * size, head_dim), kind)
+    def attend(offset, count, lengths, vmem_mib):
+        by_row = lambda kind: jax.ShapeDtypeStruct((count * size, head_dim), kind)
         by_row_spec = pl.BlockSpec((size, head_dim), lambda i, _: (i, 0))
         cache_spec = pl.BlockSpec((block_rows, ctx_len, head_dim), lambda i, _: (i + offset, 0, 0))
         token_spec = lambda width: pl.BlockSpec(
@@ -252,7 +253,7 @@
             functools.partial(cache_kernel, offset),
             grid_spec=pltpu.PrefetchScalarGridSpec(
                 num_scalar_prefetch=1,
-                grid=(half,),
+                grid=(count,),
                 in_specs=[
                     token_spec(group_size * head_dim),
                     token_spec(head_dim),
@@ -267,15 +268,15 @@
             out_shape=[by_row(f32), by_row(bf16)],
             compiler_params=pltpu.CompilerParams(vmem_limit_bytes=vmem_mib * 1024 * 1024),
             cost_estimate=pl.CostEstimate(
-                flops=2 * 2 * half * size * 2 * ctx_len * head_dim,
+                flops=2 * 2 * count * size * 2 * ctx_len * head_dim,
                 bytes_accessed=5 * 1024 * 1024,
-                transcendentals=2 * half * size * head_dim,
+                transcendentals=2 * count * size * head_dim,
             ),
         )(lengths, queries, rotated_token_keys, stored_key_cache[:, 0], stored_value_cache[:, 0])
-        return part.reshape(half, size, head_dim), weights.reshape(half, size, head_dim)
-
-    first_half = attend(0, row_cache_length, 60)
-    steps_ab, first_half = lax.optimization_barrier((steps_ab, first_half))
+        return part.reshape(count, size, head_dim), weights.reshape(count, size, head_dim)
+
+    first_part = attend(0, early_blocks, row_cache_length, 60)
+    steps_ab, first_part = lax.optimization_barrier((steps_ab, first_part))
 
     inner, new_b = pl.pallas_call(
         inner_kernel,
@@ -289,10 +290,11 @@
     inner = inner + lax.ppermute(inner, "mp", core_pairs)
     inner, base_parts = lax.optimization_barrier((inner, base_parts))
     inner, row_cache_length = lax.optimization_barrier((inner, row_cache_length))
-    second_half = attend(half, row_cache_length, 52)
-    inner_parts = [inner] + [lax.ppermute(inner, "mp", along_y(k)) for k in range(1, n_chips)]
-
-    operands = [*base_parts, *inner_parts, new_b, *first_half, *second_half]
+    second_part = attend(early_blocks, blocks - early_blocks, row_cache_length, 53)
+    distances = sorted(range(1, n_chips), key=lambda k: min(k, n_chips - k))
+    inner_parts = [inner] + [lax.ppermute(inner, "mp", along_y(k)) for k in distances]
+
+    operands = [*base_parts, *inner_parts, new_b, *first_part, *second_part]
     return pl.pallas_call(
         finish_kernel,
         out_shape=jax.ShapeDtypeStruct(queries.shape, jnp.bfloat16),

time: 74.4 us -> 71.4 us (0.960)
  waiting for transfers between devices: 15.2 us -> 11.5 us
    ppermute x3, waiting for transfers between devices: 3.47 us -> 1.51 us  [shards(): lax.ppermute(inner, 'mp', along_y(k))]
    all_to_all x1, waiting for transfers between devices: 4.52 us -> 2.83 us  [shards(): steps_ab = lax.all_to_all(mine, 'dp', 0, 0, tiled=True)]
  transfers between devices with their start and end apart: 10 -> 10, of which waited for: 5 -> 5; matrix products, arithmetic and copies ran while one was open for 0% -> 0% of each run, Pallas kernels for 23% -> 24%
where the time goes in v8:
time: 71.4 us; the launch traced here: 70.9 us
  starting transfers between devices  31.6 us (44%)
  Pallas kernels  23 us (32%)
  waiting for transfers between devices  11.5 us (16%)
  local copies, waits for them, and re-layouts  4.51 us (6%)
    all_to_all x1, starting transfers between devices, shards(): mine = lax.all_to_all(terms, 'dp', 0, 0, tiled=True)  11.9 us
    pallas_call x2, Pallas kernels, attend(): pl.pallas_call(functools.partial(cache_kernel, offset), grid_spec=pltpu.P...  11.4 us
    all_to_all x1, starting transfers between devices, shards(): steps_ab = lax.all_to_all(mine, 'dp', 0, 0, tiled=True)  5.6 us
    ppermute x3, starting transfers between devices, shards(): lax.ppermute(paired[k], 'mp', along_y(k))  5.06 us
    unnamed x22, local copies, waits for them, and re-layouts  4.51 us
    ppermute x3, starting transfers between devices, shards(): lax.ppermute(inner, 'mp', along_y(k))  4.47 us
    pallas_call x1, Pallas kernels, shards(): pl.pallas_call(project_kernel, grid_spec=pltpu.PrefetchScalarGridSpec(num...  4.07 us
    all_to_all x1, waiting for transfers between devices, shards(): mine = lax.all_to_all(terms, 'dp', 0, 0, tiled=True)  3.9 us
  transfers between devices with their start and end apart: 10, of which 5 were waited for; matrix products, arithmetic and copies ran while one was open for 0% of the time, Pallas kernels for 24%

profile of v8, /device:TPU:1, one launch (start us, length us, event | category | flops | bytes accessed | tf_op | source)
XLA Modules:
  0.0 70.9 jit_solution(6731782023151051483)
XLA Ops:
  0.0 1.9 %shard_map.109 = f32[32,2,2176]{2,1,0:T(2,128)} custom-call(bf16[64,2048]{1,0:T(8,128)(2,1)} %bitcast.25, bf16[64,128]{1,0:T(8,128)(2,1)} %bitcast.26), custom_call_target="tpu_custom_call" | custom-call | tf_op jit(solution)/shard_map/pallas_call | solution.py:189
  1.9 11.9 %all-to-all-start = ((f32[32,2,2176]{2,1,0:T(2,128)}), f32[32,2,2176]{2,1,0:T(2,128)S(1)}, u32[]{:S(2)}, u32[]{:S(2)}) async-start(f32[32,2,2176]{2,1,0:T(2,128)} %shard_map.109), calls=%async_computation | async-start | bytes 1114112 | tf_op jit(solution)/shard_map/all_to_all | solution.py:196
  13.7 0.1 pad_add_fusion.place_ref
  13.8 0.0 copy-start
  13.8 1.6 %copy-done = bf16[4,128,2048]{2,1,0:T(8,128)(2,1)S(1)} copy-done((bf16[4,128,2048]{2,1,0:T(8,128)(2,1)S(1)}, bf16[4,128,2048]{2,1,0:T(8,128)(2,1)}, u32[]{:S(2)}) %copy-start) | copy-done | bytes 2097176
  15.4 0.0 copy-start.10
  15.4 2.2 %copy-done.10 = bf16[2048,1024]{1,0:T(8,128)(2,1)S(1)} copy-done((bf16[2048,1024]{1,0:T(8,128)(2,1)S(1)}, bf16[2048,1024]{1,0:T(8,128)(2,1)}, u32[]{:S(2)}) %copy-start.10) | copy-done | bytes 4194328
  17.6 4.1 %shard_map.111 = (f32[4,512,128]{2,1,0:T(8,128)S(1)}, f32[4,512,128]{2,1,0:T(8,128)S(1)}) custom-call(s32[2]{0:T(128)S(1)} %pad_add_fusion.place_ref, bf16[512,2048]{1,0:T(8,128)(2,1)S(1)} %bitcast.14, bf16[2048,1024]{1,0:T(8,128)(2,1)S(1)} %copy-done.10), custom_call_target="tpu_custom_call" | custom-call | flops 2147483648 | bytes 10485760 | tf_op jit(solution)/shard_map/pallas_call | solution.py:204
  21.7 1.0 %collective-permute-start = (f32[4,512,128]{2,1,0:T(8,128)S(1)}, f32[4,512,128]{2,1,0:T(8,128)S(1)}, u32[]{:S(2)}, u32[]{:S(2)}) collective-permute-start(f32[4,512,128]{2,1,0:T(8,128)S(1)} %get-tuple-element.30), channel_id=1, source_target_pairs={{0,1},{1,0},{2,3},{3,2},{4,5},{5,4},{6,7},{7,6},{8,9},{9,8},{10,11... | collective-permute-start | bytes 3145736 | tf_op jit(solution)/shard_map/ppermute | solution.py:231
  22.7 2.3 %collective-permute-done.received_ref = f32[4,512,128]{2,1,0:T(8,128)S(1)} collective-permute-done((f32[4,512,128]{2,1,0:T(8,128)S(1)}, f32[4,512,128]{2,1,0:T(8,128)S(1)}, u32[]{:S(2)}, u32[]{:S(2)}) %collective-permute-start) | collective-permute-done | bytes 1048608 | tf_op jit(solution)/shard_map/ppermute | solution.py:231
  25.0 1.0 %shard_map.112 = (f32[512,128]{1,0:T(8,128)S(1)}, f32[512,128]{1,0:T(8,128)}, f32[512,128]{1,0:T(8,128)}, f32[512,128]{1,0:T(8,128)}) custom-call(f32[4,512,128]{2,1,0:T(8,128)S(1)} %get-tuple-element.29.keep_ref, f32[4,512,128]{2,1,0:T(8,128)S(1)} %collective-permute-done.received_ref), custom_call_target="tpu_custom_call" | custom-call | tf_op jit(solution)/shard_map/pallas_call | solution.py:227
  26.0 0.0 copy-start.6
  26.0 0.7 copy-done.6
  26.7 3.9 %all-to-all-done.in_ref = f32[32,2,2176]{2,1,0:T(2,128)S(1)} async-done(((f32[32,2,2176]{2,1,0:T(2,128)}), f32[32,2,2176]{2,1,0:T(2,128)S(1)}, u32[]{:S(2)}, u32[]{:S(2)}) %all-to-all-start) | async-done | bytes 557088 | tf_op jit(solution)/shard_map/all_to_all | solution.py:196
  30.6 1.1 %shard_map.110 = f32[32,2,2176]{2,1,0:T(2,128)} custom-call(f32[32,2,2176]{2,1,0:T(2,128)S(1)} %all-to-all-done.in_ref), custom_call_target="tpu_custom_call" | custom-call | tf_op jit(solution)/shard_map/pallas_call | solution.py:197
  31.7 5.6 %all-to-all-start.1 = ((f32[32,2,2176]{2,1,0:T(2,128)}), f32[32,2,2176]{2,1,0:T(2,128)S(1)}, u32[]{:S(2)}, u32[]{:S(2)}) async-start(f32[32,2,2176]{2,1,0:T(2,128)} %shard_map.110), calls=%async_computation.1 | async-start | bytes 1114112 | tf_op jit(solution)/shard_map/all_to_all | solution.py:233
  37.3 1.4 %collective-permute-start.2 = (f32[512,128]{1,0:T(8,128)}, f32[512,128]{1,0:T(8,128)}, u32[]{:S(2)}, u32[]{:S(2)}) collective-permute-start(f32[512,128]{1,0:T(8,128)} %get-tuple-element.32), channel_id=1, source_target_pairs={{0,2},{1,3},{2,4},{3,5},{4,6},{5,7},{6,0},{7,1},{8,10},{9,11},{10,... | collective-permute-start | bytes 786440 | tf_op jit(solution)/shard_map/ppermute | solution.py:235
  38.6 2.6 %collective-permute-start.3 = (f32[512,128]{1,0:T(8,128)}, f32[512,128]{1,0:T(8,128)}, u32[]{:S(2)}, u32[]{:S(2)}) collective-permute-start(f32[512,128]{1,0:T(8,128)} %get-tuple-element.33), channel_id=1, source_target_pairs={{0,4},{1,5},{2,6},{3,7},{4,0},{5,1},{6,2},{7,3},{8,12},{9,13},{10,... | collective-permute-start | bytes 786440 | tf_op jit(solution)/shard_map/ppermute | solution.py:235
  41.3 1.1 %collective-permute-start.4 = (f32[512,128]{1,0:T(8,128)}, f32[512,128]{1,0:T(8,128)}, u32[]{:S(2)}, u32[]{:S(2)}) collective-permute-start(f32[512,128]{1,0:T(8,128)} %get-tuple-element.34), channel_id=1, source_target_pairs={{0,6},{1,7},{2,0},{3,1},{4,2},{5,3},{6,4},{7,5},{8,14},{9,15},{10,... | collective-permute-start | bytes 786440 | tf_op jit(solution)/shard_map/ppermute | solution.py:235
  42.3 0.0 copy-start.1
  42.3 0.0 copy-start.4
  42.3 7.9 %shard_map.113 = (f32[3072,128]{1,0:T(8,128)}, bf16[3072,128]{1,0:T(8,128)(2,1)}) custom-call(s32[128]{0:T(128)} %length_ref.1, bf16[4,128,1024]{2,1,0:T(8,128)(2,1)} %query_ref.3, bf16[4,128,128]{2,1,0:T(8,128)(2,1)} %fresh_ref.3, bf16[128,64,128]{2,1,0:T(8,128)(2,1)} %bitcast.21, bf16[128,64,128]{2,1,0:T(8,128)(2,1)} %bitcast.23), custom_call_target="tpu_custom_call" | custom-call | flops 201326592 | bytes 5242880 | tf_op jit(solution)/shard_map/pallas_call | solution.py:252
  50.3 2.8 %all-to-all-done.1.step_ref = f32[32,2,2176]{2,1,0:T(2,128)S(1)} async-done(((f32[32,2,2176]{2,1,0:T(2,128)}), f32[32,2,2176]{2,1,0:T(2,128)S(1)}, u32[]{:S(2)}, u32[]{:S(2)}) %all-to-all-start.1) | async-done | bytes 557088 | tf_op jit(solution)/shard_map/all_to_all | solution.py:233
  53.1 0.0 copy-done.1
  53.1 0.0 copy-done.4
  53.1 0.0 copy-done.8
  53.1 0.8 %shard_map.114 = (f32[64,512]{1,0:T(8,128)S(1)}, f32[64,128]{1,0:T(8,128)S(1)}) custom-call(f32[64,2048]{1,0:T(8,128)S(1)} %copy-done.4, f32[64,128]{1,0:T(8,128)S(1)} %bitcast.20, f32[32,2,2176]{2,1,0:T(2,128)S(1)} %all-to-all-done.1.step_ref, bf16[512,2048]{1,0:T(8,128)(2,1)S(1)} %bitcast.15), custom_call_target="tpu_custom_call" | custom-call | tf_op jit(solution)/shard_map/pallas_call | solution.py:281
  54.0 3.6 %collective-permute-start.1 = (f32[64,512]{1,0:T(8,128)S(1)}, f32[64,512]{1,0:T(8,128)S(1)}, u32[]{:S(2)}, u32[]{:S(2)}) collective-permute-start(f32[64,512]{1,0:T(8,128)S(1)} %get-tuple-element.40), channel_id=1, source_target_pairs={{0,1},{1,0},{2,3},{3,2},{4,5},{5,4},{6,7},{7,6},{8,9},{9,8},{10,11... | collective-permute-start | bytes 393224 | tf_op jit(solution)/shard_map/ppermute | solution.py:290
  57.6 1.0 %collective-permute-done.1 = f32[64,512]{1,0:T(8,128)S(1)} collective-permute-done((f32[64,512]{1,0:T(8,128)S(1)}, f32[64,512]{1,0:T(8,128)S(1)}, u32[]{:S(2)}, u32[]{:S(2)}) %collective-permute-start.1) | collective-permute-done | bytes 131104 | tf_op jit(solution)/shard_map/ppermute | solution.py:290
  58.6 0.0 copy-start.2
  58.6 0.0 copy-start.3
  58.6 0.0 copy-start.7
  58.6 0.0 collective-permute-done.2.v1
  58.6 0.0 collective-permute-done.3.v2
  58.6 0.0 collective-permute-done.4.v3
  58.7 3.0 %collective-permute-start.7 = (f32[64,512]{1,0:T(8,128)S(1)}, f32[64,512]{1,0:T(8,128)S(1)}, u32[]{:S(2)}, u32[]{:S(2)}) collective-permute-start(f32[64,512]{1,0:T(8,128)S(1)} %add.9.u0), channel_id=1, source_target_pairs={{0,4},{1,5},{2,6},{3,7},{4,0},{5,1},{6,2},{7,3},{8,12},{9,13},{10,... | collective-permute-start | bytes 393224 | tf_op jit(solution)/shard_map/ppermute | solution.py:295
  61.7 0.8 %collective-permute-start.6 = (f32[64,512]{1,0:T(8,128)S(1)}, f32[64,512]{1,0:T(8,128)S(1)}, u32[]{:S(2)}, u32[]{:S(2)}) collective-permute-start(f32[64,512]{1,0:T(8,128)S(1)} %add.9.u0), channel_id=1, source_target_pairs={{0,6},{1,7},{2,0},{3,1},{4,2},{5,3},{6,4},{7,5},{8,14},{9,15},{10,... | collective-permute-start | bytes 393224 | tf_op jit(solution)/shard_map/ppermute | solution.py:295
  62.4 0.7 collective-permute-start.5
  63.1 0.0 copy-done.5
  63.1 0.0 copy-done.9
  63.1 3.5 %shard_map.115 = (f32[1024,128]{1,0:T(8,128)S(1)}, bf16[1024,128]{1,0:T(8,128)(2,1)S(1)}) custom-call(s32[128]{0:T(128)S(1)} %copy-done.9, bf16[4,128,1024]{2,1,0:T(8,128)(2,1)} %query_ref.3, bf16[4,128,128]{2,1,0:T(8,128)(2,1)S(1)} %copy-done.5, bf16[128,64,128]{2,1,0:T(8,128)(2,1)} %bitcast.22, bf16[128,64,128]{2,1,0:T(8,128)(2,1)} %bitcast.24), custom_call_target="tpu_custom_call" | custom-call | flops 67108864 | bytes 5242880 | tf_op jit(solution)/shard_map/pallas_call | solution.py:252
  66.6 0.0 collective-permute-done.7.u3
  66.6 1.5 %collective-permute-done.6.u2 = f32[64,512]{1,0:T(8,128)S(1)} collective-permute-done((f32[64,512]{1,0:T(8,128)S(1)}, f32[64,512]{1,0:T(8,128)S(1)}, u32[]{:S(2)}, u32[]{:S(2)}) %collective-permute-start.6) | collective-permute-done | bytes 131104 | tf_op jit(solution)/shard_map/ppermute | solution.py:295
  68.1 0.0 collective-permute-done.5.u1
  68.1 0.0 copy-done.2
  68.1 0.0 copy-done.3
  68.1 0.0 copy-done.7
  68.1 2.8 %shard_map.116 = bf16[4,128,1024]{2,1,0:T(8,128)(2,1)} custom-call(f32[512,128]{1,0:T(8,128)S(1)} %copy-done.7, f32[512,128]{1,0:T(8,128)} %collective-permute-done.2.v1, f32[512,128]{1,0:T(8,128)} %collective-permute-done.3.v2, f32[512,128]{1,0:T(8,128)} %collective-permute-done.4.v3, f32[64,512]{1,0:T(8,128)S(1)} %add.9.u0, ...), custom_call_target="tpu_custom_call" | custom-call | tf_op jit(solution)/shard_map/pallas_call | solution.py:298
  (4 shorter events, 0.0 us)
Async XLA Ops:
  1.9 28.7 %all-to-all-start = ((f32[32,2,2176]{2,1,0:T(2,128)}), f32[32,2,2176]{2,1,0:T(2,128)S(1)}, u32[]{:S(2)}, u32[]{:S(2)}) async-start(f32[32,2,2176]{2,1,0:T(2,128)} %shard_map.109), calls=%async_computation | async-start | bytes 1114112 | tf_op jit(solution)/shard_map/all_to_all | solution.py:196
  13.8 1.6 %copy-start = (bf16[4,128,2048]{2,1,0:T(8,128)(2,1)S(1)}, bf16[4,128,2048]{2,1,0:T(8,128)(2,1)}, u32[]{:S(2)}) copy-start(bf16[4,128,2048]{2,1,0:T(8,128)(2,1)} %param.11) | copy-start | bytes 6291460
  15.4 2.2 %copy-start.10 = (bf16[2048,1024]{1,0:T(8,128)(2,1)S(1)}, bf16[2048,1024]{1,0:T(8,128)(2,1)}, u32[]{:S(2)}) copy-start(bf16[2048,1024]{1,0:T(8,128)(2,1)} %weight_ref.1) | copy-start | bytes 12582916
  21.7 3.3 %collective-permute-start = (f32[4,512,128]{2,1,0:T(8,128)S(1)}, f32[4,512,128]{2,1,0:T(8,128)S(1)}, u32[]{:S(2)}, u32[]{:S(2)}) collective-permute-start(f32[4,512,128]{2,1,0:T(8,128)S(1)} %get-tuple-element.30), channel_id=1, source_target_pairs={{0,1},{1,0},{2,3},{3,2},{4,5},{5,4},{6,7},{7,6},{8,9},{9,8},{10,11... | collective-permute-start | bytes 3145736 | tf_op jit(solution)/shard_map/ppermute | solution.py:231
  26.0 0.7 copy-start.6
  31.7 21.5 %all-to-all-start.1 = ((f32[32,2,2176]{2,1,0:T(2,128)}), f32[32,2,2176]{2,1,0:T(2,128)S(1)}, u32[]{:S(2)}, u32[]{:S(2)}) async-start(f32[32,2,2176]{2,1,0:T(2,128)} %shard_map.110), calls=%async_computation.1 | async-start | bytes 1114112 | tf_op jit(solution)/shard_map/all_to_all | solution.py:233
  37.3 21.4 %collective-permute-start.2 = (f32[512,128]{1,0:T(8,128)}, f32[512,128]{1,0:T(8,128)}, u32[]{:S(2)}, u32[]{:S(2)}) collective-permute-start(f32[512,128]{1,0:T(8,128)} %get-tuple-element.32), channel_id=1, source_target_pairs={{0,2},{1,3},{2,4},{3,5},{4,6},{5,7},{6,0},{7,1},{8,10},{9,11},{10,... | collective-permute-start | bytes 786440 | tf_op jit(solution)/shard_map/ppermute | solution.py:235
  38.6 20.0 %collective-permute-start.3 = (f32[512,128]{1,0:T(8,128)}, f32[512,128]{1,0:T(8,128)}, u32[]{:S(2)}, u32[]{:S(2)}) collective-permute-start(f32[512,128]{1,0:T(8,128)} %get-tuple-element.33), channel_id=1, source_target_pairs={{0,4},{1,5},{2,6},{3,7},{4,0},{5,1},{6,2},{7,3},{8,12},{9,13},{10,... | collective-permute-start | bytes 786440 | tf_op jit(solution)/shard_map/ppermute | solution.py:235
  41.3 17.4 %collective-permute-start.4 = (f32[512,128]{1,0:T(8,128)}, f32[512,128]{1,0:T(8,128)}, u32[]{:S(2)}, u32[]{:S(2)}) collective-permute-start(f32[512,128]{1,0:T(8,128)} %get-tuple-element.34), channel_id=1, source_target_pairs={{0,6},{1,7},{2,0},{3,1},{4,2},{5,3},{6,4},{7,5},{8,14},{9,15},{10,... | collective-permute-start | bytes 786440 | tf_op jit(solution)/shard_map/ppermute | solution.py:235
  42.3 10.8 %copy-start.1 = (bf16[4,128,2048]{2,1,0:T(8,128)(2,1)S(1)}, bf16[4,128,2048]{2,1,0:T(8,128)(2,1)}, u32[]{:S(2)}) copy-start(bf16[4,128,2048]{2,1,0:T(8,128)(2,1)} %param.11) | copy-start | bytes 6291460
  42.3 10.8 %copy-start.4 = (f32[64,2048]{1,0:T(8,128)S(1)}, f32[64,2048]{1,0:T(8,128)}, u32[]{:S(2)}) copy-start(f32[64,2048]{1,0:T(8,128)} %a_ref.1) | copy-start | bytes 1572868
  42.3 10.8 %copy-start.8 = (f32[128,64]{0,1:T(8,128)S(1)}, f32[128,64]{0,1:T(8,128)}, u32[]{:S(2)}) copy-start(f32[128,64]{0,1:T(8,128)} %param.20) | copy-start | bytes 98308
  50.3 12.8 %copy-start.5 = (bf16[4,128,128]{2,1,0:T(8,128)(2,1)S(1)}, bf16[4,128,128]{2,1,0:T(8,128)(2,1)}, u32[]{:S(2)}) copy-start(bf16[4,128,128]{2,1,0:T(8,128)(2,1)} %fresh_ref.3) | copy-start | bytes 393220
  50.3 12.8 %copy-start.9 = (s32[128]{0:T(128)S(1)}, s32[128]{0:T(128)}, u32[]{:S(2)}) copy-start(s32[128]{0:T(128)} %length_ref.1) | copy-start | bytes 1540
  54.0 4.6 %collective-permute-start.1 = (f32[64,512]{1,0:T(8,128)S(1)}, f32[64,512]{1,0:T(8,128)S(1)}, u32[]{:S(2)}, u32[]{:S(2)}) collective-permute-start(f32[64,512]{1,0:T(8,128)S(1)} %get-tuple-element.40), channel_id=1, source_target_pairs={{0,1},{1,0},{2,3},{3,2},{4,5},{5,4},{6,7},{7,6},{8,9},{9,8},{10,11... | collective-permute-start | bytes 393224 | tf_op jit(solution)/shard_map/ppermute | solution.py:290
  58.6 9.5 %copy-start.2 = (f32[3072,128]{1,0:T(8,128)S(1)}, f32[3072,128]{1,0:T(8,128)}, u32[]{:S(2)}) copy-start(f32[3072,128]{1,0:T(8,128)} %get-tuple-element.37) | copy-start | bytes 4718596
  58.6 9.5 %copy-start.3 = (bf16[3072,128]{1,0:T(8,128)(2,1)S(1)}, bf16[3072,128]{1,0:T(8,128)(2,1)}, u32[]{:S(2)}) copy-start(bf16[3072,128]{1,0:T(8,128)(2,1)} %get-tuple-element.38) | copy-start | bytes 2359300
  58.6 9.5 %copy-start.7 = (f32[512,128]{1,0:T(8,128)S(1)}, f32[512,128]{1,0:T(8,128)}, u32[]{:S(2)}) copy-start(f32[512,128]{1,0:T(8,128)} %copy-done.6) | copy-start | bytes 786436
  58.7 8.0 %collective-permute-start.7 = (f32[64,512]{1,0:T(8,128)S(1)}, f32[64,512]{1,0:T(8,128)S(1)}, u32[]{:S(2)}, u32[]{:S(2)}) collective-permute-start(f32[64,512]{1,0:T(8,128)S(1)} %add.9.u0), channel_id=1, source_target_pairs={{0,4},{1,5},{2,6},{3,7},{4,0},{5,1},{6,2},{7,3},{8,12},{9,13},{10,... | collective-permute-start | bytes 393224 | tf_op jit(solution)/shard_map/ppermute | solution.py:295
  61.7 6.5 %collective-permute-start.6 = (f32[64,512]{1,0:T(8,128)S(1)}, f32[64,512]{1,0:T(8,128)S(1)}, u32[]{:S(2)}, u32[]{:S(2)}) collective-permute-start(f32[64,512]{1,0:T(8,128)S(1)} %add.9.u0), channel_id=1, source_target_pairs={{0,6},{1,7},{2,0},{3,1},{4,2},{5,3},{6,4},{7,5},{8,14},{9,15},{10,... | collective-permute-start | bytes 393224 | tf_op jit(solution)/shard_map/ppermute | solution.py:295
  62.4 5.7 %collective-permute-start.5 = (f32[64,512]{1,0:T(8,128)S(1)}, f32[64,512]{1,0:T(8,128)S(1)}, u32[]{:S(2)}, u32[]{:S(2)}) collective-permute-start(f32[64,512]{1,0:T(8,128)S(1)} %add.9.u0), channel_id=1, source_target_pairs={{0,2},{1,3},{2,4},{3,5},{4,6},{5,7},{6,0},{7,1},{8,10},{9,11},{10,... | collective-permute-start | bytes 393224 | tf_op jit(solution)/shard_map/ppermute | solution.py:295
